TPU v7x, 32 devices: a whole 2x2x4 slice. The times are simulated.
32 devices in a mesh: seq: 4 (over x, core), fsdp: 8 (over z, y).
Axes of the slice: x: 2, y: 2, z: 4, core: 2. Of those that a mesh axis runs over, the one named last changes fastest.
Arguments:
- tokens: bfloat16 [65536, 512], P(('fsdp', 'seq')), may hold values from -6 to 6
- doc_ids: int32 [8, 8192], P('fsdp', 'seq'), may hold values from 0 to 31, never falling along the last dimension, each value on 1 to 4096 neighbouring positions
- w_query: float32 [512, 512], P('fsdp'), may hold values from -0.375 to 0.375
- w_key: float32 [512, 512], P('fsdp'), may hold values from -0.375 to 0.375
- w_value: float32 [512, 512], P('fsdp'), may hold values from -0.25 to 0.25
- w_slots: float32 [512, 512], P('fsdp'), may hold values from -0.5 to 0.5
- w_output: float32 [512, 512], P('fsdp'), may hold values from -0.75 to 0.75
- w_hidden: float32 [512, 2048], P('fsdp'), may hold values from -0.25 to 0.25
- w_return: float32 [2048, 512], P('fsdp'), may hold values from -0.1875 to 0.1875
- gain_first: float32 [512], P('fsdp'), may hold values from 0.1 to 1.9
- shift_first: float32 [512], P('fsdp'), may hold values from -3 to 3
- gain_second: float32 [512], P('fsdp'), may hold values from 0.1 to 1.9
- shift_second: float32 [512], P('fsdp'), may hold values from -3 to 3
- bias_hidden: float32 [2048], P('fsdp'), may hold values from -3 to 3
- bias_return: float32 [512], P('fsdp'), may hold values from -3 to 3
- cotangent: bfloat16 [65536, 512], P(('fsdp', 'seq')), may hold values from -6 to 6
Outputs:
- layer_out: bfloat16 [65536, 512], P(('fsdp', 'seq'))
- grad_input: float32 [65536, 512], P(('fsdp', 'seq'))
- grad_w_query: float32 [512, 512], P('fsdp')
- grad_w_key: float32 [512, 512], P('fsdp')
- grad_w_value: float32 [512, 512], P('fsdp')
- grad_w_slots: float32 [512, 512], P('fsdp')
- grad_w_output: float32 [512, 512], P('fsdp')
- grad_w_hidden: float32 [512, 2048], P('fsdp')
- grad_w_return: float32 [2048, 512], P('fsdp')
- grad_gain_first: float32 [512], P('fsdp')
- grad_shift_first: float32 [512], P('fsdp')
- grad_gain_second: float32 [512], P('fsdp')
- grad_shift_second: float32 [512], P('fsdp')
- grad_bias_hidden: float32 [2048], P('fsdp')
- grad_bias_return: float32 [512], P('fsdp')
Inputs may be any that keep to these rules, and one draw needn't show every extreme that they name: `doc_ids`: in each packed sequence the document numbers never fall, each document has at least one token, and at most 4096 tokens, with one document of exactly 4096 tokens.
All inputs are finite; a program needn't handle non-finite values.
Results may differ from a plain program's by a relative error of at most 0.01.
The roundings to bfloat16 on the way count: a program that leaves them out, or rounds other values in their place, can miss the bound.
Values may be sent and summed in bfloat16 or wider, within the bound.
A program may use at most 192 MiB of HBM per device.

v0:
```python
import jax
import jax.numpy as jnp
from jax import lax
from jax.sharding import PartitionSpec as P

D = 512
H = 8
M = 64
BLOCK = 512


EPS = 1e-05
HIGH = lax.Precision.HIGHEST


def normed(values, gain, shift):
    centre = jnp.mean(values, axis=-1, keepdims=True)
    centred = values - centre
    spread = jnp.mean(centred * centred, axis=-1, keepdims=True)
    return centred * lax.rsqrt(spread + EPS) * gain + shift


def smooth_gate(values):
    return jax.nn.gelu(values, approximate=True)


def mix_head(
    queries,
    key_rows,
    value_rows,
    slot_logits,
    doc_row,
    key_start,
    value_start,
    norm_start,
    doc_start,
):
    length, width = queries.shape
    block_rows = min(BLOCK, length)
    block_count = length // block_rows
    score_scale = width ** (-0.5)
    positions = jnp.arange(block_rows)
    causal = positions[:, None] >= positions[None, :]

    def advance(state, pieces):
        key_state, value_state, norm_state, last_doc = state
        q_rows, k_rows, v_rows, p_rows, d_rows = pieces
        written = jnp.exp(p_rows)
        visible = (causal & (d_rows[:, None] == d_rows[None, :])).astype(jnp.float32)
        carried = (d_rows == last_doc).astype(jnp.float32)[:, None]
        affinity = jnp.dot(q_rows, k_rows.T, precision=HIGH) * visible
        numer = jnp.dot(affinity, written, precision=HIGH) + carried * jnp.dot(
            q_rows, key_state.T, precision=HIGH
        )
        total = jnp.dot(visible, written, precision=HIGH) + carried * norm_state[None, :]
        probs = jax.nn.softmax(numer / total * score_scale, axis=-1)
        reading = probs / total
        mixed = jnp.dot(
            jnp.dot(reading, written.T, precision=HIGH) * visible, v_rows, precision=HIGH
        )
        mixed = mixed + carried * jnp.dot(reading, value_state, precision=HIGH)
        newest = d_rows[-1]
        tail = (d_rows == newest).astype(jnp.float32)[:, None] * written
        kept = (last_doc == newest).astype(jnp.float32)
        state = (
            kept * key_state + jnp.dot(tail.T, k_rows, precision=HIGH),
            kept * value_state + jnp.dot(tail.T, v_rows, precision=HIGH),
            kept * norm_state + jnp.sum(tail, axis=0),
            newest,
        )
        return (state, mixed)

    start = (key_start, value_start, norm_start, doc_start)
    pieces = (
        queries.reshape(block_count, block_rows, width),
        key_rows.reshape(block_count, block_rows, width),
        value_rows.reshape(block_count, block_rows, width),
        slot_logits.reshape(block_count, block_rows, slot_logits.shape[1]),
        doc_row.reshape(block_count, block_rows),
    )
    final, outputs = lax.scan(jax.checkpoint(advance), start, pieces)
    return outputs.reshape(length, width)


def split_heads(rows, heads_here, width):
    return rows.astype(jnp.float32).reshape(rows.shape[0], heads_here, width).transpose(1, 0, 2)


def merge_heads(values):
    return values.transpose(1, 0, 2).reshape(values.shape[1], -1).astype(jnp.bfloat16)


def on_device(
    tokens,
    doc_ids,
    w_query,
    w_key,
    w_value,
    w_slots,
    w_output,
    w_hidden,
    w_return,
    gain_first,
    shift_first,
    gain_second,
    shift_second,
    bias_hidden,
    bias_return,
    cotangent,
):
    masters = (
        w_query,
        w_key,
        w_value,
        w_slots,
        w_output,
        w_hidden,
        w_return,
        gain_first,
        shift_first,
        gain_second,
        shift_second,
        bias_hidden,
        bias_return,
    )
    rounded = tuple((piece.astype(jnp.bfloat16) for piece in masters))
    gathered = (
        lax.all_gather(rounded[0], "fsdp", axis=0, tiled=True),
        lax.all_gather(rounded[1], "fsdp", axis=0, tiled=True),
        lax.all_gather(rounded[2], "fsdp", axis=0, tiled=True),
        lax.all_gather(rounded[3], "fsdp", axis=0, tiled=True),
        lax.all_gather(rounded[4], "fsdp", axis=0, tiled=True),
        lax.all_gather(rounded[5], "fsdp", axis=0, tiled=True),
        lax.all_gather(rounded[6], "fsdp", axis=0, tiled=True),
        lax.all_gather(rounded[7], "fsdp", axis=0, tiled=True),
        lax.all_gather(rounded[8], "fsdp", axis=0, tiled=True),
        lax.all_gather(rounded[9], "fsdp", axis=0, tiled=True),
        lax.all_gather(rounded[10], "fsdp", axis=0, tiled=True),
        lax.all_gather(rounded[11], "fsdp", axis=0, tiled=True),
        lax.all_gather(rounded[12], "fsdp", axis=0, tiled=True),
    )
    (
        q_weight,
        k_weight,
        v_weight,
        s_weight,
        o_weight,
        h_weight,
        r_weight,
        gain_one,
        shift_one,
        gain_two,
        shift_two,
        b_hidden,
        b_return,
    ) = gathered
    seq_count = lax.axis_size("seq")
    heads_here = H // seq_count
    width = D // H
    vmapped = jax.vmap(mix_head, in_axes=(0, 0, 0, 0, None, 0, 0, 0, None))
    resid = tokens.astype(jnp.float32)
    normed_one, pull_one = jax.vjp(
        normed, resid, gain_one.astype(jnp.float32), shift_one.astype(jnp.float32)
    )
    hidden_one = normed_one.astype(jnp.bfloat16)

    def project(weights):
        return jnp.dot(hidden_one, weights, preferred_element_type=jnp.float32).astype(jnp.bfloat16)

    queries = project(q_weight)
    key_rows = project(k_weight)
    value_rows = project(v_weight)
    slot_rows = project(s_weight)
    doc_full = lax.all_gather(doc_ids, "seq", axis=1, tiled=True)[0]
    head_q, head_k, head_v, head_s = (
        lax.all_to_all(queries, "seq", split_axis=1, concat_axis=0, tiled=True),
        lax.all_to_all(key_rows, "seq", split_axis=1, concat_axis=0, tiled=True),
        lax.all_to_all(value_rows, "seq", split_axis=1, concat_axis=0, tiled=True),
        lax.all_to_all(slot_rows, "seq", split_axis=1, concat_axis=0, tiled=True),
    )
    empty_state = jnp.zeros((heads_here, M, width), jnp.float32)
    empty_norm = jnp.zeros((heads_here, M), jnp.float32)

    def mix_local(part_q, part_k, part_v, part_s):
        return vmapped(
            part_q,
            part_k,
            part_v,
            part_s,
            doc_full,
            empty_state,
            empty_state,
            empty_norm,
            jnp.array(-1, jnp.int32),
        )

    mixed, pull_mix = jax.vjp(
        mix_local,
        split_heads(head_q, heads_here, width),
        split_heads(head_k, heads_here, width),
        split_heads(head_v, heads_here, width),
        split_heads(head_s, heads_here, M),
    )
    attended = lax.all_to_all(merge_heads(mixed), "seq", split_axis=0, concat_axis=1, tiled=True)
    middle = resid + jnp.dot(attended, o_weight, preferred_element_type=jnp.float32)
    normed_two, pull_two = jax.vjp(
        normed, middle, gain_two.astype(jnp.float32), shift_two.astype(jnp.float32)
    )
    hidden_two = normed_two.astype(jnp.bfloat16)
    inner = jnp.dot(hidden_two, h_weight, preferred_element_type=jnp.float32) + b_hidden.astype(
        jnp.float32
    )
    gated, pull_gate = jax.vjp(smooth_gate, inner)
    active = gated.astype(jnp.bfloat16)
    output = (
        middle
        + jnp.dot(active, r_weight, preferred_element_type=jnp.float32)
        + b_return.astype(jnp.float32)
    )
    again_rows = (
        lax.all_gather(rounded[0], "fsdp", axis=0, tiled=True),
        lax.all_gather(rounded[1], "fsdp", axis=0, tiled=True),
        lax.all_gather(rounded[2], "fsdp", axis=0, tiled=True),
        lax.all_gather(rounded[3], "fsdp", axis=0, tiled=True),
        lax.all_gather(rounded[4], "fsdp", axis=0, tiled=True),
        lax.all_gather(rounded[5], "fsdp", axis=0, tiled=True),
        lax.all_gather(rounded[6], "fsdp", axis=0, tiled=True),
    )
    q_back, k_back, v_back, s_back, o_back, h_back, r_back = again_rows
    grad_return = jnp.dot(active.T, cotangent, preferred_element_type=jnp.float32)
    grad_bias_return = jnp.sum(cotangent.astype(jnp.float32), axis=0)
    grad_active = jnp.dot(cotangent, r_back.T, preferred_element_type=jnp.float32)
    grad_inner = pull_gate(grad_active)[0].astype(jnp.bfloat16)
    grad_hidden = jnp.dot(hidden_two.T, grad_inner, preferred_element_type=jnp.float32)
    grad_bias_hidden = jnp.sum(grad_inner.astype(jnp.float32), axis=0)
    grad_norm_two = jnp.dot(grad_inner, h_back.T, preferred_element_type=jnp.float32)
    back_middle, grad_gain_two, grad_shift_two = pull_two(grad_norm_two)
    grad_middle = cotangent.astype(jnp.float32) + back_middle
    grad_branch = grad_middle.astype(jnp.bfloat16)
    grad_output_rows = jnp.dot(attended.T, grad_branch, preferred_element_type=jnp.float32)
    grad_attended = jnp.dot(grad_branch, o_back.T, preferred_element_type=jnp.float32).astype(
        jnp.bfloat16
    )
    head_grad = lax.all_to_all(grad_attended, "seq", split_axis=1, concat_axis=0, tiled=True)
    grad_q, grad_k, grad_v, grad_s = pull_mix(split_heads(head_grad, heads_here, width))
    back_q, back_k, back_v, back_s = (
        lax.all_to_all(merge_heads(grad_q), "seq", split_axis=0, concat_axis=1, tiled=True),
        lax.all_to_all(merge_heads(grad_k), "seq", split_axis=0, concat_axis=1, tiled=True),
        lax.all_to_all(merge_heads(grad_v), "seq", split_axis=0, concat_axis=1, tiled=True),
        lax.all_to_all(merge_heads(grad_s), "seq", split_axis=0, concat_axis=1, tiled=True),
    )

    def weight_grad(back_rows):
        return jnp.dot(hidden_one.T, back_rows, preferred_element_type=jnp.float32)

    def input_part(back_rows, weights):
        return jnp.dot(back_rows, weights.T, preferred_element_type=jnp.float32)

    grad_norm_one = (
        input_part(back_q, q_back)
        + input_part(back_k, k_back)
        + input_part(back_v, v_back)
        + input_part(back_s, s_back)
    )
    back_input, grad_gain_one, grad_shift_one = pull_one(grad_norm_one)
    grad_input = grad_middle + back_input
    partials = (
        weight_grad(back_q),
        weight_grad(back_k),
        weight_grad(back_v),
        weight_grad(back_s),
        grad_output_rows,
        grad_hidden,
        grad_return,
        grad_gain_one,
        grad_shift_one,
        grad_gain_two,
        grad_shift_two,
        grad_bias_hidden,
        grad_bias_return,
    )
    shares = (
        lax.psum_scatter(partials[0], "fsdp", scatter_dimension=0, tiled=True),
        lax.psum_scatter(partials[1], "fsdp", scatter_dimension=0, tiled=True),
        lax.psum_scatter(partials[2], "fsdp", scatter_dimension=0, tiled=True),
        lax.psum_scatter(partials[3], "fsdp", scatter_dimension=0, tiled=True),
        lax.psum_scatter(partials[4], "fsdp", scatter_dimension=0, tiled=True),
        lax.psum_scatter(partials[5], "fsdp", scatter_dimension=0, tiled=True),
        lax.psum_scatter(partials[6], "fsdp", scatter_dimension=0, tiled=True),
        lax.psum_scatter(partials[7], "fsdp", scatter_dimension=0, tiled=True),
        lax.psum_scatter(partials[8], "fsdp", scatter_dimension=0, tiled=True),
        lax.psum_scatter(partials[9], "fsdp", scatter_dimension=0, tiled=True),
        lax.psum_scatter(partials[10], "fsdp", scatter_dimension=0, tiled=True),
        lax.psum_scatter(partials[11], "fsdp", scatter_dimension=0, tiled=True),
        lax.psum_scatter(partials[12], "fsdp", scatter_dimension=0, tiled=True),
    )
    owned = lax.psum(
        (
            shares[0],
            shares[1],
            shares[2],
            shares[3],
            shares[4],
            shares[5],
            shares[6],
            shares[7],
            shares[8],
            shares[9],
            shares[10],
            shares[11],
            shares[12],
        ),
        "seq",
    )
    return (
        output.astype(jnp.bfloat16),
        grad_input,
        owned[0],
        owned[1],
        owned[2],
        owned[3],
        owned[4],
        owned[5],
        owned[6],
        owned[7],
        owned[8],
        owned[9],
        owned[10],
        owned[11],
        owned[12],
    )


def solution(mesh):
    placed = (
        P(("fsdp", "seq"), None),
        P("fsdp", "seq"),
        P("fsdp", None),
        P("fsdp", None),
        P("fsdp", None),
        P("fsdp", None),
        P("fsdp", None),
        P("fsdp", None),
        P("fsdp", None),
        P("fsdp"),
        P("fsdp"),
        P("fsdp"),
        P("fsdp"),
        P("fsdp"),
        P("fsdp"),
        P(("fsdp", "seq"), None),
    )
    return jax.shard_map(
        on_device,
        mesh=mesh,
        in_specs=placed,
        out_specs=(
            P(("fsdp", "seq"), None),
            P(("fsdp", "seq"), None),
            P("fsdp", None),
            P("fsdp", None),
            P("fsdp", None),
            P("fsdp", None),
            P("fsdp", None),
            P("fsdp", None),
            P("fsdp", None),
            P("fsdp"),
            P("fsdp"),
            P("fsdp"),
            P("fsdp"),
            P("fsdp"),
            P("fsdp"),
        ),
        check_vma=False,
    )
```

profile of v0, /device:TPU:0, one launch (start us, length us, event | category | flops | bytes accessed | tf_op | source)
XLA Modules:
  0.0 2025.6 jit_solution(2754947224960085338)
XLA Ops:
  13.6 23.9 %all-reduce.14 = (bf16[512]{0:T(512)(128)(2,1)S(1)}, bf16[512]{0:T(512)(128)(2,1)S(1)}, bf16[512]{0:T(512)(128)(2,1)S(1)}, bf16[512]{0:T(512)(128)(2,1)S(1)}, bf16[512]{0:T(512)(128)(2,1)}) all-reduce(bf16[512]{0:T(512)(128)(2,1)S(1)} %dynamic-update-slice.1, ...), channel_id=1, replica_groups=mesh['seq'=4,'fsdp'=8] {'fsdp'}, use_global_device_ids=true, to_apply=%add.1 | all-reduce | flops 2560 | bytes 10240
  42.1 31.4 %all_gather.52 = bf16[512,512]{1,0:T(8,128)(2,1)S(1)} all-gather(bf16[64,512]{1,0:T(8,128)(2,1)S(1)} %convert_element_type.286), channel_id=1, replica_groups=mesh['seq'=4,'fsdp'=8] {'fsdp'}, dimensions={0}, use_global_device_ids=true | all-gather | bytes 589824 | tf_op jit(solution)/shard_map/all_gather | solution.py:131
  77.0 4.6 all-to-all-start
  81.7 31.4 %all_gather.53 = bf16[512,512]{1,0:T(8,128)(2,1)S(1)} all-gather(bf16[64,512]{1,0:T(8,128)(2,1)S(1)} %convert_element_type.290), channel_id=1, replica_groups=mesh['seq'=4,'fsdp'=8] {'fsdp'}, dimensions={0}, use_global_device_ids=true | all-gather | bytes 589824 | tf_op jit(solution)/shard_map/all_gather | solution.py:129
  122.7 31.3 %all_gather.54 = bf16[512,512]{1,0:T(8,128)(2,1)S(1)} all-gather(bf16[64,512]{1,0:T(8,128)(2,1)S(1)} %convert_element_type.294), channel_id=1, replica_groups=mesh['seq'=4,'fsdp'=8] {'fsdp'}, dimensions={0}, use_global_device_ids=true | all-gather | bytes 589824 | tf_op jit(solution)/shard_map/all_gather | solution.py:130
  164.5 25.8 %all_gather.49 = s32[1,8192]{1,0:T(1,128)S(1)} all-gather(s32[1,2048]{1,0:T(1,128)S(1)} %copy-done.46), channel_id=1, replica_groups=mesh['seq'=4,'fsdp'=8] {'seq'}, dimensions={1}, use_global_device_ids=true | all-gather | bytes 40960 | tf_op jit(solution)/shard_map/all_gather | solution.py:174
  191.5 32.7 %all_gather.55 = bf16[512,512]{1,0:T(8,128)(2,1)S(1)} all-gather(bf16[64,512]{1,0:T(8,128)(2,1)S(1)} %convert_element_type.298), channel_id=1, replica_groups=mesh['seq'=4,'fsdp'=8] {'fsdp'}, dimensions={0}, use_global_device_ids=true | all-gather | bytes 589824 | tf_op jit(solution)/shard_map/all_gather | solution.py:128
  228.6 4.7 all-to-all-start.3
  235.4 4.7 copy.92
  240.2 6.0 reshape.276
  246.2 5.4 copy.143
  258.2 4.6 copy.93
  262.8 6.5 reshape.277
  269.4 5.4 copy.144
  281.4 4.6 copy.94
  286.0 6.3 reshape.278
  292.3 5.4 copy.145
  304.4 4.7 copy.95
  309.1 6.0 reshape.279
  315.1 5.4 copy.146
  326.5 335.4 %while.54 = (s32[]{:T(128)}, f32[2,64,64]{2,1,0:T(8,128)S(1)}, f32[2,64,64]{2,1,0:T(8,128)S(1)}, f32[2,64]{1,0:T(2,128)S(1)}, s32[]{:T(128)}, /*index=5*/bf16[16...) while((s32[]{:T(128)}, f32[2,64,64]{2,1,0:T(8,128)S(1)}, ...), condition=%wide.region_6.7_spmd.clone, body=%wide.region_2.6_spmd.clone.sunk | while | flops 2219196672 | bytes 18811660 | solution.py:81
  679.0 16.6 all-gather
  699.6 32.7 %all_gather.56 = bf16[512,512]{1,0:T(8,128)(2,1)S(1)} all-gather(bf16[64,512]{1,0:T(8,128)(2,1)S(1)} %convert_element_type.307), channel_id=1, replica_groups=mesh['seq'=4,'fsdp'=8] {'fsdp'}, dimensions={0}, use_global_device_ids=true | all-gather | bytes 589824 | tf_op jit(solution)/shard_map/all_gather | solution.py:132
  738.0 16.2 multiply_convert_fusion
  754.2 18.3 convert_reduce_fusion
  772.5 7.0 fusion.230
  779.4 5.9 copy.104
  785.3 5.4 multiply_reduce_fusion.2
  805.6 21.0 %all-to-all-done.5 = bf16[2048,4,128]{0,2,1:T(8,128)(2,1)S(1)} async-done(((bf16[2048,4,128]{0,2,1:T(8,128)(2,1)}), bf16[2048,4,128]{0,2,1:T(8,128)(2,1)S(1)}, u32[]{:S(2)}, u32[]{:S(2)}) %all-to-all-start.5) | async-done | bytes 2097184 | tf_op jit(solution)/shard_map/all_to_all | solution.py:244
  827.2 4.6 copy.105
  831.8 6.1 reshape.280
  837.9 7.4 copy.147
  851.5 622.0 %while.55 = (s32[]{:T(128)}, f32[2,64,64]{2,1,0:T(8,128)S(1)}, f32[2,64,64]{2,1,0:T(8,128)S(1)}, f32[2,64]{1,0:T(2,128)S(1)}, bf16[16,2,512,64]{2,3,1,0:T(8,128)...) while((s32[]{:T(128)}, f32[2,64,64]{2,1,0:T(8,128)S(1)}, ...), condition=%wide.region_16.17_spmd.clone, body=%wide.region_11.16_spmd.clone.sunk | while | flops 5698603008 | bytes 54807344 | solution.py:81
  1481.0 28.2 %all_to_all.145 = bf16[4,2048,128]{1,2,0:T(8,128)(2,1)S(1)} all-to-all(bf16[4,2048,128]{1,2,0:T(8,128)(2,1)S(1)} %copy.115), channel_id=1, replica_groups=mesh['seq'=4,'fsdp'=8] {'seq'}, dimensions={0} | all-to-all | bytes 4194304 | tf_op jit(solution)/shard_map/all_to_all | solution.py:248
  1522.1 28.2 %all_to_all.146 = bf16[4,2048,128]{1,2,0:T(8,128)(2,1)S(1)} all-to-all(bf16[4,2048,128]{1,2,0:T(8,128)(2,1)S(1)} %copy.119), channel_id=1, replica_groups=mesh['seq'=4,'fsdp'=8] {'seq'}, dimensions={0} | all-to-all | bytes 4194304 | tf_op jit(solution)/shard_map/all_to_all | solution.py:249
  1564.6 28.2 %all_to_all.147 = bf16[4,2048,128]{1,2,0:T(8,128)(2,1)S(1)} all-to-all(bf16[4,2048,128]{1,2,0:T(8,128)(2,1)S(1)} %copy.122), channel_id=1, replica_groups=mesh['seq'=4,'fsdp'=8] {'seq'}, dimensions={0} | all-to-all | bytes 4194304 | tf_op jit(solution)/shard_map/all_to_all | solution.py:250
  1607.0 28.3 %all_to_all.148 = bf16[4,2048,128]{1,2,0:T(8,128)(2,1)S(1)} all-to-all(bf16[4,2048,128]{1,2,0:T(8,128)(2,1)S(1)} %copy.113), channel_id=1, replica_groups=mesh['seq'=4,'fsdp'=8] {'seq'}, dimensions={0} | all-to-all | bytes 4194304 | tf_op jit(solution)/shard_map/all_to_all | solution.py:247
  1639.0 11.1 fusion.222
  1650.2 10.5 fusion.238
  1662.2 11.2 add_convert_fusion
  1690.6 13.8 reduce-scatter.14.cloned.1.call-done
  1704.4 65.8 %reduce-scatter.8.cloned.1.call-done = f32[64,512]{1,0:T(8,128)} async-done(((f32[512,512]{1,0:T(8,128)}), f32[64,512]{1,0:T(8,128)}) %reduce-scatter.8.cloned.1.call-update) | async-done | bytes 131088 | tf_op jit(solution)/shard_map/reduce_scatter | solution.py:283
  1770.3 91.0 %reduce-scatter.18.cloned.1.call-done = f32[64,2048]{1,0:T(8,128)} async-done(((f32[512,2048]{1,0:T(8,128)}), f32[64,2048]{1,0:T(8,128)}) %reduce-scatter.18.cloned.1.call-update) | async-done | bytes 524304 | tf_op jit(solution)/shard_map/reduce_scatter | solution.py:288
  1861.3 91.3 %reduce-scatter.20.cloned.1.call-done = f32[256,512]{1,0:T(8,128)} async-done(((f32[2048,512]{1,0:T(8,128)}), f32[256,512]{1,0:T(8,128)}) %reduce-scatter.20.cloned.1.call-update) | async-done | bytes 524304 | tf_op jit(solution)/shard_map/reduce_scatter | solution.py:289
  1952.7 6.3 convert_reduce_fusion.2
  1959.0 35.9 %all-reduce.11 = (f32[512]{0:T(512)S(1)}, f32[512]{0:T(512)S(1)}, f32[512]{0:T(512)S(1)}, f32[512]{0:T(512)S(1)}, f32[2048]{0:T(1024)S(1)}, /*index=5*/f32[512]{0:T(512)S(1)}) all-reduce(f32[512]{0:T(512)S(1)} %get-tuple-element.750, f32[512]{0:T(512)S(1)} %get-tuple-element.752, ...), channel_id=9, replica_groups=mesh['seq'=4,'fsdp'=8] {'fsdp'}, use_global_device_ids=true, to_apply=%region_34.35.clone | all-reduce | flops 4608 | bytes 36864
  1995.3 5.3 copy.126
  2000.7 6.2 all-reduce.12
  (1272 shorter events, 1106.2 us)
Async XLA Ops:
  37.5 36.0 %copy-start.43 = (f32[512]{0:T(512)}, f32[512]{0:T(512)S(1)}, u32[]{:S(2)}) copy-start(f32[512]{0:T(512)S(1)} %convert_element_type.282) | copy-start | bytes 6148
  37.5 4.0 copy-start.34
  40.5 691.9 %copy-start = (bf16[2048,512]{0,1:T(8,128)(2,1)}, bf16[2048,512]{0,1:T(8,128)(2,1)S(1)}, u32[]{:S(2)}) copy-start(bf16[2048,512]{0,1:T(8,128)(2,1)S(1)} %copy.91) | copy-start | bytes 6291460
  40.9 36.1 %copy-start.30 = (f32[2048]{0:T(1024)}, f32[2048]{0:T(1024)S(1)}, u32[]{:S(2)}) copy-start(f32[2048]{0:T(1024)S(1)} %broadcast_multiply_fusion.1) | copy-start | bytes 24580
  41.5 35.5 %copy-start.32 = (f32[2048]{0:T(1024)}, f32[2048]{0:T(1024)S(1)}, u32[]{:S(2)}) copy-start(f32[2048]{0:T(1024)S(1)} %fusion.220) | copy-start | bytes 24580
  73.5 3.5 copy-start.19
  77.0 4.6 copy-start.35
  77.0 41.0 %all-to-all-start = ((bf16[2048,4,128]{0,2,1:T(8,128)(2,1)}), bf16[2048,4,128]{0,2,1:T(8,128)(2,1)}, u32[]{:S(2)}, u32[]{:S(2)}) async-start(bf16[2048,4,128]{0,2,1:T(8,128)(2,1)} %bitcast.519), calls=%async_computation | async-start | bytes 4194304 | tf_op jit(solution)/shard_map/all_to_all | solution.py:179
  118.0 4.6 copy-start.36
  118.0 40.9 %all-to-all-start.1 = ((bf16[2048,4,128]{0,2,1:T(8,128)(2,1)}), bf16[2048,4,128]{0,2,1:T(8,128)(2,1)}, u32[]{:S(2)}, u32[]{:S(2)}) async-start(bf16[2048,4,128]{0,2,1:T(8,128)(2,1)} %bitcast.518), calls=%async_computation.1 | async-start | bytes 4194304 | tf_op jit(solution)/shard_map/all_to_all | solution.py:177
  159.0 4.7 copy-start.28
  159.0 5.5 copy-start.37
  159.0 5.5 copy-start.46
  159.0 69.7 %all-to-all-start.2 = ((bf16[2048,4,128]{0,2,1:T(8,128)(2,1)}), bf16[2048,4,128]{0,2,1:T(8,128)(2,1)}, u32[]{:S(2)}, u32[]{:S(2)}) async-start(bf16[2048,4,128]{0,2,1:T(8,128)(2,1)} %bitcast.515), calls=%async_computation.2 | async-start | bytes 4194304 | tf_op jit(solution)/shard_map/all_to_all | solution.py:178
  163.6 574.4 %all-gather.4.cloned.1.call-start = ((), (), s32[]{:S(2)}) async-start(), calls=%async_computation.17 | async-start | bytes 2359296 | tf_op jit(solution)/shard_map/all_gather | solution.py:133
  224.2 4.4 copy-start.26
  228.6 73.7 %all-to-all-start.3 = ((bf16[2048,4,128]{0,2,1:T(8,128)(2,1)}), bf16[2048,4,128]{0,2,1:T(8,128)(2,1)}, u32[]{:S(2)}, u32[]{:S(2)}) async-start(bf16[2048,4,128]{0,2,1:T(8,128)(2,1)} %bitcast.516), calls=%async_computation.3 | async-start | bytes 4194304 | tf_op jit(solution)/shard_map/all_to_all | solution.py:176
  669.5 8.6 copy-start.29
  669.5 9.4 copy-start.38
  669.5 9.4 copy-start.53
  673.6 58.7 %all-to-all-start.4 = ((bf16[4,2048,128]{1,2,0:T(8,128)(2,1)}), bf16[4,2048,128]{1,2,0:T(8,128)(2,1)}, u32[]{:S(2)}, u32[]{:S(2)}) async-start(bf16[4,2048,128]{1,2,0:T(8,128)(2,1)} %copy.101), calls=%async_computation.4 | async-start | bytes 4194304 | tf_op jit(solution)/shard_map/all_to_all | solution.py:204
  678.1 76.1 %all-gather.6.cloned.1.call-start = ((), (), s32[]{:S(2)}) async-start(), calls=%async_computation.18 | async-start | bytes 2359296 | tf_op jit(solution)/shard_map/all_gather | solution.py:134
  679.0 59.0 %copy-start.49 = (f32[512]{0:T(512)}, f32[512]{0:T(512)S(1)}, u32[]{:S(2)}) copy-start(f32[512]{0:T(512)S(1)} %convert_element_type.311) | copy-start | bytes 6148
  737.9 16.3 copy-start.21
  754.2 18.3 copy-start.52
  772.5 7.0 copy-start.54
  785.3 5.4 copy-start.3
  785.3 5.9 copy-start.5
  797.4 29.3 %all-to-all-start.5 = ((bf16[2048,4,128]{0,2,1:T(8,128)(2,1)}), bf16[2048,4,128]{0,2,1:T(8,128)(2,1)S(1)}, u32[]{:S(2)}, u32[]{:S(2)}) async-start(bf16[2048,4,128]{0,2,1:T(8,128)(2,1)} %bitcast.517), calls=%async_computation.5 | async-start | bytes 4194304 | tf_op jit(solution)/shard_map/all_to_all | solution.py:244
  801.0 889.6 %reduce-scatter.16.cloned.1.call-start = ((), (), s32[]{:S(2)}) async-start(), calls=%async_computation.23 | async-start | bytes 1179648 | tf_op jit(solution)/shard_map/reduce_scatter | solution.py:287
  805.6 885.0 %reduce-scatter.10.cloned.1.call-start = ((), (), s32[]{:S(2)}) async-start(), calls=%async_computation.20 | async-start | bytes 1179648 | tf_op jit(solution)/shard_map/reduce_scatter | solution.py:284
  1478.1 31.1 %copy-start.15 = (bf16[2048,512]{0,1:T(8,128)(2,1)S(1)}, bf16[2048,512]{0,1:T(8,128)(2,1)}, u32[]{:S(2)}) copy-start(bf16[2048,512]{0,1:T(8,128)(2,1)} %copy-done.14) | copy-start | bytes 6291460
  1511.5 179.1 %reduce-scatter.12.cloned.1.call-start = ((), (), s32[]{:S(2)}) async-start(), calls=%async_computation.21 | async-start | bytes 1179648 | tf_op jit(solution)/shard_map/reduce_scatter | solution.py:285
  1519.2 32.4 %copy-start.16 = (bf16[2048,512]{0,1:T(8,128)(2,1)S(1)}, bf16[2048,512]{0,1:T(8,128)(2,1)}, u32[]{:S(2)}) copy-start(bf16[2048,512]{0,1:T(8,128)(2,1)} %copy-done.14) | copy-start | bytes 6291460
  1553.9 150.5 %reduce-scatter.14.cloned.1.call-start = ((), (), s32[]{:S(2)}) async-start(), calls=%async_computation.22 | async-start | bytes 1179648 | tf_op jit(solution)/shard_map/reduce_scatter | solution.py:286
  1561.7 32.4 %copy-start.17 = (bf16[2048,512]{0,1:T(8,128)(2,1)S(1)}, bf16[2048,512]{0,1:T(8,128)(2,1)}, u32[]{:S(2)}) copy-start(bf16[2048,512]{0,1:T(8,128)(2,1)} %copy-done.14) | copy-start | bytes 6291460
  1596.4 173.8 %reduce-scatter.8.cloned.1.call-start = ((), (), s32[]{:S(2)}) async-start(), calls=%async_computation.19 | async-start | bytes 1179648 | tf_op jit(solution)/shard_map/reduce_scatter | solution.py:283
  1604.1 32.6 %copy-start.18 = (bf16[2048,512]{0,1:T(8,128)(2,1)S(1)}, bf16[2048,512]{0,1:T(8,128)(2,1)}, u32[]{:S(2)}) copy-start(bf16[2048,512]{0,1:T(8,128)(2,1)} %copy-done.14) | copy-start | bytes 6291460
  1639.0 222.3 %reduce-scatter.18.cloned.1.call-start = ((), (), s32[]{:S(2)}) async-start(), calls=%async_computation.24 | async-start | bytes 4718592 | tf_op jit(solution)/shard_map/reduce_scatter | solution.py:288
  1650.2 302.4 %reduce-scatter.20.cloned.1.call-start = ((), (), s32[]{:S(2)}) async-start(), calls=%async_computation.25 | async-start | bytes 4718592 | tf_op jit(solution)/shard_map/reduce_scatter | solution.py:289
  1660.8 346.1 %all-reduce.17.cloned.1.call-start = ((), (), s32[]{:S(2)}) async-start(), calls=%async_computation.26 | async-start | bytes 3407872 | tf_op jit(solution)/shard_map/psum | solution.py:297
  1673.4 4.1 copy-start.27
  1677.5 2.9 copy-start.23
  1684.5 4.3 copy-start.33
  1686.7 265.9 %copy-start.40 = (f32[2048]{0:T(1024)S(1)}, f32[2048]{0:T(1024)}, u32[]{:S(2)}) copy-start(f32[2048]{0:T(1024)} %copy-done.39) | copy-start | bytes 24580
  1952.6 6.4 copy-start.45
  1952.7 6.4 copy-start.47
  1952.7 6.4 copy-start.48
  (23 other events, 41.0 us)
Sparse Core Ops, SparseCore 0:
  166.5 54.9 all-gather.3
  681.6 52.4 all-gather.5
  805.7 62.4 reduce-scatter.15
  1511.6 60.9 reduce-scatter.9
  1575.8 62.4 reduce-scatter.11
  1641.9 62.4 reduce-scatter.13
  1707.8 62.3 reduce-scatter.7
  1774.3 86.9 reduce-scatter.17
  1864.9 87.6 reduce-scatter.19
  1955.6 45.8 all-reduce.16
where the time goes:
time: 2040 us; the launch traced here: 2030 us
  matrix products  824 us (40%)
  blocking collectives  381 us (19%)
  local copies, waits for them, and re-layouts  334 us (16%)
  waiting for transfers between devices  283 us (14%)
  other arithmetic  110 us (5%)
  loops' own time  48.3 us (2%)
  starting transfers between devices  26.9 us (1%)
    dot_general x64, matrix products, advance(): affinity = jnp.dot(q_rows, k_rows.T, precision=HIGH) * visible  157 us
    dot_general x64, matrix products, advance(): jnp.dot(reading, written.T, precision=HIGH) * visible  133 us
    dot_general x64, matrix products, advance(): jnp.dot(affinity, written, precision=HIGH)  126 us
    dot_general x48, matrix products, advance(): jnp.dot(jnp.dot(reading, written.T, precision=HIGH) * visible, v_rows, pr...  126 us
    reduce_scatter x1, waiting for transfers between devices, on_device(): lax.psum_scatter(partials[6], 'fsdp', scatter_dimension=0, tiled=True)  91.3 us
    unnamed x148, local copies, waits for them, and re-layouts  91.2 us
    reduce_scatter x1, waiting for transfers between devices, on_device(): lax.psum_scatter(partials[5], 'fsdp', scatter_dimension=0, tiled=True)  91 us
    reduce_scatter x1, waiting for transfers between devices, on_device(): lax.psum_scatter(partials[0], 'fsdp', scatter_dimension=0, tiled=True)  65.8 us
  transfers between devices with their start and end apart: 16, of which 5 were waited for; matrix products, arithmetic and copies ran while one was open for 59% of the time, Pallas kernels for 0%

commit v1 on v0

v1 whole, which is shorter than its diff:
```python
import functools

import jax
import jax.numpy as jnp
from jax import lax
from jax.experimental import pallas as pl
from jax.experimental.pallas import tpu as pltpu
from jax.sharding import PartitionSpec as P

D = 512
H = 8
M = 64
FF = 2048
C = 256
GROUP = 256
EPS = 1e-05
SCALE = 0.125
F32 = jnp.float32
BF16 = jnp.bfloat16
LIMIT = 60 * 1024 * 1024


def dot(a, b):
    return lax.dot_general(a, b, (((1,), (0,)), ((), ())), preferred_element_type=F32)


def dot_nt(a, b):
    return lax.dot_general(a, b, (((1,), (1,)), ((), ())), preferred_element_type=F32)


def dot_tn(a, b):
    return lax.dot_general(a, b, (((0,), (0,)), ((), ())), preferred_element_type=F32)


def lane_heads(rows, lanes):
    return lax.broadcasted_iota(jnp.int32, (rows, lanes), 1) // M


def stacked(values):
    heads = lane_heads(C, GROUP)
    zero = jnp.zeros_like(values)
    return jnp.concatenate([jnp.where(heads == h, values, zero) for h in range(4)], axis=0)


def select(values):
    heads = lane_heads(C, GROUP)
    out = values[3 * C :]
    for h in (2, 1, 0):
        out = jnp.where(heads == h, values[h * C : (h + 1) * C], out)
    return out


def masked(values, mask):
    return jnp.concatenate(
        [values[h * C : (h + 1) * C].astype(BF16) * mask for h in range(4)], axis=0
    )


def expand(compact):
    rows = lax.broadcasted_iota(jnp.int32, (GROUP, GROUP), 0) // M
    full = jnp.concatenate([compact] * 4, axis=0)
    return jnp.where(rows == lane_heads(GROUP, GROUP), full, jnp.zeros_like(full))


def compacted(full):
    heads = lane_heads(M, GROUP)
    out = full[3 * M :]
    for h in (2, 1, 0):
        out = jnp.where(heads == h, full[h * M : (h + 1) * M], out)
    return out


def split(values):
    high = values.astype(BF16)
    return high, (values - high.astype(F32)).astype(BF16)


def ones_block():
    rows = lax.broadcasted_iota(jnp.int32, (GROUP, GROUP), 0) // M
    return (rows == lane_heads(GROUP, GROUP)).astype(BF16)


def head_sums(values):
    high, low = split(values)
    ones = ones_block()
    return dot(high, ones) + dot(low, ones)


def head_max(values):
    left = lane_heads(C, 128) == 0
    out = []
    for p in range(2):
        pair = values[:, p * 128 : (p + 1) * 128]
        one = jnp.max(jnp.where(left, pair, -jnp.inf), axis=1, keepdims=True)
        two = jnp.max(jnp.where(left, -jnp.inf, pair), axis=1, keepdims=True)
        out.append(jnp.where(left, one, two))
    return jnp.concatenate(out, axis=1)


def wide(values, times):
    return jnp.concatenate([values] * times, axis=1)


def visible(doc_col, doc_row):
    same = wide(doc_col, 2) == doc_row
    here = lax.broadcasted_iota(jnp.int32, (C, C), 0)
    there = lax.broadcasted_iota(jnp.int32, (C, C), 1)
    return jnp.where(same & (here >= there), 1.0, 0.0).astype(BF16)


def visible_back(doc_col, doc_row):
    same = wide(doc_col, 2) == doc_row
    here = lax.broadcasted_iota(jnp.int32, (C, C), 0)
    there = lax.broadcasted_iota(jnp.int32, (C, C), 1)
    return jnp.where(same & (there >= here), 1.0, 0.0).astype(BF16)


def flag(doc_col, doc):
    return jnp.where(doc_col == doc[:, :128], 1.0, 0.0)


def norm_parts(values):
    centre = jnp.mean(values, axis=-1, keepdims=True)
    centred = values - centre
    spread = jnp.mean(centred * centred, axis=-1, keepdims=True)
    scale = lax.rsqrt(spread + EPS)
    return centred * scale, scale


def norm_back(unit, scale, gain, grad):
    inner = grad * gain
    return scale * (
        inner
        - jnp.mean(inner, axis=-1, keepdims=True)
        - unit * jnp.mean(inner * unit, axis=-1, keepdims=True)
    )


def groups(values):
    return values[:, :GROUP], values[:, GROUP:]


def state_terms(slots, left, right):
    one, two = [], []
    for g in range(2):
        lanes = slice(g * GROUP, (g + 1) * GROUP)
        both = dot_tn(slots[:, lanes], jnp.concatenate([left[:, lanes], right[:, lanes]], axis=1))
        one.append(compacted(both[:, :GROUP]))
        two.append(compacted(both[:, GROUP:]))
    return jnp.concatenate(one, axis=1), jnp.concatenate(two, axis=1)


def project_kernel(x_ref, col_ref, edge_ref, small_ref, w_ref, qkvf_ref, tail_ref):
    step = pl.program_id(0)
    unit, _ = norm_parts(x_ref[...].astype(F32))
    hidden = (unit * small_ref[0:1] + small_ref[1:2]).astype(BF16)
    rows = dot(hidden, w_ref[...]).astype(BF16)
    qkvf_ref[...] = rows
    written = jnp.exp(rows[:, 3 * D :].astype(F32))
    newest = edge_ref[15:16]
    tail = wide(flag(col_ref[...], newest), 4) * written
    slots = tail.astype(BF16)
    keys, values = state_terms(slots, rows[:, D : 2 * D], rows[:, 2 * D : 3 * D])

    @pl.when(step == 0)
    def _():
        tail_ref[...] = jnp.zeros_like(tail_ref)
        tail_ref[129:130] = newest.astype(F32)

    tail_ref[0:64] += keys
    tail_ref[64:128] += values
    tail_ref[128:129] += jnp.sum(slots.astype(F32), axis=0, keepdims=True)


def attend_kernel(
    qkvf_ref, col_ref, row_ref, edge_ref, start_ref, o_ref, p_ref, s_ref, z_ref, kept_ref, state
):
    step = pl.program_id(0)

    @pl.when(step == 0)
    def _():
        state[...] = start_ref[...]

    kept_ref[0] = state[0:128]
    first = edge_ref[pl.ds(0, 1)]
    before = edge_ref[pl.ds(8 + jnp.maximum(step - 1, 0), 1)]
    last = jnp.where(step == 0, first, before)
    newest = edge_ref[pl.ds(8 + step, 1)]
    col = col_ref[...]
    vis = visible(col, row_ref[...])
    carried = wide(flag(col, last), 2)
    written = jnp.exp(qkvf_ref[:, 3 * D :].astype(F32))
    slots = written.astype(BF16)
    norm = dot(vis, slots)
    for g in range(2):
        lanes = slice(g * GROUP, (g + 1) * GROUP)
        queries, keys, values = (
            qkvf_ref[:, part * D + g * GROUP : part * D + (g + 1) * GROUP] for part in range(3)
        )
        here = slots[:, lanes]
        affinity = masked(dot_nt(stacked(queries), keys), vis)
        numer = select(dot(affinity, here))
        numer = numer + carried * dot_nt(queries, expand(state[0:64, lanes]).astype(BF16))
        total = norm[:, lanes] + carried * state[128:129, lanes]
        inverse = 1.0 / total
        score = numer * inverse * SCALE
        grown = jnp.exp(score - head_max(score))
        probs = grown / head_sums(grown)
        reading = (probs * inverse).astype(BF16)
        mix = masked(dot_nt(stacked(reading), here), vis)
        mixed = select(dot(mix, values))
        mixed = mixed + carried * dot(reading, expand(state[64:128, lanes]).astype(BF16))
        o_ref[:, lanes] = mixed.astype(BF16)
        p_ref[:, lanes] = probs
        s_ref[:, lanes] = score
        z_ref[:, lanes] = inverse
    tail = (wide(flag(col, newest), 4) * written).astype(BF16)
    new_keys, new_values = state_terms(tail, qkvf_ref[:, D : 2 * D], qkvf_ref[:, 2 * D : 3 * D])
    same = jnp.where(last == newest, 1.0, 0.0)
    state[0:64] = same * state[0:64] + new_keys
    state[64:128] = same * state[64:128] + new_values
    state[128:129] = same * state[128:129] + jnp.sum(tail.astype(F32), axis=0, keepdims=True)


ROOT = 0.7978845608028654
CUBE = 0.044715


def gelu_both(u):
    square = u * u
    bent = jnp.tanh(ROOT * u * (1.0 + CUBE * square))
    half = 0.5 * (1.0 + bent)
    slope = half + 0.5 * u * (1.0 - bent * bent) * (ROOT * (1.0 + 3.0 * CUBE * square))
    return u * half, slope


def forward_kernel(
    x_ref, o_ref, g_ref, small_ref, bias_ref, wo_ref, wh_ref, wr_ref,
    y_ref, dy_ref, do_ref, gwo_ref, gwh_ref, gwr_ref, gsmall_ref, gbias_ref, dz_buf,
):
    step = pl.program_id(0)

    @pl.when(step == 0)
    def _():
        for ref in (gwo_ref, gwh_ref, gwr_ref, gsmall_ref, gbias_ref):
            ref[...] = jnp.zeros_like(ref)

    attended, cot = o_ref[...], g_ref[...]
    middle = x_ref[...].astype(F32) + dot(attended, wo_ref[...])
    unit, scale = norm_parts(middle)
    hidden = (unit * small_ref[2:3] + small_ref[3:4]).astype(BF16)
    out = middle + small_ref[4:5]
    grad_hidden = jnp.zeros((x_ref.shape[0], D), F32)
    cot32 = cot.astype(F32)
    for j in range(4):
        cols = slice(j * 512, (j + 1) * 512)
        inner = dot(hidden, wh_ref[:, cols]) + bias_ref[0:1, cols]
        gated, slope = gelu_both(inner)
        active = gated.astype(BF16)
        out = out + dot(active, wr_ref[cols, :])
        gwr_ref[:, cols] += dot_tn(cot, active)
        grad = dot_nt(cot, wr_ref[cols, :]) * slope
        low = grad.astype(BF16)
        gbias_ref[0:1, cols] += jnp.sum(low.astype(F32), axis=0, keepdims=True)
        gwh_ref[:, cols] += dot_tn(hidden, low)
        grad_hidden = grad_hidden + dot_nt(low, wh_ref[:, cols])
    y_ref[...] = out.astype(BF16)
    gsmall_ref[2:3] += jnp.sum(grad_hidden * unit, axis=0, keepdims=True)
    gsmall_ref[3:4] += jnp.sum(grad_hidden, axis=0, keepdims=True)
    gsmall_ref[4:5] += jnp.sum(cot32, axis=0, keepdims=True)
    grad_middle = cot32 + norm_back(unit, scale, small_ref[2:3], grad_hidden)
    dy_ref[...] = grad_middle
    branch = grad_middle.astype(BF16)
    gwo_ref[...] += dot_tn(attended, branch)
    do_ref[...] = dot_nt(branch, wo_ref[...]).astype(BF16)


def row_kernel(
    qkvf_ref, do_ref, p_ref, s_ref, z_ref, kept_ref, col_ref, row_ref, edge_ref,
    dq_ref, r_ref, dn_ref, dz_ref, head_ref,
):
    step = pl.program_id(0)
    first = edge_ref[pl.ds(0, 1)]
    before = edge_ref[pl.ds(8 + jnp.maximum(step - 1, 0), 1)]
    last = jnp.where(step == 0, first, before)
    col = col_ref[...]
    vis = visible(col, row_ref[...])
    carried = wide(flag(col, last), 2)
    slots = jnp.exp(qkvf_ref[:, 3 * D :].astype(F32)).astype(BF16)
    own = wide(flag(col, first), 4)

    @pl.when(step == 0)
    def _():
        head_ref[...] = jnp.zeros_like(head_ref)
        head_ref[129:130] = first.astype(F32)

    for g in range(2):
        lanes = slice(g * GROUP, (g + 1) * GROUP)
        queries, keys, values = (
            qkvf_ref[:, part * D + g * GROUP : part * D + (g + 1) * GROUP] for part in range(3)
        )
        here, grads = slots[:, lanes], do_ref[:, lanes]
        probs, score, inverse = p_ref[:, lanes], s_ref[:, lanes], z_ref[:, lanes]
        back_mix = masked(dot_nt(stacked(grads), values), vis)
        back_reading = select(dot(back_mix, here))
        back_reading = back_reading + carried * dot_nt(
            grads, expand(kept_ref[0, 64:128, lanes]).astype(BF16)
        )
        back_probs = back_reading * inverse
        shared = back_probs * probs
        back_score = shared - probs * head_sums(shared)
        back_numer = back_score * inverse * SCALE
        back_total = -(shared + back_score * score) * inverse
        low = back_numer.astype(BF16)
        back_affinity = masked(dot_nt(stacked(low), here), vis)
        back_queries = select(dot(back_affinity, keys))
        back_queries = back_queries + carried * dot(
            low, expand(kept_ref[0, 0:64, lanes]).astype(BF16)
        )
        dq_ref[:, lanes] = back_queries.astype(BF16)
        reading = (probs * inverse).astype(BF16)
        r_ref[:, lanes] = reading
        dn_ref[:, lanes] = back_numer
        dz_ref[:, lanes] = back_total
        mine = own[:, lanes]
        head_ref[0:64, lanes] += compacted(dot_tn((mine * back_numer).astype(BF16), queries))
        head_ref[64:128, lanes] += compacted(
            dot_tn((mine * reading.astype(F32)).astype(BF16), grads)
        )
        head_ref[128:129, lanes] += jnp.sum(mine * back_total, axis=0, keepdims=True)


def column_kernel(
    x_ref, qkvf_ref, do_ref, dq_ref, r_ref, dn_ref, dz_ref, col_ref, row_ref, edge_ref, small_ref,
    start_ref, d_ref, gw_ref, state,
):
    step = pl.program_id(0)
    here_at = 7 - step

    @pl.when(step == 0)
    def _():
        state[...] = start_ref[...]
        gw_ref[...] = jnp.zeros_like(gw_ref)

    newest = edge_ref[15:16]
    after = edge_ref[pl.ds(jnp.minimum(here_at + 1, 7), 1)]
    following = jnp.where(step == 0, newest, after)
    first = edge_ref[pl.ds(here_at, 1)]
    col = col_ref[...]
    vis = visible_back(col, row_ref[...])
    carried = wide(flag(col, following), 2)
    own = wide(flag(col, first), 2)
    same = jnp.where(following == first, 1.0, 0.0)
    written = jnp.exp(qkvf_ref[:, 3 * D :].astype(F32))
    slots = written.astype(BF16)
    total_high, total_low = split(dz_ref[...])
    back_norm = dot(vis, total_high) + dot(vis, total_low)
    d_ref[:, 0:D] = dq_ref[...]
    left = lane_heads(C, 128) == 0
    for g in range(2):
        lanes = slice(g * GROUP, (g + 1) * GROUP)
        queries, keys, values = (
            qkvf_ref[:, part * D + g * GROUP : part * D + (g + 1) * GROUP] for part in range(3)
        )
        here, grads, reading = slots[:, lanes], do_ref[:, lanes], r_ref[:, lanes]
        numer_high, numer_low = split(dn_ref[:, lanes])
        key_state = expand(state[0:64, lanes]).astype(BF16)
        value_state = expand(state[64:128, lanes]).astype(BF16)
        apart = stacked(here)
        mix = masked(dot_nt(apart, reading), vis)
        back_values = select(dot(mix, grads)) + carried * dot(here, value_state)
        d_ref[:, 2 * D + g * GROUP : 2 * D + (g + 1) * GROUP] = back_values.astype(BF16)
        back_affinity = masked(dot_nt(apart, numer_high), vis)
        back_keys = select(dot(back_affinity, queries)) + carried * dot(here, key_state)
        d_ref[:, D + g * GROUP : D + (g + 1) * GROUP] = back_keys.astype(BF16)
        back_mix = masked(dot_nt(stacked(values), grads), vis)
        back_slots = back_norm[:, lanes] + select(dot(back_mix, reading))
        affinity = masked(dot_nt(stacked(keys), queries), vis)
        parts = []
        for p in range(2):
            pair = slice(p * 128, (p + 1) * 128)
            both = dot(
                affinity[p * 512 : (p + 1) * 512],
                jnp.concatenate([numer_high[:, pair], numer_low[:, pair]], axis=1),
            )
            both = both[:, :128] + both[:, 128:]
            parts.append(jnp.where(left, both[:C], both[C:]))
        back_slots = back_slots + jnp.concatenate(parts, axis=1)
        back_slots = back_slots + carried * (
            dot_nt(keys, key_state) + dot_nt(values, value_state) + state[128:129, lanes]
        )
        d_ref[:, 3 * D + g * GROUP : 3 * D + (g + 1) * GROUP] = (
            back_slots * written[:, lanes]
        ).astype(BF16)
        kept = same[:, lanes]
        state[0:64, lanes] = kept * state[0:64, lanes] + compacted(
            dot_tn((own * dn_ref[:, lanes]).astype(BF16), queries)
        )
        state[64:128, lanes] = kept * state[64:128, lanes] + compacted(
            dot_tn((own * reading.astype(F32)).astype(BF16), grads)
        )
        state[128:129, lanes] = kept * state[128:129, lanes] + jnp.sum(
            own * dz_ref[:, lanes], axis=0, keepdims=True
        )
    unit, _ = norm_parts(x_ref[...].astype(F32))
    hidden = (unit * small_ref[0:1] + small_ref[1:2]).astype(BF16)
    gw_ref[...] += dot_tn(hidden, d_ref[...])


def input_kernel(x_ref, d_ref, dy_ref, w_ref, small_ref, gi_ref, gsmall_ref):
    step = pl.program_id(0)

    @pl.when(step == 0)
    def _():
        gsmall_ref[...] = jnp.zeros_like(gsmall_ref)

    grad = dot_nt(d_ref[...], w_ref[...])
    unit, scale = norm_parts(x_ref[...].astype(F32))
    gsmall_ref[0:1] += jnp.sum(grad * unit, axis=0, keepdims=True)
    gsmall_ref[1:2] += jnp.sum(grad, axis=0, keepdims=True)
    gi_ref[...] = dy_ref[...] + norm_back(unit, scale, small_ref[0:1], grad)


def rows_of(lanes, order=lambda i: i):
    return pl.BlockSpec((C, lanes), lambda i: (order(i), 0))


def whole(*shape):
    return pl.BlockSpec(shape, lambda i: (0,) * len(shape))


def row_of(order=lambda i: i):
    return pl.BlockSpec((1, C), lambda i: (0, order(i)))


def shape_of(shape, kind):
    return jax.ShapeDtypeStruct(shape, kind)


PARAMS = pltpu.CompilerParams(vmem_limit_bytes=LIMIT)


def on_device(
    tokens, doc_ids, w_query, w_key, w_value, w_slots, w_output, w_hidden, w_return,
    gain_first, shift_first, gain_second, shift_second, bias_hidden, bias_return, cotangent,
):
    rows = tokens.shape[0]
    steps = rows // C
    seq = lax.axis_index("seq")
    gather = lambda a: lax.all_gather(a.astype(BF16), "fsdp", axis=0, tiled=True)
    w_qkvf = gather(jnp.concatenate([w_query, w_key, w_value, w_slots], axis=1))
    w_o, w_h, w_r = gather(w_output), gather(w_hidden), gather(w_return)
    smalls = lax.all_gather(
        jnp.concatenate(
            [gain_first, shift_first, gain_second, shift_second, bias_return, bias_hidden]
        ).astype(BF16),
        "fsdp",
    ).astype(F32)
    part = gain_first.shape[0]
    small = jnp.stack([smalls[:, n * part : (n + 1) * part].reshape(-1) for n in range(5)])
    small = jnp.concatenate([small, jnp.zeros((3, D), F32)], axis=0)
    bias = smalls[:, 5 * part :].reshape(1, FF)
    doc_col = jnp.broadcast_to(doc_ids.reshape(rows, 1), (rows, 128))
    pieces = doc_ids.reshape(steps, C)
    edges = jnp.concatenate([pieces[:, 0], pieces[:, -1]])
    edges = jnp.broadcast_to(edges[:, None], (2 * steps, D))

    qkvf, tail = pl.pallas_call(
        project_kernel,
        grid=(steps,),
        in_specs=[rows_of(D), rows_of(128), whole(16, D), whole(8, D), whole(D, 4 * D)],
        out_specs=[rows_of(4 * D), whole(136, D)],
        out_shape=[shape_of((rows, 4 * D), BF16), shape_of((136, D), F32)],
        compiler_params=PARAMS,
        name="project",
    )(tokens, doc_col, edges, small, w_qkvf)
    tails = lax.all_gather(tail, "seq")
    use = (jnp.arange(4) < seq) & (tails[:, 129, 0] == edges[0, 0].astype(F32))
    start = jnp.sum(jnp.where(use[:, None, None], tails, 0.0), axis=0)

    attended, probs, score, inverse, kept = pl.pallas_call(
        attend_kernel,
        grid=(steps,),
        in_specs=[rows_of(4 * D), rows_of(128), row_of(), whole(16, D), whole(136, D)],
        out_specs=[rows_of(D)] * 4 + [pl.BlockSpec((1, 128, D), lambda i: (i, 0, 0))],
        out_shape=[shape_of((rows, D), BF16)]
        + [shape_of((rows, D), F32)] * 3
        + [shape_of((steps, 128, D), F32)],
        scratch_shapes=[pltpu.VMEM((136, D), F32)],
        compiler_params=PARAMS,
        name="attend",
    )(qkvf, doc_col, doc_ids, edges, start)

    out, grad_middle, grad_attended, g_wo, g_wh, g_wr, g_small, g_bias = pl.pallas_call(
        forward_kernel,
        grid=(steps,),
        in_specs=[rows_of(D)] * 3
        + [whole(8, D), whole(1, FF), whole(D, D), whole(D, FF), whole(FF, D)],
        out_specs=[rows_of(D)] * 3
        + [whole(D, D), whole(D, FF), whole(D, FF), whole(8, D), whole(1, FF)],
        out_shape=[
            shape_of((rows, D), BF16),
            shape_of((rows, D), F32),
            shape_of((rows, D), BF16),
            shape_of((D, D), F32),
            shape_of((D, FF), F32),
            shape_of((D, FF), F32),
            shape_of((8, D), F32),
            shape_of((1, FF), F32),
        ],
        scratch_shapes=[pltpu.VMEM((C, FF), BF16)],
        compiler_params=PARAMS,
        name="feed",
    )(tokens, attended, cotangent, small, bias, w_o, w_h, w_r)

    grad_q, reading, grad_numer, grad_total, head = pl.pallas_call(
        row_kernel,
        grid=(steps,),
        in_specs=[rows_of(4 * D)]
        + [rows_of(D)] * 4
        + [pl.BlockSpec((1, 128, D), lambda i: (i, 0, 0)), rows_of(128), row_of(), whole(16, D)],
        out_specs=[rows_of(D)] * 4 + [whole(136, D)],
        out_shape=[
            shape_of((rows, D), BF16),
            shape_of((rows, D), BF16),
            shape_of((rows, D), F32),
            shape_of((rows, D), F32),
            shape_of((136, D), F32),
        ],
        compiler_params=PARAMS,
        name="rowside",
    )(qkvf, grad_attended, probs, score, inverse, kept, doc_col, doc_ids, edges)
    heads = lax.all_gather(head, "seq")
    use = (jnp.arange(4) > seq) & (heads[:, 129, 0] == edges[-1, 0].astype(F32))
    finish = jnp.sum(jnp.where(use[:, None, None], heads, 0.0), axis=0)

    back = lambda i: steps - 1 - i
    grads, g_qkvf = pl.pallas_call(
        column_kernel,
        grid=(steps,),
        in_specs=[rows_of(D, back), rows_of(4 * D, back)]
        + [rows_of(D, back)] * 5
        + [rows_of(128, back), row_of(back), whole(16, D), whole(8, D), whole(136, D)],
        out_specs=[rows_of(4 * D, back), whole(D, 4 * D)],
        out_shape=[shape_of((rows, 4 * D), BF16), shape_of((D, 4 * D), F32)],
        scratch_shapes=[pltpu.VMEM((136, D), F32)],
        compiler_params=PARAMS,
        name="colside",
    )(
        tokens, qkvf, grad_attended, grad_q, reading, grad_numer, grad_total, doc_col, doc_ids,
        edges, small, finish,
    )

    grad_input, g_small_one = pl.pallas_call(
        input_kernel,
        grid=(steps,),
        in_specs=[rows_of(D), rows_of(4 * D), rows_of(D), whole(D, 4 * D), whole(8, D)],
        out_specs=[rows_of(D), whole(8, D)],
        out_shape=[shape_of((rows, D), F32), shape_of((8, D), F32)],
        compiler_params=PARAMS,
        name="inputside",
    )(tokens, grads, grad_middle, w_qkvf, small)

    scatter = lambda a, dim=0: lax.psum(
        lax.psum_scatter(a, "fsdp", scatter_dimension=dim, tiled=True), "seq"
    )
    g_qkvf = scatter(g_qkvf)
    g_wo, g_wh, g_wr = scatter(g_wo), scatter(g_wh), scatter(g_wr, 1).T
    vector = jnp.concatenate(
        [g_small_one[0], g_small_one[1], g_small[2], g_small[3], g_bias[0], g_small[4]]
    )
    vector = lax.psum(vector, ("fsdp", "seq"))
    at = lax.axis_index("fsdp")
    pick = lambda start, size: lax.dynamic_slice(vector, (start + at * size,), (size,))
    return (
        out,
        grad_input,
        g_qkvf[:, 0:D],
        g_qkvf[:, D : 2 * D],
        g_qkvf[:, 2 * D : 3 * D],
        g_qkvf[:, 3 * D :],
        g_wo,
        g_wh,
        g_wr,
        pick(0, part),
        pick(D, part),
        pick(2 * D, part),
        pick(3 * D, part),
        pick(4 * D, 4 * part),
        pick(4 * D + FF, part),
    )


def solution(mesh):
    tall, flat, one = P(("fsdp", "seq"), None), P("fsdp", None), P("fsdp")
    return jax.shard_map(
        on_device,
        mesh=mesh,
        in_specs=(tall, P("fsdp", "seq")) + (flat,) * 7 + (one,) * 6 + (tall,),
        out_specs=(tall, tall) + (flat,) * 7 + (one,) * 6,
        check_vma=False,
    )
```

time: 2040 us -> 697 us (0.34)
  matrix products: 824 us -> 0 us
  local copies, waits for them, and re-layouts: 334 us -> 15.9 us
  blocking collectives: 381 us -> 108 us
  Pallas kernels: 0 us -> 168 us
  other arithmetic: 110 us -> 14.3 us
  waiting for transfers between devices: 283 us -> 374 us
  loops' own time: 48.3 us -> 0 us
  starting transfers between devices: 26.9 us -> 0.63 us
    dot_general x485 -> x0, matrix products: 801 us -> none  [the longest x64 157 us: advance(): affinity = jnp.dot(q_rows, k_rows.T, precision=HIGH) * visible]
    pallas_call x0 -> x6, Pallas kernels: none -> 168 us  [the longest x1 53.7 us: on_device(): pl.pallas_call(forward_kernel, grid=(steps,), in_specs=[rows_of(D)] * 3 +...]
    all_gather x7 -> x2, blocking collectives: 202 us -> 66.5 us  [the longest x1 34.2 us: on_device(): lax.all_gather(a.astype(BF16), 'fsdp', axis=0, tiled=True)]
    all_to_all x4 -> x0, blocking collectives: 113 us -> none  [the longest x1 28.3 us: on_device(): lax.all_to_all(merge_heads(grad_q), 'seq', split_axis=0, concat_axis=1, t...]
    unnamed x148 -> x28, local copies, waits for them, and re-layouts: 91.2 us -> 5.08 us
    all_gather x2 -> x5, waiting for transfers between devices: 0.02 us -> 79.7 us  [the longest x3 67 us: on_device(): lax.all_gather(a.astype(BF16), 'fsdp', axis=0, tiled=True)]
    unnamed x2 -> x0, blocking collectives: 59.8 us -> none
    transpose x10 -> x0, local copies, waits for them, and re-layouts: 54.4 us -> none  [the longest x8 43.6 us: mix_head(): final, outputs = lax.scan(jax.checkpoint(advance), start, pieces)]
  transfers between devices with their start and end apart: 16 -> 10, of which waited for: 5 -> 9; matrix products, arithmetic and copies ran while one was open for 59% -> 3% of each run, Pallas kernels for 0% -> 11%
where the time goes in v1:
time: 697 us; the launch traced here: 696 us
  waiting for transfers between devices  374 us (54%)
  Pallas kernels  168 us (24%)
  blocking collectives  108 us (15%)
  local copies, waits for them, and re-layouts  15.9 us (2%)
  between operations  15.6 us (2%)
  other arithmetic  14.3 us (2%)
    reduce_scatter x4, waiting for transfers between devices, on_device(): lax.psum_scatter(a, 'fsdp', scatter_dimension=dim, tiled=True)  287 us
    all_gather x3, waiting for transfers between devices, on_device(): lax.all_gather(a.astype(BF16), 'fsdp', axis=0, tiled=True)  67 us
    pallas_call x1, Pallas kernels, on_device(): pl.pallas_call(forward_kernel, grid=(steps,), in_specs=[rows_of(D)] * 3 +...  53.7 us
    psum x1, blocking collectives, on_device(): vector = lax.psum(vector, ('fsdp', 'seq'))  41.2 us
    pallas_call x1, Pallas kernels, on_device(): pl.pallas_call(column_kernel, grid=(steps,), in_specs=[rows_of(D, back),...  37.7 us
    all_gather x1, blocking collectives, on_device(): lax.all_gather(a.astype(BF16), 'fsdp', axis=0, tiled=True)  34.2 us
    all_gather x1, blocking collectives, on_device(): lax.all_gather(jnp.concatenate([gain_first, shift_first, gain_second, shi...  32.3 us
    pallas_call x1, Pallas kernels, on_device(): pl.pallas_call(row_kernel, grid=(steps,), in_specs=[rows_of(4 * D)] + [ro...  25 us
  transfers between devices with their start and end apart: 10, of which 9 were waited for; matrix products, arithmetic and copies ran while one was open for 3% of the time, Pallas kernels for 11%

profile of v1, /device:TPU:0, one launch (start us, length us, event | category | flops | bytes accessed | tf_op | source)
XLA Modules:
  0.0 696.1 jit_solution(12680494735774976970)
XLA Ops:
  7.2 0.9 convert.42
  8.1 0.9 convert.43
  9.1 0.9 convert.44
  10.0 0.9 convert.45
  10.9 0.7 pad_maximum_fusion
  11.7 0.7 convert.41
  12.4 0.7 convert_bitcast_fusion.4
  13.0 0.7 convert_bitcast_fusion
  13.7 0.7 convert_bitcast_fusion.2
  14.5 32.3 %all-gather.2 = bf16[8,1,576]{2,1,0:T(2,128)(2,1)S(1)} all-gather(bf16[1,1,576]{2,1,0:T(2,128)(2,1)S(1)} %bitcast.45), channel_id=1, replica_groups=mesh['seq'=4,'fsdp'=8] {'fsdp'}, dimensions={0}, use_global_device_ids=true | all-gather | bytes 10368 | tf_op jit(solution)/shard_map/all_gather | solution.py:453
  47.8 1.4 reduce.3
  49.4 0.6 concatenate.44.small_ref
  50.1 13.9 %all-gather.9.cloned.1.call-done.w_ref = bf16[512,2048]{1,0:T(8,128)(2,1)} async-done(((bf16[64,2048]{1,0:T(8,128)(2,1)}), bf16[512,2048]{1,0:T(8,128)(2,1)}) %all-gather.9.cloned.1.call-update) | async-done | bytes 2097168 | tf_op jit(solution)/shard_map/all_gather | solution.py:450
  64.0 0.7 broadcast_in_dim.42.edge_ref
  64.7 2.0 broadcast_in_dim.41.col_ref
  66.7 13.7 %project.1 = (bf16[2048,2048]{1,0:T(8,128)(2,1)}, f32[136,512]{1,0:T(8,128)}) custom-call(bf16[2048,512]{1,0:T(8,128)(2,1)} %x_ref.7, s32[2048,128]{1,0:T(8,128)} %broadcast_in_dim.41.col_ref, s32[16,512]{1,0:T(8,128)} %broadcast_in_dim.42.edge_ref, f32[8,512]{1,0:T(8,128)} %concatenate.44.small_ref, bf16[512,2048]{1,0:T(8,128)(2,1)} %all-gather.9.cloned.1.call-done.w_ref), custom_call_target="tpu_custom_call" | custom-call | tf_op jit(solution)/shard_map/project/pallas_call | solution.py:468
  80.5 0.7 convert_element_type.37
  81.4 0.7 convert_element_type.38
  83.5 0.6 copy.46
  84.1 34.2 %all_gather.32.wo_ref = bf16[512,512]{1,0:T(8,128)(2,1)} all-gather(bf16[64,512]{1,0:T(8,128)(2,1)S(1)} %convert_element_type.36), channel_id=1, replica_groups=mesh['seq'=4,'fsdp'=8] {'fsdp'}, dimensions={0}, use_global_device_ids=true | all-gather | bytes 589824 | tf_op jit(solution)/shard_map/all_gather | solution.py:450
  118.3 0.7 slice.99
  119.1 2.2 select_reduce_fusion.1.start_ref
  121.3 24.8 %attend.1 = (bf16[2048,512]{1,0:T(8,128)(2,1)}, f32[2048,512]{1,0:T(8,128)}, f32[2048,512]{1,0:T(8,128)}, f32[2048,512]{1,0:T(8,128)}, f32[8,128,512]{2,1,0:T(8,128)}) custom-call(bf16[2048,2048]{1,0:T(8,128)(2,1)} %get-tuple-element.39.qkvf_ref, s32[2048,128]{1,0:T(8,128)} %broadcast_in_dim.41.col_ref, s32[1,2048]{1,0:T(1,128)} %row_ref.5, ...), custom_call_target="tpu_custom_call" | custom-call | tf_op jit(solution)/shard_map/attend/pallas_call | solution.py:481
  146.1 2.7 all-gather.11.cloned.1.call-done.wh_ref
  148.8 50.4 %all-gather.13.cloned.1.call-done.wr_ref = bf16[2048,512]{1,0:T(8,128)(2,1)} async-done(((bf16[256,512]{1,0:T(8,128)(2,1)}), bf16[2048,512]{1,0:T(8,128)(2,1)}) %all-gather.13.cloned.1.call-update) | async-done | bytes 2097168 | tf_op jit(solution)/shard_map/all_gather | solution.py:450
  199.2 53.7 %feed.1 = (bf16[2048,512]{1,0:T(8,128)(2,1)}, f32[2048,512]{1,0:T(8,128)}, bf16[2048,512]{1,0:T(8,128)(2,1)}, f32[512,512]{1,0:T(8,128)}, f32[512,2048]{1,0:T(8,...) custom-call(bf16[2048,512]{1,0:T(8,128)(2,1)} %x_ref.7, ...), custom_call_target="tpu_custom_call" | custom-call | tf_op jit(solution)/shard_map/feed/pallas_call | solution.py:494
  252.9 25.0 %rowside.1 = (bf16[2048,512]{1,0:T(8,128)(2,1)}, bf16[2048,512]{1,0:T(8,128)(2,1)}, f32[2048,512]{1,0:T(8,128)}, f32[2048,512]{1,0:T(8,128)}, f32[136,512]{1,0:T(8,128)}) custom-call(bf16[2048,2048]{1,0:T(8,128)(2,1)} %get-tuple-element.39.qkvf_ref, bf16[2048,512]{1,0:T(8,128)(2,1)} %get-tuple-element.43.do_ref, f32[2048,512]{1,0:T(8,128)} %get-tuple-element.44.p_ref, ...), custom_call_target="tpu_custom_call" | custom-call | tf_op jit(solution)/shard_map/rowside/pallas_call | solution.py:516
  278.5 0.7 reduce-scatter.11.cloned.1.call-update
  279.3 0.7 reduce-scatter.9.cloned.1.call-update
  280.9 12.7 %all-gather.17.cloned.1.call-done = f32[544,512]{1,0:T(8,128)} async-done(((f32[136,512]{1,0:T(8,128)}), f32[544,512]{1,0:T(8,128)}) %all-gather.17.cloned.1.call-update) | async-done | bytes 1114128 | tf_op jit(solution)/shard_map/all_gather | solution.py:533
  293.7 0.7 slice.102
  294.5 2.2 select_reduce_fusion.start_ref
  296.6 37.7 %colside.1 = (bf16[2048,2048]{1,0:T(8,128)(2,1)}, f32[512,2048]{1,0:T(8,128)}) custom-call(bf16[2048,512]{1,0:T(8,128)(2,1)} %x_ref.7, bf16[2048,2048]{1,0:T(8,128)(2,1)} %get-tuple-element.39.qkvf_ref, bf16[2048,512]{1,0:T(8,128)(2,1)} %get-tuple-element.43.do_ref, bf16[2048,512]{1,0:T(8,128)(2,1)} %get-tuple-element.48.dq_ref, ...), custom_call_target="tpu_custom_call" | custom-call | tf_op jit(solution)/shard_map/colside/pallas_call | solution.py:538
  334.4 0.8 fusion.3
  335.3 13.3 %inputside.1 = (f32[2048,512]{1,0:T(8,128)}, f32[8,512]{1,0:T(8,128)}) custom-call(bf16[2048,512]{1,0:T(8,128)(2,1)} %x_ref.7, bf16[2048,2048]{1,0:T(8,128)(2,1)} %get-tuple-element.53.d_ref, f32[2048,512]{1,0:T(8,128)} %get-tuple-element.54.dy_ref, bf16[512,2048]{1,0:T(8,128)(2,1)} %all-gather.9.cloned.1.call-done.w_ref, f32[8,512]{1,0:T(8,128)} %concatenate.44.small_ref), custom_call_target="tpu_custom_call" | custom-call | tf_op jit(solution)/shard_map/inputside/pallas_call | solution.py:554
  348.5 11.9 %reduce-scatter.7.cloned.1.call-done = f32[64,512]{1,0:T(8,128)} async-done(((f32[512,512]{1,0:T(8,128)}), f32[64,512]{1,0:T(8,128)}) %reduce-scatter.7.cloned.1.call-update) | async-done | bytes 131088 | tf_op jit(solution)/shard_map/reduce_scatter | solution.py:565
  360.4 91.6 %reduce-scatter.11.cloned.1.call-done = f32[512,256]{1,0:T(8,128)} async-done(((f32[512,2048]{1,0:T(8,128)}), f32[512,256]{1,0:T(8,128)}) %reduce-scatter.11.cloned.1.call-update) | async-done | bytes 524304 | tf_op jit(solution)/shard_map/reduce_scatter | solution.py:565
  452.0 91.3 %reduce-scatter.9.cloned.1.call-done = f32[64,2048]{1,0:T(8,128)} async-done(((f32[512,2048]{1,0:T(8,128)}), f32[64,2048]{1,0:T(8,128)}) %reduce-scatter.9.cloned.1.call-update) | async-done | bytes 524304 | tf_op jit(solution)/shard_map/reduce_scatter | solution.py:565
  543.3 91.8 %reduce-scatter.5.cloned.1.call-done = f32[64,2048]{1,0:T(8,128)} async-done(((f32[512,2048]{1,0:T(8,128)}), f32[64,2048]{1,0:T(8,128)}) %reduce-scatter.5.cloned.1.call-update) | async-done | bytes 524304 | tf_op jit(solution)/shard_map/reduce_scatter | solution.py:565
  635.1 0.8 fusion.4
  636.0 41.2 %psum.39 = f32[4608]{0:T(1024)S(1)} all-reduce(f32[4608]{0:T(1024)S(1)} %constant_dynamic-update-slice_fusion), channel_id=1, replica_groups=mesh['seq'=4,'fsdp'=8] {'fsdp','seq'}, use_global_device_ids=true, to_apply=%region_10.11 | all-reduce | flops 4608 | bytes 36864 | tf_op jit(solution)/shard_map/psum | solution.py:572
  677.1 0.6 dynamic_slice.22
  677.8 0.6 fusion.1
  678.4 5.5 all-reduce.3.cloned.1.call-done
  683.8 2.0 fusion
  685.8 2.0 copy.40
  687.8 0.7 copy.59
  688.5 0.8 copy.60
  (61 shorter events, 3.6 us)
Async XLA Ops:
  7.2 56.8 %all-gather.9.cloned.1.call-start = ((), (), s32[]{:S(2)}) async-start(), calls=%async_computation.4 | async-start | bytes 2359296 | tf_op jit(solution)/shard_map/all_gather | solution.py:450
  11.6 106.7 %all-gather.15.cloned.1.call-start = ((), (), s32[]{:S(2)}) async-start(), calls=%async_computation.11 | async-start | bytes 1392640 | tf_op jit(solution)/shard_map/all_gather | solution.py:477
  66.7 13.8 %copy-start = (f32[64,2048]{1,0:T(8,128)S(1)}, f32[64,2048]{1,0:T(8,128)}, u32[]{:S(2)}) copy-start(f32[64,2048]{1,0:T(8,128)} %param.23) | copy-start | bytes 1572868
  66.7 14.6 %copy-start.1 = (f32[256,512]{1,0:T(8,128)S(1)}, f32[256,512]{1,0:T(8,128)}, u32[]{:S(2)}) copy-start(f32[256,512]{1,0:T(8,128)} %param.24) | copy-start | bytes 1572868
  80.5 3.6 copy-start.3
  80.5 68.4 %all-gather.11.cloned.1.call-start = ((), (), s32[]{:S(2)}) async-start(), calls=%async_computation.5 | async-start | bytes 2359296 | tf_op jit(solution)/shard_map/all_gather | solution.py:450
  81.3 117.9 %all-gather.13.cloned.1.call-start = ((), (), s32[]{:S(2)}) async-start(), calls=%async_computation.6 | async-start | bytes 2359296 | tf_op jit(solution)/shard_map/all_gather | solution.py:450
  82.1 211.5 %all-gather.17.cloned.1.call-start = ((), (), s32[]{:S(2)}) async-start(), calls=%async_computation.12 | async-start | bytes 1392640 | tf_op jit(solution)/shard_map/all_gather | solution.py:533
  277.9 82.5 %reduce-scatter.7.cloned.1.call-start = ((), (), s32[]{:S(2)}) async-start(), calls=%async_computation.8 | async-start | bytes 1179648 | tf_op jit(solution)/shard_map/reduce_scatter | solution.py:565
  278.5 173.5 %reduce-scatter.11.cloned.1.call-start = ((), (), s32[]{:S(2)}) async-start(), calls=%async_computation.10 | async-start | bytes 4718592 | tf_op jit(solution)/shard_map/reduce_scatter | solution.py:565
  279.2 264.1 %reduce-scatter.9.cloned.1.call-start = ((), (), s32[]{:S(2)}) async-start(), calls=%async_computation.9 | async-start | bytes 4718592 | tf_op jit(solution)/shard_map/reduce_scatter | solution.py:565
  280.0 355.1 %reduce-scatter.5.cloned.1.call-start = ((), (), s32[]{:S(2)}) async-start(), calls=%async_computation.7 | async-start | bytes 4718592 | tf_op jit(solution)/shard_map/reduce_scatter | solution.py:565
  334.4 349.5 %all-reduce.3.cloned.1.call-start = ((), (), s32[]{:S(2)}) async-start(), calls=%async_computation.13 | async-start | bytes 3407872 | tf_op jit(solution)/shard_map/psum | solution.py:564
  335.3 300.7 %copy-start.5 = (f32[1,2048]{1,0:T(1,128)S(1)}, f32[1,2048]{1,0:T(1,128)}, u32[]{:S(2)}) copy-start(f32[1,2048]{1,0:T(1,128)} %get-tuple-element.62) | copy-start | bytes 24580
  683.8 4.0 copy-start.4
  683.8 4.7 copy-start.2
Sparse Core Ops, SparseCore 0:
  11.8 52.2 all-gather.8
  80.6 15.5 all-gather.14
  98.9 49.8 all-gather.10
  151.4 47.7 all-gather.12
  278.0 15.5 all-gather.16
  296.9 63.4 reduce-scatter.6
  364.5 87.4 reduce-scatter.10
  455.6 87.6 reduce-scatter.8
  547.4 87.6 reduce-scatter.4
  637.5 46.2 all-reduce.2

commit v2 on v1

--- a/solution.py
+++ b/solution.py
@@ -150,44 +150,15 @@
     return jnp.concatenate(one, axis=1), jnp.concatenate(two, axis=1)
 
 
-def project_kernel(x_ref, col_ref, edge_ref, small_ref, w_ref, qkvf_ref, tail_ref):
-    step = pl.program_id(0)
-    unit, _ = norm_parts(x_ref[...].astype(F32))
-    hidden = (unit * small_ref[0:1] + small_ref[1:2]).astype(BF16)
-    rows = dot(hidden, w_ref[...]).astype(BF16)
-    qkvf_ref[...] = rows
-    written = jnp.exp(rows[:, 3 * D :].astype(F32))
-    newest = edge_ref[15:16]
-    tail = wide(flag(col_ref[...], newest), 4) * written
-    slots = tail.astype(BF16)
-    keys, values = state_terms(slots, rows[:, D : 2 * D], rows[:, 2 * D : 3 * D])
-
-    @pl.when(step == 0)
-    def _():
-        tail_ref[...] = jnp.zeros_like(tail_ref)
-        tail_ref[129:130] = newest.astype(F32)
-
-    tail_ref[0:64] += keys
-    tail_ref[64:128] += values
-    tail_ref[128:129] += jnp.sum(slots.astype(F32), axis=0, keepdims=True)
-
-
-def attend_kernel(
-    qkvf_ref, col_ref, row_ref, edge_ref, start_ref, o_ref, p_ref, s_ref, z_ref, kept_ref, state
+def attend_body(
+    n, qkvf_ref, col, row, edge_ref, state, o_ref, p_ref, s_ref, z_ref, kept_ref
 ):
-    step = pl.program_id(0)
-
-    @pl.when(step == 0)
-    def _():
-        state[...] = start_ref[...]
-
     kept_ref[0] = state[0:128]
     first = edge_ref[pl.ds(0, 1)]
-    before = edge_ref[pl.ds(8 + jnp.maximum(step - 1, 0), 1)]
-    last = jnp.where(step == 0, first, before)
-    newest = edge_ref[pl.ds(8 + step, 1)]
-    col = col_ref[...]
-    vis = visible(col, row_ref[...])
+    before = edge_ref[pl.ds(8 + jnp.maximum(n - 1, 0), 1)]
+    last = jnp.where(n == 0, first, before)
+    newest = edge_ref[pl.ds(8 + n, 1)]
+    vis = visible(col, row)
     carried = wide(flag(col, last), 2)
     written = jnp.exp(qkvf_ref[:, 3 * D :].astype(F32))
     slots = written.astype(BF16)
@@ -220,6 +191,407 @@
     state[0:64] = same * state[0:64] + new_keys
     state[64:128] = same * state[64:128] + new_values
     state[128:129] = same * state[128:129] + jnp.sum(tail.astype(F32), axis=0, keepdims=True)
+
+
+MESH_ID = pl.DeviceIdType.MESH
+
+
+def places():
+    seq, at = lax.axis_index("seq"), lax.axis_index("fsdp")
+    core = lax.rem(seq, 2)
+    return seq, at, seq + 1 - 2 * core, lax.rem(seq + 2, 4)
+
+
+def push(src, dst, send, recv, **device):
+    return pltpu.make_async_remote_copy(
+        src_ref=src, dst_ref=dst, send_sem=send, recv_sem=recv,
+        device_id=device, device_id_type=MESH_ID,
+    )
+
+
+def greet(count):
+    seq, at, _, _ = places()
+    barrier = pltpu.get_barrier_semaphore()
+    for k in range(1, count):
+        pl.semaphore_signal(barrier, inc=1, device_id={"fsdp": at ^ k}, device_id_type=MESH_ID)
+    for k in range(1, 4):
+        pl.semaphore_signal(barrier, inc=1, device_id={"seq": seq ^ k}, device_id_type=MESH_ID)
+    pl.semaphore_wait(barrier, count - 1 + 3)
+
+
+class Gather:
+    def __init__(self, count, mine, held, sems):
+        self.count, self.mine, self.held = count, mine, held
+        self.across, self.core, self.chip, self.onward, self.local = sems
+        self.seq, self.at, self.sibling, self.beside = places()
+        self.quarter = held.shape[2] // 4
+
+    def lanes(self, seq):
+        return pl.ds(pl.multiple_of(seq * self.quarter, self.quarter), self.quarter)
+
+    def part(self, owner, seq):
+        return self.held.at[owner, :, self.lanes(seq)]
+
+    def first(self, k):
+        return push(
+            self.mine.at[:, self.lanes(self.seq)], self.part(self.at, self.seq),
+            self.across[0].at[k], self.across[1].at[k], fsdp=self.at ^ k,
+        )
+
+    def first_in(self, k):
+        here = self.part(self.at ^ k, self.seq)
+        return push(here, here, self.across[0].at[k], self.across[1].at[k], fsdp=self.at ^ k)
+
+    def own(self):
+        return pltpu.make_async_copy(
+            self.mine.at[:, self.lanes(self.seq)], self.part(self.at, self.seq), self.local
+        )
+
+    def start(self):
+        for k in range(1, self.count):
+            self.first(k).start()
+        self.own().start()
+
+    def hop(self, sems, source, target, k):
+        if k is None:
+            ref, n = self.held.at[:, :, self.lanes(source)], 0
+        else:
+            ref, n = self.part(self.at ^ k, source), k
+        return push(ref, ref, sems[0].at[n], sems[1].at[n], seq=target)
+
+    def sent(self, n, k):
+        if n == 0:
+            return self.hop(self.core, self.seq, self.sibling, k)
+        if n == 1:
+            return self.hop(self.chip, self.seq, self.beside, k)
+        return self.hop(self.onward, self.beside, self.sibling, k)
+
+    def come(self, n, k):
+        if n == 0:
+            return self.hop(self.core, self.sibling, self.sibling, k)
+        if n == 1:
+            return self.hop(self.chip, self.beside, self.beside, k)
+        return self.hop(self.onward, lax.rem(self.sibling + 2, 4), self.sibling, k)
+
+    def second(self):
+        self.own().wait()
+        for k in range(1, self.count):
+            self.first_in(k).wait_recv()
+        self.sent(0, None).start()
+        self.sent(1, None).start()
+
+    def third(self):
+        self.come(1, None).wait_recv()
+        self.sent(2, None).start()
+
+    def finish(self):
+        for n in range(3):
+            self.sent(n, None).wait_send()
+        self.come(0, None).wait_recv()
+        self.come(2, None).wait_recv()
+        for k in range(1, self.count):
+            self.first(k).wait_send()
+
+    def second_each(self):
+        for k in range(self.count):
+            if k:
+                self.first_in(k).wait_recv()
+            else:
+                self.own().wait()
+            self.sent(0, k).start()
+            self.sent(1, k).start()
+        for k in range(self.count):
+            self.come(1, k).wait_recv()
+            self.sent(2, k).start()
+        for k in range(self.count):
+            self.come(0, k).wait_recv()
+            self.come(2, k).wait_recv()
+
+    def drain_each(self):
+        for k in range(self.count):
+            for n in range(3):
+                self.sent(n, k).wait_send()
+        for k in range(1, self.count):
+            self.first(k).wait_send()
+
+
+def gather_sems(count, each):
+    n = count if each else 1
+    pair = lambda size: [pltpu.SemaphoreType.DMA((size,)), pltpu.SemaphoreType.DMA((size,))]
+    return pair(count) + pair(n) + pair(n) + pair(n) + [pltpu.SemaphoreType.DMA]
+
+
+def bundle(refs):
+    return (refs[0], refs[1]), (refs[2], refs[3]), (refs[4], refs[5]), (refs[6], refs[7]), refs[8]
+
+
+class States:
+    def __init__(self, big, small, sems):
+        self.refs, self.sems = (big, small), sems
+        self.seq, _, self.sibling, self.beside = places()
+
+    def hop(self, n, source, target):
+        out = []
+        for m, ref in enumerate(self.refs):
+            here = ref.at[source]
+            out.append(push(here, here, self.sems[0].at[n, m], self.sems[1].at[n, m], seq=target))
+        return out
+
+    def start(self):
+        for copy in self.hop(0, self.seq, self.sibling) + self.hop(1, self.seq, self.beside):
+            copy.start()
+
+    def finish(self):
+        for copy in self.hop(1, self.beside, self.beside):
+            copy.wait_recv()
+        for copy in self.hop(2, self.beside, self.sibling):
+            copy.start()
+        for copy in self.hop(0, self.sibling, self.sibling):
+            copy.wait_recv()
+        for copy in self.hop(2, lax.rem(self.sibling + 2, 4), self.sibling):
+            copy.wait_recv()
+
+    def drain(self):
+        for copy in (
+            self.hop(0, self.seq, self.sibling)
+            + self.hop(1, self.seq, self.beside)
+            + self.hop(2, self.beside, self.sibling)
+        ):
+            copy.wait_send()
+
+
+def doc_parts(doc_ref, col_ref, edge_ref):
+    here = lax.broadcasted_iota(jnp.int32, (C, C), 0)
+    there = lax.broadcasted_iota(jnp.int32, (C, C), 1)
+    eye = jnp.where(here == there, 1.0, 0.0).astype(BF16)
+    for n in range(doc_ref.shape[1] // C):
+        row = doc_ref[:, n * C : (n + 1) * C].astype(F32)
+        col_ref[n * C : (n + 1) * C] = dot_nt(eye, jnp.broadcast_to(row, (128, C)).astype(BF16))
+        low = jnp.min(row, axis=1, keepdims=True)
+        high = jnp.max(row, axis=1, keepdims=True)
+        edge_ref[n : n + 1] = jnp.broadcast_to(low, (1, D))
+        edge_ref[n + 8 : n + 9] = jnp.broadcast_to(high, (1, D))
+
+
+def spread_small(vec_refs, bias_ref, out_ref):
+    part = vec_refs[0].shape[1]
+
+    def repeat(values):
+        width = values.shape[1]
+        rows = lax.broadcasted_iota(jnp.int32, (width, D), 0)
+        lanes = lax.broadcasted_iota(jnp.int32, (width, D), 1)
+        pick = jnp.where(lax.rem(lanes, width) == rows, 1.0, 0.0).astype(BF16)
+        return dot(jnp.broadcast_to(values, (8, width)).astype(BF16), pick)[0:1]
+
+    out_ref[...] = jnp.zeros_like(out_ref)
+    for n, ref in enumerate(vec_refs):
+        out_ref[n : n + 1] = repeat(ref[...])
+    out_ref[5:6] = repeat(bias_ref[...])
+    return part
+
+
+def join_small(count, part, gathered, vec_ref, bias_ref):
+    lanes = lax.broadcasted_iota(jnp.int32, (8, D), 1)
+    total = jnp.zeros((8, D), F32)
+    for f in range(count):
+        total = jnp.where(lanes // part == f, gathered[f], total)
+    vec_ref[...] = total
+    for r in range(4):
+        row = jnp.zeros((8, D), F32)
+        for f in range(count):
+            row = jnp.where((lanes + r * D) // (4 * part) == f, gathered[f], row)
+        bias_ref[0:1, r * D : (r + 1) * D] = row[5:6]
+
+
+def front_kernel(
+    count, x_ref, doc_ref, wq_ref, wk_ref, wv_ref, ws_ref, wo_ref, wh_ref, wr_ref,
+    v0, v1, v2, v3, v4, bias_in,
+    qkvf_out, o_ref, p_ref, s_ref, z_ref, kept_ref, w_out, wo_out, wh_out, wr_out, vec_out, bias_out,
+    qkvf, hidden, w_all, mine, mine_o, mine_h, mine_r, spread, smalls, col_ref, edge_ref, state,
+    tail, tails, tail_rows, *sems,
+):
+    step = pl.program_id(0)
+    seq, at, _, _ = places()
+    link = mine.dtype
+    first_sems, sems = bundle(sems[:9]), sems[9:]
+    o_sems, sems = bundle(sems[:9]), sems[9:]
+    h_sems, sems = bundle(sems[:9]), sems[9:]
+    r_sems, sems = bundle(sems[:9]), sems[9:]
+    small_send, small_recv, state_send, state_recv, out_sem = sems
+    main = Gather(count, mine, w_all, first_sems)
+    later = [
+        Gather(count, mine_o, wo_out, o_sems),
+        Gather(count, mine_h, wh_out, h_sems),
+        Gather(count, mine_r, wr_out, r_sems),
+    ]
+    states = States(tails, tail_rows, (state_send, state_recv))
+
+    def small_copy(k, owner):
+        return push(
+            spread, smalls.at[owner], small_send.at[k], small_recv.at[k], fsdp=at ^ k
+        )
+
+    def save():
+        return (
+            pltpu.make_async_copy(qkvf, qkvf_out, out_sem.at[0]),
+            pltpu.make_async_copy(w_all, w_out, out_sem.at[1]),
+        )
+
+    @pl.when(step == 0)
+    def _():
+        greet(count)
+        for n, ref in enumerate((wq_ref, wk_ref, wv_ref, ws_ref)):
+            mine[:, n * D : (n + 1) * D] = ref[...].astype(BF16).astype(link)
+        spread_small((v0, v1, v2, v3, v4), bias_in, spread)
+        main.start()
+        for k in range(1, count):
+            small_copy(k, at).start()
+        mine_o[...] = wo_ref[...].astype(BF16).astype(link)
+        mine_h[...] = wh_ref[...].astype(BF16).astype(link)
+        mine_r[...] = wr_ref[...].astype(BF16).astype(link)
+        doc_parts(doc_ref, col_ref, edge_ref)
+        tail[...] = jnp.zeros_like(tail)
+        smalls[at] = spread[...]
+        main.second_each()
+        for k in range(1, count):
+            small_copy(k, at ^ k).wait_recv()
+        join_small(count, v0.shape[1], smalls, vec_out, bias_out)
+        for piece in later:
+            piece.start()
+
+    @pl.when(step < 8)
+    def _():
+        unit, _ = norm_parts(x_ref[...].astype(F32))
+        normed = (unit * vec_out[0:1] + vec_out[1:2]).astype(BF16)
+        here = pl.ds(pl.multiple_of(step * C, C), C)
+        hidden[here] = normed
+        weights = w_all[:, :, D:].reshape(D, 3 * D).astype(BF16)
+        rows = dot(normed, weights).astype(BF16)
+        qkvf[here, D:] = rows
+        slots = wide(flag(col_ref[here], edge_ref[15:16]), 4) * jnp.exp(rows[:, 2 * D :].astype(F32))
+        slots = slots.astype(BF16)
+        keys, values = state_terms(slots, rows[:, 0:D], rows[:, D : 2 * D])
+        tail[0:64] += keys
+        tail[64:128] += values
+        tail[128:129] += jnp.sum(slots.astype(F32), axis=0, keepdims=True)
+
+    @pl.when(step == 5)
+    def _():
+        for piece in later:
+            piece.second()
+
+    @pl.when(step == 7)
+    def _():
+        tails[seq] = tail[0:128].astype(link)
+        tail_rows[seq, 0:1] = tail[128:129]
+        tail_rows[seq, 1:2] = edge_ref[15:16]
+        tail_rows[seq, 2:8] = jnp.zeros((6, D), F32)
+        states.start()
+
+    @pl.when(step == 8)
+    def _():
+        @pl.loop(0, 8)
+        def _(n):
+            here = pl.ds(pl.multiple_of(n * C, C), C)
+            weights = w_all[:, :, 0:D].reshape(D, D).astype(BF16)
+            qkvf[here, 0:D] = dot(hidden[here], weights).astype(BF16)
+
+        for copy in save():
+            copy.start()
+        states.finish()
+        first = edge_ref[0:1]
+        state[...] = jnp.zeros_like(state)
+        for n in range(4):
+            use = jnp.where(tail_rows[n, 1:2] == first, 1.0, 0.0) * (n < seq).astype(F32)
+            state[0:128] += use * tails[n].astype(F32)
+            state[128:129] += use * tail_rows[n, 0:1]
+
+    @pl.when(step == 12)
+    def _():
+        for piece in later:
+            piece.third()
+
+    @pl.when(step >= 9)
+    def _():
+        n = step - 9
+        here = pl.ds(pl.multiple_of(n * C, C), C)
+        attend_body(
+            n, qkvf.at[here], col_ref[here], doc_ref[:, here].astype(F32), edge_ref,
+            state, o_ref, p_ref, s_ref, z_ref, kept_ref,
+        )
+
+    @pl.when(step == 16)
+    def _():
+        for piece in later:
+            piece.finish()
+        main.drain_each()
+        states.drain()
+        for k in range(1, count):
+            small_copy(k, at).wait_send()
+        for copy in save():
+            copy.wait()
+
+
+def front(count, tokens, doc_ids, weights, vectors, bias):
+    rows = tokens.shape[0]
+    part = weights[0].shape[0]
+    link = BF16 if part % 16 == 0 else F32
+    once = lambda a: pl.BlockSpec(a.shape, lambda i: (0,) * a.ndim)
+    early = lambda i: jnp.minimum(i, 7)
+    late = lambda i: jnp.maximum(i - 9, 0)
+    anywhere = pl.BlockSpec(memory_space=pl.ANY)
+    vmem = pltpu.VMEM
+    return pl.pallas_call(
+        functools.partial(front_kernel, count),
+        grid=(17,),
+        in_specs=[rows_of(D, early), once(doc_ids)] + [once(a) for a in (*weights, *vectors, bias)],
+        out_specs=[anywhere]
+        + [rows_of(D, late)] * 4
+        + [pl.BlockSpec((1, 128, D), lambda i: (late(i), 0, 0))]
+        + [anywhere] * 4
+        + [whole(8, D), whole(1, FF)],
+        out_shape=[shape_of((rows, 4 * D), BF16), shape_of((rows, D), BF16)]
+        + [shape_of((rows, D), F32)] * 3
+        + [
+            shape_of((8, 128, D), F32),
+            shape_of((count, part, 4 * D), link),
+            shape_of((count, part, D), link),
+            shape_of((count, part, FF), link),
+            shape_of((count, 4 * part, D), link),
+            shape_of((8, D), F32),
+            shape_of((1, FF), F32),
+        ],
+        scratch_shapes=[
+            vmem((rows, 4 * D), BF16),
+            vmem((rows, D), BF16),
+            vmem((count, part, 4 * D), link),
+            vmem((part, 4 * D), link),
+            vmem((part, D), link),
+            vmem((part, FF), link),
+            vmem((4 * part, D), link),
+            vmem((8, D), F32),
+            vmem((count, 8, D), F32),
+            vmem((rows, 128), F32),
+            vmem((16, D), F32),
+            vmem((136, D), F32),
+            vmem((136, D), F32),
+            vmem((4, 128, D), link),
+            vmem((4, 8, D), F32),
+        ]
+        + gather_sems(count, True)
+        + gather_sems(count, False) * 3
+        + [
+            pltpu.SemaphoreType.DMA((count,)),
+            pltpu.SemaphoreType.DMA((count,)),
+            pltpu.SemaphoreType.DMA((3, 2)),
+            pltpu.SemaphoreType.DMA((3, 2)),
+            pltpu.SemaphoreType.DMA((2,)),
+        ],
+        compiler_params=pltpu.CompilerParams(
+            vmem_limit_bytes=LIMIT, collective_id=1, has_side_effects=True
+        ),
+        name="front",
+    )(tokens, doc_ids, *weights, *vectors, bias)
 
 
 ROOT = 0.7978845608028654
@@ -447,49 +819,22 @@
     rows = tokens.shape[0]
     steps = rows // C
     seq = lax.axis_index("seq")
-    gather = lambda a: lax.all_gather(a.astype(BF16), "fsdp", axis=0, tiled=True)
-    w_qkvf = gather(jnp.concatenate([w_query, w_key, w_value, w_slots], axis=1))
-    w_o, w_h, w_r = gather(w_output), gather(w_hidden), gather(w_return)
-    smalls = lax.all_gather(
-        jnp.concatenate(
-            [gain_first, shift_first, gain_second, shift_second, bias_return, bias_hidden]
-        ).astype(BF16),
-        "fsdp",
-    ).astype(F32)
+    count = lax.axis_size("fsdp")
     part = gain_first.shape[0]
-    small = jnp.stack([smalls[:, n * part : (n + 1) * part].reshape(-1) for n in range(5)])
-    small = jnp.concatenate([small, jnp.zeros((3, D), F32)], axis=0)
-    bias = smalls[:, 5 * part :].reshape(1, FF)
+    flat = lambda a: a.reshape(1, a.shape[0])
+    qkvf, attended, probs, score, inverse, kept, w_qkvf, w_o, w_h, w_r, small, bias = front(
+        count, tokens, doc_ids,
+        (w_query, w_key, w_value, w_slots, w_output, w_hidden, w_return),
+        [flat(a) for a in (gain_first, shift_first, gain_second, shift_second, bias_return)],
+        flat(bias_hidden),
+    )
+    w_qkvf, w_o, w_h, w_r = (
+        a.reshape(-1, a.shape[2]).astype(BF16) for a in (w_qkvf, w_o, w_h, w_r)
+    )
     doc_col = jnp.broadcast_to(doc_ids.reshape(rows, 1), (rows, 128))
     pieces = doc_ids.reshape(steps, C)
     edges = jnp.concatenate([pieces[:, 0], pieces[:, -1]])
     edges = jnp.broadcast_to(edges[:, None], (2 * steps, D))
-
-    qkvf, tail = pl.pallas_call(
-        project_kernel,
-        grid=(steps,),
-        in_specs=[rows_of(D), rows_of(128), whole(16, D), whole(8, D), whole(D, 4 * D)],
-        out_specs=[rows_of(4 * D), whole(136, D)],
-        out_shape=[shape_of((rows, 4 * D), BF16), shape_of((136, D), F32)],
-        compiler_params=PARAMS,
-        name="project",
-    )(tokens, doc_col, edges, small, w_qkvf)
-    tails = lax.all_gather(tail, "seq")
-    use = (jnp.arange(4) < seq) & (tails[:, 129, 0] == edges[0, 0].astype(F32))
-    start = jnp.sum(jnp.where(use[:, None, None], tails, 0.0), axis=0)
-
-    attended, probs, score, inverse, kept = pl.pallas_call(
-        attend_kernel,
-        grid=(steps,),
-        in_specs=[rows_of(4 * D), rows_of(128), row_of(), whole(16, D), whole(136, D)],
-        out_specs=[rows_of(D)] * 4 + [pl.BlockSpec((1, 128, D), lambda i: (i, 0, 0))],
-        out_shape=[shape_of((rows, D), BF16)]
-        + [shape_of((rows, D), F32)] * 3
-        + [shape_of((steps, 128, D), F32)],
-        scratch_shapes=[pltpu.VMEM((136, D), F32)],
-        compiler_params=PARAMS,
-        name="attend",
-    )(qkvf, doc_col, doc_ids, edges, start)
 
     out, grad_middle, grad_attended, g_wo, g_wh, g_wr, g_small, g_bias = pl.pallas_call(
         forward_kernel,

time: 697 us -> 596 us (0.86)
  waiting for transfers between devices: 374 us -> 295 us
  blocking collectives: 108 us -> 41.2 us
  Pallas kernels: 168 us -> 225 us
  other arithmetic: 14.3 us -> 3.62 us
    all_gather x4 -> x0, waiting for transfers between devices: 67 us -> none  [the longest x3 67 us: on_device(): lax.all_gather(a.astype(BF16), 'fsdp', axis=0, tiled=True)]
    all_gather x2 -> x0, blocking collectives: 66.5 us -> none  [the longest x1 34.2 us: on_device(): lax.all_gather(a.astype(BF16), 'fsdp', axis=0, tiled=True)]
    pallas_call x2 -> x1, Pallas kernels: 38.5 us -> 95.5 us  [front(): pl.pallas_call(functools.partial(front_kernel, count), grid=(17,), in_spe...]
    reduce_scatter x4, waiting for transfers between devices: 287 us -> 269 us  [on_device(): lax.psum_scatter(a, 'fsdp', scatter_dimension=dim, tiled=True)]
    all_gather x1, waiting for transfers between devices: 12.7 us -> 21.3 us  [on_device(): heads = lax.all_gather(head, 'seq')]
  transfers between devices with their start and end apart: 10 -> 6, of which waited for: 9 -> 5; matrix products, arithmetic and copies ran while one was open for 3% -> 1% of each run, Pallas kernels for 11% -> 9%
where the time goes in v2:
time: 596 us; the launch traced here: 595 us
  waiting for transfers between devices  295 us (49%)
  Pallas kernels  225 us (38%)
  blocking collectives  41.2 us (7%)
  between operations  16.5 us (3%)
  local copies, waits for them, and re-layouts  12.5 us (2%)
    reduce_scatter x4, waiting for transfers between devices, on_device(): lax.psum_scatter(a, 'fsdp', scatter_dimension=dim, tiled=True)  269 us
    pallas_call x1, Pallas kernels, front(): pl.pallas_call(functools.partial(front_kernel, count), grid=(17,), in_spe...  95.5 us
    pallas_call x1, Pallas kernels, on_device(): pl.pallas_call(forward_kernel, grid=(steps,), in_specs=[rows_of(D)] * 3 +...  53.8 us
    psum x1, blocking collectives, on_device(): vector = lax.psum(vector, ('fsdp', 'seq'))  41.2 us
    pallas_call x1, Pallas kernels, on_device(): pl.pallas_call(column_kernel, grid=(steps,), in_specs=[rows_of(D, back),...  37.8 us
    pallas_call x1, Pallas kernels, on_device(): pl.pallas_call(row_kernel, grid=(steps,), in_specs=[rows_of(4 * D)] + [ro...  25.1 us
    all_gather x1, waiting for transfers between devices, on_device(): heads = lax.all_gather(head, 'seq')  21.3 us
    pallas_call x1, Pallas kernels, on_device(): pl.pallas_call(input_kernel, grid=(steps,), in_specs=[rows_of(D), rows_of...  13.3 us
  transfers between devices with their start and end apart: 6, of which 5 were waited for; matrix products, arithmetic and copies ran while one was open for 1% of the time, Pallas kernels for 9%

profile of v2, /device:TPU:0, one launch (start us, length us, event | category | flops | bytes accessed | tf_op | source)
XLA Modules:
  0.0 594.9 jit_solution(7160145731431196136)
XLA Ops:
  8.0 0.0 all-gather.3.cloned.1.call-start
  8.1 0.5 broadcast.13
  8.6 1.4 reduce.3
  9.9 0.1 fusion.4
  10.0 0.1 copy.35
  10.1 0.1 copy.36
  10.2 0.1 pad_add_fusion
  10.3 95.5 %front.1 = (bf16[2048,2048]{1,0:T(8,128)(2,1)}, bf16[2048,512]{1,0:T(8,128)(2,1)}, f32[2048,512]{1,0:T(8,128)}, f32[2048,512]{1,0:T(8,128)}, f32[2048,512]{1,0:T...) custom-call(bf16[2048,512]{1,0:T(8,128)(2,1)} %x_ref.7, ...), custom_call_target="tpu_custom_call" | custom-call | tf_op jit(solution)/shard_map/front/pallas_call | solution.py:544
  105.7 0.0 copy-start.1
  105.7 53.8 %feed.1 = (bf16[2048,512]{1,0:T(8,128)(2,1)}, f32[2048,512]{1,0:T(8,128)}, bf16[2048,512]{1,0:T(8,128)(2,1)}, f32[512,512]{1,0:T(8,128)}, f32[512,2048]{1,0:T(8,...) custom-call(bf16[2048,512]{1,0:T(8,128)(2,1)} %x_ref.7, ...), custom_call_target="tpu_custom_call" | custom-call | tf_op jit(solution)/shard_map/feed/pallas_call | solution.py:839
  159.5 0.7 broadcast_in_dim.30.edge_ref
  160.2 0.0 copy-done.1
  160.2 1.3 broadcast_in_dim.29.col_ref
  161.5 25.1 %rowside.1 = (bf16[2048,512]{1,0:T(8,128)(2,1)}, bf16[2048,512]{1,0:T(8,128)(2,1)}, f32[2048,512]{1,0:T(8,128)}, f32[2048,512]{1,0:T(8,128)}, f32[136,512]{1,0:T(8,128)}) custom-call(bf16[2048,2048]{1,0:T(8,128)(2,1)} %get-tuple-element.51.qkvf_ref, bf16[2048,512]{1,0:T(8,128)(2,1)} %get-tuple-element.52.do_ref, f32[2048,512]{1,0:T(8,128)} %get-tuple-element.53.p_ref, ...), custom_call_target="tpu_custom_call" | custom-call | tf_op jit(solution)/shard_map/rowside/pallas_call | solution.py:861
  186.6 0.0 all-gather.3.cloned.1.call-update
  186.7 0.0 reduce-scatter.7.cloned.1.call-start
  186.7 0.5 reduce-scatter.7.cloned.1.call-update
  187.2 0.0 reduce-scatter.11.cloned.1.call-start
  187.3 0.5 reduce-scatter.11.cloned.1.call-update
  187.8 0.0 reduce-scatter.9.cloned.1.call-start
  187.9 0.5 reduce-scatter.9.cloned.1.call-update
  188.4 0.0 reduce-scatter.5.cloned.1.call-start
  188.5 0.6 slice.59
  189.7 21.3 %all-gather.3.cloned.1.call-done = f32[544,512]{1,0:T(8,128)} async-done(((f32[136,512]{1,0:T(8,128)}), f32[544,512]{1,0:T(8,128)}) %all-gather.3.cloned.1.call-update) | async-done | bytes 1114128 | tf_op jit(solution)/shard_map/all_gather | solution.py:878
  211.0 0.7 slice.58
  211.7 0.1 copy.37
  211.8 2.2 select_reduce_fusion.start_ref
  213.9 37.8 %colside.1 = (bf16[2048,2048]{1,0:T(8,128)(2,1)}, f32[512,2048]{1,0:T(8,128)}) custom-call(bf16[2048,512]{1,0:T(8,128)(2,1)} %x_ref.7, bf16[2048,2048]{1,0:T(8,128)(2,1)} %get-tuple-element.51.qkvf_ref, bf16[2048,512]{1,0:T(8,128)(2,1)} %get-tuple-element.52.do_ref, bf16[2048,512]{1,0:T(8,128)(2,1)} %get-tuple-element.57.dq_ref, ...), custom_call_target="tpu_custom_call" | custom-call | tf_op jit(solution)/shard_map/colside/pallas_call | solution.py:883
  251.7 0.0 reduce-scatter.5.cloned.1.call-update
  251.8 0.0 all-reduce.3.cloned.1.call-start
  251.8 0.8 fusion.2
  252.7 13.3 %inputside.1 = (f32[2048,512]{1,0:T(8,128)}, f32[8,512]{1,0:T(8,128)}) custom-call(bf16[2048,512]{1,0:T(8,128)(2,1)} %x_ref.7, bf16[2048,2048]{1,0:T(8,128)(2,1)} %get-tuple-element.62.d_ref, f32[2048,512]{1,0:T(8,128)} %get-tuple-element.63.dy_ref, bf16[512,2048]{1,0:T(8,128)(2,1)} %bitcast.24, f32[8,512]{1,0:T(8,128)} %get-tuple-element.45.small_ref), custom_call_target="tpu_custom_call" | custom-call | tf_op jit(solution)/shard_map/inputside/pallas_call | solution.py:899
  265.9 86.5 %reduce-scatter.11.cloned.1.call-done = f32[512,256]{1,0:T(8,128)} async-done(((f32[512,2048]{1,0:T(8,128)}), f32[512,256]{1,0:T(8,128)}) %reduce-scatter.11.cloned.1.call-update) | async-done | bytes 524304 | tf_op jit(solution)/shard_map/reduce_scatter | solution.py:910
  352.4 91.0 %reduce-scatter.9.cloned.1.call-done = f32[64,2048]{1,0:T(8,128)} async-done(((f32[512,2048]{1,0:T(8,128)}), f32[64,2048]{1,0:T(8,128)}) %reduce-scatter.9.cloned.1.call-update) | async-done | bytes 524304 | tf_op jit(solution)/shard_map/reduce_scatter | solution.py:910
  443.5 91.8 %reduce-scatter.5.cloned.1.call-done = f32[64,2048]{1,0:T(8,128)} async-done(((f32[512,2048]{1,0:T(8,128)}), f32[64,2048]{1,0:T(8,128)}) %reduce-scatter.5.cloned.1.call-update) | async-done | bytes 524304 | tf_op jit(solution)/shard_map/reduce_scatter | solution.py:910
  535.3 0.0 all-reduce.3.cloned.1.call-update
  535.3 0.8 fusion.3
  536.1 0.0 copy-done.3
  536.2 41.2 %psum.39 = f32[4608]{0:T(1024)S(1)} all-reduce(f32[4608]{0:T(1024)S(1)} %constant_dynamic-update-slice_fusion), channel_id=1, replica_groups=mesh['seq'=4,'fsdp'=8] {'fsdp','seq'}, use_global_device_ids=true, to_apply=%region_9.10 | all-reduce | flops 4608 | bytes 36864 | tf_op jit(solution)/shard_map/psum | solution.py:917
  577.3 0.6 dynamic_slice.22
  578.0 0.6 fusion.1
  578.6 3.2 all-reduce.3.cloned.1.call-done
  581.8 2.0 fusion
  583.8 2.0 copy.34
  585.8 0.0 copy-done.2
  585.8 0.7 copy.48
  586.5 0.0 copy-done
  586.5 0.8 copy.49
  (13 shorter events, 0.1 us)
Async XLA Ops:
  8.0 202.9 %all-gather.3.cloned.1.call-start = ((), (), s32[]{:S(2)}) async-start(), calls=%async_computation.8 | async-start | bytes 1392640 | tf_op jit(solution)/shard_map/all_gather | solution.py:878
  105.7 54.5 %copy-start.1 = (s32[1,2048]{1,0:T(1,128)S(1)}, s32[1,2048]{1,0:T(1,128)}, u32[]{:S(2)}) copy-start(s32[1,2048]{1,0:T(1,128)} %row_ref.3) | copy-start | bytes 24580
  186.7 79.3 %reduce-scatter.7.cloned.1.call-start = ((), (), s32[]{:S(2)}) async-start(), calls=%async_computation.5 | async-start | bytes 1179648 | tf_op jit(solution)/shard_map/reduce_scatter | solution.py:910
  187.2 165.2 %reduce-scatter.11.cloned.1.call-start = ((), (), s32[]{:S(2)}) async-start(), calls=%async_computation.7 | async-start | bytes 4718592 | tf_op jit(solution)/shard_map/reduce_scatter | solution.py:910
  187.8 255.6 %reduce-scatter.9.cloned.1.call-start = ((), (), s32[]{:S(2)}) async-start(), calls=%async_computation.6 | async-start | bytes 4718592 | tf_op jit(solution)/shard_map/reduce_scatter | solution.py:910
  188.4 346.9 %reduce-scatter.5.cloned.1.call-start = ((), (), s32[]{:S(2)}) async-start(), calls=%async_computation.4 | async-start | bytes 4718592 | tf_op jit(solution)/shard_map/reduce_scatter | solution.py:910
  251.8 330.1 %all-reduce.3.cloned.1.call-start = ((), (), s32[]{:S(2)}) async-start(), calls=%async_computation.9 | async-start | bytes 3407872 | tf_op jit(solution)/shard_map/psum | solution.py:909
  252.7 283.5 %copy-start.3 = (f32[1,2048]{1,0:T(1,128)S(1)}, f32[1,2048]{1,0:T(1,128)}, u32[]{:S(2)}) copy-start(f32[1,2048]{1,0:T(1,128)} %get-tuple-element.72) | copy-start | bytes 24580
  581.8 4.0 copy-start.2
  581.8 4.7 copy-start
Sparse Core Ops, SparseCore 0:
  186.8 24.1 all-gather.2
  535.4 46.3 all-reduce.2
Sparse Core Ops, SparseCore 1:
  190.5 70.5 reduce-scatter.6
  265.0 87.4 reduce-scatter.10
  355.9 87.5 reduce-scatter.8
  447.6 87.7 reduce-scatter.4

commit v3 on v2

--- a/solution.py
+++ b/solution.py
@@ -17,7 +17,8 @@
 SCALE = 0.125
 F32 = jnp.float32
 BF16 = jnp.bfloat16
-LIMIT = 60 * 1024 * 1024
+FEED_ROWS = 512
+LIMIT = 62 * 1024 * 1024
 
 
 def dot(a, b):
@@ -608,13 +609,13 @@
 
 def forward_kernel(
     x_ref, o_ref, g_ref, small_ref, bias_ref, wo_ref, wh_ref, wr_ref,
-    y_ref, dy_ref, do_ref, gwo_ref, gwh_ref, gwr_ref, gsmall_ref, gbias_ref, dz_buf,
+    y_ref, dy_ref, do_ref, pack_ref, gsmall_ref, gwo_ref, gwh_ref, gwr_ref,
 ):
     step = pl.program_id(0)
 
     @pl.when(step == 0)
     def _():
-        for ref in (gwo_ref, gwh_ref, gwr_ref, gsmall_ref, gbias_ref):
+        for ref in (gwo_ref, gwh_ref, gwr_ref, gsmall_ref):
             ref[...] = jnp.zeros_like(ref)
 
     attended, cot = o_ref[...], g_ref[...]
@@ -633,7 +634,7 @@
         gwr_ref[:, cols] += dot_tn(cot, active)
         grad = dot_nt(cot, wr_ref[cols, :]) * slope
         low = grad.astype(BF16)
-        gbias_ref[0:1, cols] += jnp.sum(low.astype(F32), axis=0, keepdims=True)
+        gsmall_ref[8 + j : 9 + j] += jnp.sum(low.astype(F32), axis=0, keepdims=True)
         gwh_ref[:, cols] += dot_tn(hidden, low)
         grad_hidden = grad_hidden + dot_nt(low, wh_ref[:, cols])
     y_ref[...] = out.astype(BF16)
@@ -646,26 +647,32 @@
     gwo_ref[...] += dot_tn(attended, branch)
     do_ref[...] = dot_nt(branch, wo_ref[...]).astype(BF16)
 
-
-def row_kernel(
-    qkvf_ref, do_ref, p_ref, s_ref, z_ref, kept_ref, col_ref, row_ref, edge_ref,
+    @pl.when(step == pl.num_programs(0) - 1)
+    def _():
+        _, count, part, _ = pack_ref.shape
+        for q in range(4):
+            hidden_part = gwh_ref[:, q * 512 : (q + 1) * 512].reshape(count, part, 512)
+            pack_ref[q, :, :, 0:512] = hidden_part.astype(pack_ref.dtype)
+            out_part = gwo_ref[:, q * 128 : (q + 1) * 128].reshape(count, part, 128)
+            pack_ref[q, :, :, 512:640] = out_part.astype(pack_ref.dtype)
+            turned = gwr_ref[q * 128 : (q + 1) * 128].T.reshape(count, 4, part, 128)
+            for j in range(4):
+                pack_ref[q, :, :, 640 + j * 128 : 768 + j * 128] = turned[:, j].astype(
+                    pack_ref.dtype
+                )
+
+
+def row_body(
+    n, qkvf_ref, do_ref, p_ref, s_ref, z_ref, kept_ref, col, row, edge_ref,
     dq_ref, r_ref, dn_ref, dz_ref, head_ref,
 ):
-    step = pl.program_id(0)
     first = edge_ref[pl.ds(0, 1)]
-    before = edge_ref[pl.ds(8 + jnp.maximum(step - 1, 0), 1)]
-    last = jnp.where(step == 0, first, before)
-    col = col_ref[...]
-    vis = visible(col, row_ref[...])
+    before = edge_ref[pl.ds(8 + jnp.maximum(n - 1, 0), 1)]
+    last = jnp.where(n == 0, first, before)
+    vis = visible(col, row)
     carried = wide(flag(col, last), 2)
     slots = jnp.exp(qkvf_ref[:, 3 * D :].astype(F32)).astype(BF16)
     own = wide(flag(col, first), 4)
-
-    @pl.when(step == 0)
-    def _():
-        head_ref[...] = jnp.zeros_like(head_ref)
-        head_ref[129:130] = first.astype(F32)
-
     for g in range(2):
         lanes = slice(g * GROUP, (g + 1) * GROUP)
         queries, keys, values = (
@@ -702,95 +709,523 @@
         head_ref[128:129, lanes] += jnp.sum(mine * back_total, axis=0, keepdims=True)
 
 
-def column_kernel(
-    x_ref, qkvf_ref, do_ref, dq_ref, r_ref, dn_ref, dz_ref, col_ref, row_ref, edge_ref, small_ref,
-    start_ref, d_ref, gw_ref, state,
+def column_body(
+    n, g, qkvf_ref, do_ref, r_ref, dn_ref, dz_ref, col, row, edge_ref, state, d_ref
+):
+    newest = edge_ref[15:16]
+    after = edge_ref[pl.ds(jnp.minimum(n + 1, 7), 1)]
+    following = jnp.where(n == 7, newest, after)
+    first = edge_ref[pl.ds(n, 1)]
+    vis = visible_back(col, row)
+    carried = wide(flag(col, following), 2)
+    own = wide(flag(col, first), 2)
+    kept = jnp.where(following == first, 1.0, 0.0)[:, :GROUP]
+    left = lane_heads(C, 128) == 0
+
+    def lanes_of(part):
+        return pl.ds(pl.multiple_of(part * D + g * GROUP, GROUP), GROUP)
+
+    lanes = lanes_of(0)
+    queries, keys, values = (qkvf_ref[:, lanes_of(part)] for part in range(3))
+    written = jnp.exp(qkvf_ref[:, lanes_of(3)].astype(F32))
+    here = written.astype(BF16)
+    back_total = dz_ref[:, lanes]
+    total_high, total_low = split(back_total)
+    back_norm = dot(vis, total_high) + dot(vis, total_low)
+    grads, reading, back_numer = do_ref[:, lanes], r_ref[:, lanes], dn_ref[:, lanes]
+    numer_high, numer_low = split(back_numer)
+    key_state = expand(state[0:64, lanes]).astype(BF16)
+    value_state = expand(state[64:128, lanes]).astype(BF16)
+    apart = stacked(here)
+    mix = masked(dot_nt(apart, reading), vis)
+    back_values = select(dot(mix, grads)) + carried * dot(here, value_state)
+    d_ref[:, lanes_of(2)] = back_values.astype(BF16)
+    back_affinity = masked(dot_nt(apart, numer_high), vis)
+    back_keys = select(dot(back_affinity, queries)) + carried * dot(here, key_state)
+    d_ref[:, lanes_of(1)] = back_keys.astype(BF16)
+    back_mix = masked(dot_nt(stacked(values), grads), vis)
+    back_slots = back_norm + select(dot(back_mix, reading))
+    affinity = masked(dot_nt(stacked(keys), queries), vis)
+    parts = []
+    for p in range(2):
+        pair = slice(p * 128, (p + 1) * 128)
+        both = dot(
+            affinity[p * 512 : (p + 1) * 512],
+            jnp.concatenate([numer_high[:, pair], numer_low[:, pair]], axis=1),
+        )
+        both = both[:, :128] + both[:, 128:]
+        parts.append(jnp.where(left, both[:C], both[C:]))
+    back_slots = back_slots + jnp.concatenate(parts, axis=1)
+    back_slots = back_slots + carried * (
+        dot_nt(keys, key_state) + dot_nt(values, value_state) + state[128:129, lanes]
+    )
+    d_ref[:, lanes_of(3)] = (back_slots * written).astype(BF16)
+    state[0:64, lanes] = kept * state[0:64, lanes] + compacted(
+        dot_tn((own * back_numer).astype(BF16), queries)
+    )
+    state[64:128, lanes] = kept * state[64:128, lanes] + compacted(
+        dot_tn((own * reading.astype(F32)).astype(BF16), grads)
+    )
+    state[128:129, lanes] = kept * state[128:129, lanes] + jnp.sum(
+        own * back_total, axis=0, keepdims=True
+    )
+
+
+class Scatter:
+    def __init__(self, count, source, own, from_core, to_chip, from_chip, from_row, total, out, sems):
+        self.count, self.source, self.own, self.out = count, source, own, out
+        self.from_core, self.to_chip, self.from_chip = from_core, to_chip, from_chip
+        self.to_row, self.from_row, self.total = to_chip, from_row, total
+        (self.core, self.local, self.chip, self.row, self.last, self.done) = sems
+        self.seq, self.at, self.sibling, self.beside = places()
+        self.c = lax.rem(self.seq, 2)
+        self.x = self.seq // 2
+
+    def copy_core(self, n):
+        return push(
+            self.source.at[2 * n + 1 - self.c], self.from_core.at[n],
+            self.core.at[0, n], self.core.at[1, n], seq=self.sibling,
+        )
+
+    def copy_own(self, n):
+        return pltpu.make_async_copy(self.source.at[2 * n + self.c], self.own, self.local)
+
+    def copy_chip(self):
+        return push(
+            self.to_chip, self.from_chip, self.chip.at[0], self.chip.at[1], seq=self.beside
+        )
+
+    def copy_row(self, k):
+        return push(
+            self.to_row.at[self.at ^ k], self.from_row.at[self.at],
+            self.row.at[0, k], self.row.at[1, k], fsdp=self.at ^ k,
+        )
+
+    def row_in(self, k):
+        here = self.from_row.at[self.at ^ k]
+        return push(here, here, self.row.at[0, k], self.row.at[1, k], fsdp=self.at ^ k)
+
+    def copy_done(self):
+        return pltpu.make_async_copy(self.total, self.out.at[self.seq], self.done)
+
+    def sent(self, n):
+        if n == 2:
+            here = self.out.at[self.beside]
+            return push(here, here, self.last.at[0, 2], self.last.at[1, 2], seq=self.sibling)
+        target = (self.sibling, self.beside)[n]
+        return push(
+            self.total, self.out.at[self.seq], self.last.at[0, n], self.last.at[1, n], seq=target
+        )
+
+    def come(self, n):
+        if n == 2:
+            here = self.out.at[lax.rem(self.sibling + 2, 4)]
+            return push(here, here, self.last.at[0, 2], self.last.at[1, 2], seq=self.sibling)
+        source = (self.sibling, self.beside)[n]
+        here = self.out.at[source]
+        return push(here, here, self.last.at[0, n], self.last.at[1, n], seq=source)
+
+    def mine(self, n, f):
+        if self.own is None:
+            return self.source[2 * n + self.c, f].astype(F32)
+        return self.own[f].astype(F32)
+
+    def start(self):
+        for n in range(2):
+            self.copy_core(n).start()
+        if self.own is not None:
+            self.copy_own(1 - self.x).start()
+
+    def second(self):
+        for n in range(2):
+            self.copy_core(n).wait_recv()
+        n = 1 - self.x
+        if self.own is not None:
+            self.copy_own(n).wait()
+
+        @pl.loop(0, self.count)
+        def _(f):
+            both = self.mine(n, f) + self.from_core[n, f].astype(F32)
+            self.to_chip[f] = both.astype(self.to_chip.dtype)
+
+        self.copy_chip().start()
+        if self.own is not None:
+            self.copy_own(self.x).start()
+
+    def third(self):
+        self.copy_chip().wait_recv()
+        self.copy_chip().wait_send()
+        n = self.x
+        if self.own is not None:
+            self.copy_own(n).wait()
+
+        @pl.loop(0, self.count)
+        def _(f):
+            three = self.mine(n, f) + self.from_core[n, f].astype(F32) + self.from_chip[f].astype(F32)
+            self.to_row[f] = three.astype(self.to_row.dtype)
+
+        for k in range(1, self.count):
+            self.copy_row(k).start()
+        self.total[...] = (
+            self.mine(n, self.at)
+            + self.from_core[n, self.at].astype(F32)
+            + self.from_chip[self.at].astype(F32)
+        )
+
+    def fourth(self):
+        for k in range(1, self.count):
+            self.row_in(k).wait_recv()
+        total = self.total[...]
+        for k in range(1, self.count):
+            total = total + self.from_row[self.at ^ k].astype(F32)
+        self.total[...] = total
+        self.copy_done().start()
+        self.sent(0).start()
+        self.sent(1).start()
+
+    def fifth(self):
+        self.come(1).wait_recv()
+        self.sent(2).start()
+
+    def finish(self):
+        self.come(0).wait_recv()
+        self.come(2).wait_recv()
+        self.copy_done().wait()
+        for n in range(3):
+            self.sent(n).wait_send()
+        for n in range(2):
+            self.copy_core(n).wait_send()
+        for k in range(1, self.count):
+            self.copy_row(k).wait_send()
+
+
+def scatter_scratch(count, part, lanes, link, hbm):
+    vmem, dma = pltpu.VMEM, pltpu.SemaphoreType.DMA
+    block = (count, part, lanes)
+    own = [vmem(block, link)] if hbm else []
+    return (
+        own
+        + [vmem((2, *block), link)]
+        + [vmem(block, link)] * 3
+        + [vmem((part, lanes), F32)]
+        + [dma((2, 2)), dma, dma((2,)), dma((2, count)), dma((2, 3)), dma]
+    )
+
+
+class SmallSum:
+    def __init__(self, count, mine, from_seq, half, from_fsdp, sems):
+        self.count, self.mine, self.from_seq = count, mine, from_seq
+        self.half, self.from_fsdp, self.sems = half, from_fsdp, sems
+        self.seq, self.at, _, _ = places()
+
+    def over_seq(self, k, slot):
+        return push(
+            self.mine, self.from_seq.at[slot], self.sems[0].at[0, k], self.sems[0].at[1, k],
+            seq=self.seq ^ k,
+        )
+
+    def over_fsdp(self, k, slot):
+        return push(
+            self.half, self.from_fsdp.at[slot], self.sems[1].at[0, k], self.sems[1].at[1, k],
+            fsdp=self.at ^ k,
+        )
+
+    def start(self):
+        for k in range(1, 4):
+            self.over_seq(k, self.seq).start()
+        self.from_seq[self.seq] = self.mine[...]
+
+    def second(self):
+        for k in range(1, 4):
+            self.over_seq(k, self.seq ^ k).wait_recv()
+        total = self.from_seq[0]
+        for n in range(1, 4):
+            total = total + self.from_seq[n]
+        self.half[...] = total
+        for k in range(1, self.count):
+            self.over_fsdp(k, self.at).start()
+        self.from_fsdp[self.at] = total
+
+    def finish(self, out_ref):
+        for k in range(1, self.count):
+            self.over_fsdp(k, self.at ^ k).wait_recv()
+        total = self.from_fsdp[0]
+        for n in range(1, self.count):
+            total = total + self.from_fsdp[n]
+        out_ref[...] = total
+        for k in range(1, 4):
+            self.over_seq(k, self.seq).wait_send()
+        for k in range(1, self.count):
+            self.over_fsdp(k, self.at).wait_send()
+
+
+def small_scratch(count, rows):
+    vmem, dma = pltpu.VMEM, pltpu.SemaphoreType.DMA
+    return [
+        vmem((4, rows, D), F32), vmem((rows, D), F32), vmem((count, rows, D), F32),
+        dma((2, 4)), dma((2, count)),
+    ]
+
+
+ROW_STEPS, COLUMN_STEPS = 8, 16
+FIRST_COLUMN = ROW_STEPS + 1
+FIRST_INPUT = FIRST_COLUMN + COLUMN_STEPS
+
+
+def back_kernel(
+    count, last_step, x_ref, xs_ref, qkvf_ref, do_ref, p_ref, s_ref, z_ref, kept_ref, dy_ref, doc_ref,
+    small_ref, w_ref, ffg_ref, ffs_ref,
+    gi_ref, ff_out, g0_out, g1_out, s1_out, s2_out,
+    d_all, h_turned, reading, numer, total, col_ref, edge_ref, head, state, heads, head_rows,
+    piece0, piece1, last_small, *rest,
 ):
     step = pl.program_id(0)
-    here_at = 7 - step
+    seq, at, _, _ = places()
+    link = piece0.dtype
+    ff = Scatter(count, ffg_ref, *rest[:6], ff_out, rest[6:12])
+    rest = rest[12:]
+    first_piece = Scatter(count, piece0, None, *rest[:5], g0_out, rest[5:11])
+    rest = rest[11:]
+    second_piece = Scatter(count, piece1, None, *rest[:5], g1_out, rest[5:11])
+    rest = rest[11:]
+    small_one = SmallSum(count, ffs_ref, *rest[:3], rest[3:5])
+    small_two = SmallSum(count, last_small, *rest[5:8], rest[8:10])
+    states = States(heads, head_rows, (rest[10], rest[11]))
 
     @pl.when(step == 0)
     def _():
-        state[...] = start_ref[...]
-        gw_ref[...] = jnp.zeros_like(gw_ref)
-
-    newest = edge_ref[15:16]
-    after = edge_ref[pl.ds(jnp.minimum(here_at + 1, 7), 1)]
-    following = jnp.where(step == 0, newest, after)
-    first = edge_ref[pl.ds(here_at, 1)]
-    col = col_ref[...]
-    vis = visible_back(col, row_ref[...])
-    carried = wide(flag(col, following), 2)
-    own = wide(flag(col, first), 2)
-    same = jnp.where(following == first, 1.0, 0.0)
-    written = jnp.exp(qkvf_ref[:, 3 * D :].astype(F32))
-    slots = written.astype(BF16)
-    total_high, total_low = split(dz_ref[...])
-    back_norm = dot(vis, total_high) + dot(vis, total_low)
-    d_ref[:, 0:D] = dq_ref[...]
-    left = lane_heads(C, 128) == 0
-    for g in range(2):
-        lanes = slice(g * GROUP, (g + 1) * GROUP)
-        queries, keys, values = (
-            qkvf_ref[:, part * D + g * GROUP : part * D + (g + 1) * GROUP] for part in range(3)
-        )
-        here, grads, reading = slots[:, lanes], do_ref[:, lanes], r_ref[:, lanes]
-        numer_high, numer_low = split(dn_ref[:, lanes])
-        key_state = expand(state[0:64, lanes]).astype(BF16)
-        value_state = expand(state[64:128, lanes]).astype(BF16)
-        apart = stacked(here)
-        mix = masked(dot_nt(apart, reading), vis)
-        back_values = select(dot(mix, grads)) + carried * dot(here, value_state)
-        d_ref[:, 2 * D + g * GROUP : 2 * D + (g + 1) * GROUP] = back_values.astype(BF16)
-        back_affinity = masked(dot_nt(apart, numer_high), vis)
-        back_keys = select(dot(back_affinity, queries)) + carried * dot(here, key_state)
-        d_ref[:, D + g * GROUP : D + (g + 1) * GROUP] = back_keys.astype(BF16)
-        back_mix = masked(dot_nt(stacked(values), grads), vis)
-        back_slots = back_norm[:, lanes] + select(dot(back_mix, reading))
-        affinity = masked(dot_nt(stacked(keys), queries), vis)
-        parts = []
-        for p in range(2):
-            pair = slice(p * 128, (p + 1) * 128)
-            both = dot(
-                affinity[p * 512 : (p + 1) * 512],
-                jnp.concatenate([numer_high[:, pair], numer_low[:, pair]], axis=1),
-            )
-            both = both[:, :128] + both[:, 128:]
-            parts.append(jnp.where(left, both[:C], both[C:]))
-        back_slots = back_slots + jnp.concatenate(parts, axis=1)
-        back_slots = back_slots + carried * (
-            dot_nt(keys, key_state) + dot_nt(values, value_state) + state[128:129, lanes]
-        )
-        d_ref[:, 3 * D + g * GROUP : 3 * D + (g + 1) * GROUP] = (
-            back_slots * written[:, lanes]
-        ).astype(BF16)
-        kept = same[:, lanes]
-        state[0:64, lanes] = kept * state[0:64, lanes] + compacted(
-            dot_tn((own * dn_ref[:, lanes]).astype(BF16), queries)
-        )
-        state[64:128, lanes] = kept * state[64:128, lanes] + compacted(
-            dot_tn((own * reading.astype(F32)).astype(BF16), grads)
-        )
-        state[128:129, lanes] = kept * state[128:129, lanes] + jnp.sum(
-            own * dz_ref[:, lanes], axis=0, keepdims=True
-        )
-    unit, _ = norm_parts(x_ref[...].astype(F32))
-    hidden = (unit * small_ref[0:1] + small_ref[1:2]).astype(BF16)
-    gw_ref[...] += dot_tn(hidden, d_ref[...])
-
-
-def input_kernel(x_ref, d_ref, dy_ref, w_ref, small_ref, gi_ref, gsmall_ref):
-    step = pl.program_id(0)
-
-    @pl.when(step == 0)
-    def _():
-        gsmall_ref[...] = jnp.zeros_like(gsmall_ref)
-
-    grad = dot_nt(d_ref[...], w_ref[...])
-    unit, scale = norm_parts(x_ref[...].astype(F32))
-    gsmall_ref[0:1] += jnp.sum(grad * unit, axis=0, keepdims=True)
-    gsmall_ref[1:2] += jnp.sum(grad, axis=0, keepdims=True)
-    gi_ref[...] = dy_ref[...] + norm_back(unit, scale, small_ref[0:1], grad)
+        greet(count)
+        ff.start()
+        small_one.start()
+        doc_parts(doc_ref, col_ref, edge_ref)
+        head[...] = jnp.zeros_like(head)
+        last_small[...] = jnp.zeros_like(last_small)
+
+    @pl.when(step < ROW_STEPS)
+    def _():
+        n = step
+        here = pl.ds(pl.multiple_of(n * C, C), C)
+        unit, _ = norm_parts(x_ref[...].astype(F32))
+        h_turned[:, here] = (unit * small_ref[0:1] + small_ref[1:2]).astype(BF16).T
+        row_body(
+            n, qkvf_ref, do_ref, p_ref, s_ref, z_ref, kept_ref, col_ref[here],
+            doc_ref[:, here].astype(F32), edge_ref,
+            d_all.at[here, 0:D], reading.at[here], numer.at[here], total.at[here], head,
+        )
+
+    @pl.when(step == 2)
+    def _():
+        ff.second()
+        small_one.second()
+
+    @pl.when(step == 5)
+    def _():
+        small_one.finish(s1_out)
+
+    @pl.when(step == ROW_STEPS - 1)
+    def _():
+        heads[seq] = head[0:128].astype(link)
+        head_rows[seq, 0:1] = head[128:129]
+        head_rows[seq, 1:2] = edge_ref[0:1]
+        head_rows[seq, 2:8] = jnp.zeros((6, D), F32)
+        states.start()
+
+    def weight_grad(piece, n, lanes):
+        grad = dot(h_turned[...], d_all[:, lanes])
+        piece[n] = grad.reshape(count, D // count, GROUP).astype(link)
+
+    @pl.when(step == ROW_STEPS)
+    def _():
+        weight_grad(piece0, 0, slice(0, GROUP))
+        weight_grad(piece1, 0, slice(GROUP, D))
+        states.finish()
+        newest = edge_ref[15:16]
+        state[...] = jnp.zeros_like(state)
+        for n in range(4):
+            use = jnp.where(head_rows[n, 1:2] == newest, 1.0, 0.0) * (n > seq).astype(F32)
+            state[0:128] += use * heads[n].astype(F32)
+            state[128:129] += use * head_rows[n, 0:1]
+
+    @pl.when((step >= FIRST_COLUMN) & (step < FIRST_INPUT))
+    def _():
+        n = 7 - lax.rem(step - FIRST_COLUMN, 8)
+        g = (step - FIRST_COLUMN) // 8
+        here = pl.ds(pl.multiple_of(n * C, C), C)
+        column_body(
+            n, g, qkvf_ref, do_ref, reading.at[here], numer.at[here], total.at[here], col_ref[here],
+            doc_ref[:, here].astype(F32), edge_ref, state, d_all.at[here],
+        )
+
+    @pl.when(step == FIRST_COLUMN + 2)
+    def _():
+        ff.third()
+
+    @pl.when(step == FIRST_COLUMN + 7)
+    def _():
+        for w in range(1, 4):
+            weight_grad(piece0, w, slice(w * D, w * D + GROUP))
+        first_piece.start()
+
+    @pl.when(step == FIRST_COLUMN + 9)
+    def _():
+        first_piece.second()
+
+    @pl.when(step == FIRST_COLUMN + 12)
+    def _():
+        first_piece.third()
+
+    @pl.when(step == FIRST_COLUMN + 15)
+    def _():
+        for w in range(1, 4):
+            weight_grad(piece1, w, slice(w * D + GROUP, (w + 1) * D))
+        second_piece.start()
+        first_piece.fourth()
+        ff.fourth()
+
+    @pl.when(step >= FIRST_INPUT)
+    def _():
+        n = step - FIRST_INPUT
+        size = xs_ref.shape[0]
+        here = pl.ds(pl.multiple_of(n * size, size), size)
+        grad = dot_nt(d_all[here], w_ref[...])
+        unit, scale = norm_parts(xs_ref[...].astype(F32))
+        last_small[0:1] += jnp.sum(grad * unit, axis=0, keepdims=True)
+        last_small[1:2] += jnp.sum(grad, axis=0, keepdims=True)
+        gi_ref[...] = dy_ref[...] + norm_back(unit, scale, small_ref[0:1], grad)
+
+    @pl.when(step == FIRST_INPUT)
+    def _():
+        second_piece.second()
+        first_piece.fifth()
+        ff.fifth()
+
+    @pl.when(step == last_step - 1)
+    def _():
+        second_piece.third()
+
+    @pl.when(step == last_step)
+    def _():
+        small_two.start()
+        ff.finish()
+        first_piece.finish()
+        small_two.second()
+        second_piece.fourth()
+        second_piece.fifth()
+        small_two.finish(s2_out)
+        second_piece.finish()
+        states.drain()
+
+
+def back(count, tokens, qkvf, do, probs, score, inverse, kept, dy, doc_ids, small, w_all, ffg, ffs):
+    rows = tokens.shape[0]
+    part, link = ffg.shape[2], ffg.dtype
+    size = 512 if link == BF16 else 256
+    last = FIRST_INPUT + rows // size - 1
+    once = lambda a: pl.BlockSpec(a.shape, lambda i: (0,) * a.ndim)
+    anywhere = pl.BlockSpec(memory_space=pl.ANY)
+    vmem, dma = pltpu.VMEM, pltpu.SemaphoreType.DMA
+
+    def early(i):
+        return jnp.minimum(i, ROW_STEPS - 1)
+
+    def both(i):
+        turned = 7 - lax.rem(jnp.clip(i - FIRST_COLUMN, 0, COLUMN_STEPS - 1), 8)
+        return jnp.where(i < ROW_STEPS, i, turned)
+
+    late = lambda i: (jnp.maximum(i - FIRST_INPUT, 0), 0)
+    tall = pl.BlockSpec((size, D), late)
+    return pl.pallas_call(
+        functools.partial(back_kernel, count, last),
+        grid=(last + 1,),
+        in_specs=[rows_of(D, early), tall, rows_of(4 * D, both), rows_of(D, both)]
+        + [rows_of(D, early)] * 3
+        + [pl.BlockSpec((1, 128, D), lambda i: (early(i), 0, 0)), tall]
+        + [once(doc_ids), once(small), once(w_all), anywhere, once(ffs)],
+        out_specs=[tall] + [anywhere] * 3 + [whole(16, D), whole(8, D)],
+        out_shape=[
+            shape_of((rows, D), F32),
+            shape_of((4, part, 1152), F32),
+            shape_of((4, part, GROUP), F32),
+            shape_of((4, part, GROUP), F32),
+            shape_of((16, D), F32),
+            shape_of((8, D), F32),
+        ],
+        scratch_shapes=[
+            vmem((rows, 4 * D), BF16),
+            vmem((D, rows), BF16),
+            vmem((rows, D), BF16),
+            vmem((rows, D), F32),
+            vmem((rows, D), F32),
+            vmem((rows, 128), F32),
+            vmem((16, D), F32),
+            vmem((136, D), F32),
+            vmem((136, D), F32),
+            vmem((4, 128, D), link),
+            vmem((4, 8, D), F32),
+            vmem((4, count, part, GROUP), link),
+            vmem((4, count, part, GROUP), link),
+            vmem((8, D), F32),
+        ]
+        + scatter_scratch(count, part, 1152, link, True)
+        + scatter_scratch(count, part, GROUP, link, False) * 2
+        + small_scratch(count, 16)
+        + small_scratch(count, 8)
+        + [dma((3, 2)), dma((3, 2))],
+        compiler_params=pltpu.CompilerParams(
+            vmem_limit_bytes=LIMIT, collective_id=2, has_side_effects=True
+        ),
+        name="back",
+    )(
+        tokens, tokens, qkvf, do, probs, score, inverse, kept, dy, doc_ids, small, w_all, ffg, ffs
+    )
+
+
+def finish_kernel(count, part, ff_ref, g0_ref, g1_ref, s1_ref, s2_ref, *outs):
+    at = lax.axis_index("fsdp")
+    for n in range(4):
+        outs[n][:, 0:GROUP] = g0_ref[n]
+        outs[n][:, GROUP:D] = g1_ref[n]
+        outs[4][:, n * 128 : (n + 1) * 128] = ff_ref[n, :, 512:640]
+        outs[5][:, n * 512 : (n + 1) * 512] = ff_ref[n, :, 0:512]
+        for j in range(4):
+            outs[6][j * part : (j + 1) * part, n * 128 : (n + 1) * 128] = ff_ref[
+                n, :, 640 + j * 128 : 768 + j * 128
+            ]
+
+    def pick(row, size):
+        out = row(0, size)
+        for f in range(1, count):
+            out = jnp.where(at == f, row(f * size, size), out)
+        return out
+
+    def bias(start, size):
+        r = start // D
+        return s1_ref[8 + r : 9 + r, start - r * D : start - r * D + size]
+
+    def row_of_sums(ref, n):
+        return lambda start, size: ref[n : n + 1, start : start + size]
+
+    outs[7][...] = pick(row_of_sums(s2_ref, 0), part)
+    outs[8][...] = pick(row_of_sums(s2_ref, 1), part)
+    outs[9][...] = pick(row_of_sums(s1_ref, 2), part)
+    outs[10][...] = pick(row_of_sums(s1_ref, 3), part)
+    outs[11][...] = pick(bias, 4 * part)
+    outs[12][...] = pick(row_of_sums(s1_ref, 4), part)
+
+
+def finish(count, part, ff, g0, g1, s1, s2):
+    once = lambda shape: pl.BlockSpec(shape, lambda: (0,) * len(shape))
+    shapes = [(part, D)] * 5 + [(part, FF), (4 * part, D)]
+    shapes += [(1, part)] * 4 + [(1, 4 * part), (1, part)]
+    args = (ff, g0, g1, s1, s2)
+    return pl.pallas_call(
+        functools.partial(finish_kernel, count, part),
+        in_specs=[once(a.shape) for a in args],
+        out_specs=[once(s) for s in shapes],
+        out_shape=[shape_of(s, F32) for s in shapes],
+        compiler_params=PARAMS,
+        name="finish",
+    )(*args)
 
 
 def rows_of(lanes, order=lambda i: i):
@@ -817,8 +1252,6 @@
     gain_first, shift_first, gain_second, shift_second, bias_hidden, bias_return, cotangent,
 ):
     rows = tokens.shape[0]
-    steps = rows // C
-    seq = lax.axis_index("seq")
     count = lax.axis_size("fsdp")
     part = gain_first.shape[0]
     flat = lambda a: a.reshape(1, a.shape[0])
@@ -828,112 +1261,39 @@
         [flat(a) for a in (gain_first, shift_first, gain_second, shift_second, bias_return)],
         flat(bias_hidden),
     )
+    link = w_qkvf.dtype
     w_qkvf, w_o, w_h, w_r = (
         a.reshape(-1, a.shape[2]).astype(BF16) for a in (w_qkvf, w_o, w_h, w_r)
     )
-    doc_col = jnp.broadcast_to(doc_ids.reshape(rows, 1), (rows, 128))
-    pieces = doc_ids.reshape(steps, C)
-    edges = jnp.concatenate([pieces[:, 0], pieces[:, -1]])
-    edges = jnp.broadcast_to(edges[:, None], (2 * steps, D))
-
-    out, grad_middle, grad_attended, g_wo, g_wh, g_wr, g_small, g_bias = pl.pallas_call(
+    tall = pl.BlockSpec((FEED_ROWS, D), lambda i: (i, 0))
+    out, grad_middle, grad_attended, pack, ff_small = pl.pallas_call(
         forward_kernel,
-        grid=(steps,),
-        in_specs=[rows_of(D)] * 3
+        grid=(rows // FEED_ROWS,),
+        in_specs=[tall] * 3
         + [whole(8, D), whole(1, FF), whole(D, D), whole(D, FF), whole(FF, D)],
-        out_specs=[rows_of(D)] * 3
-        + [whole(D, D), whole(D, FF), whole(D, FF), whole(8, D), whole(1, FF)],
+        out_specs=[tall] * 3 + [whole(4, count, part, 1152), whole(16, D)],
         out_shape=[
             shape_of((rows, D), BF16),
             shape_of((rows, D), F32),
             shape_of((rows, D), BF16),
-            shape_of((D, D), F32),
-            shape_of((D, FF), F32),
-            shape_of((D, FF), F32),
-            shape_of((8, D), F32),
-            shape_of((1, FF), F32),
+            shape_of((4, count, part, 1152), link),
+            shape_of((16, D), F32),
         ],
-        scratch_shapes=[pltpu.VMEM((C, FF), BF16)],
+        scratch_shapes=[
+            pltpu.VMEM((D, D), F32),
+            pltpu.VMEM((D, FF), F32),
+            pltpu.VMEM((D, FF), F32),
+        ],
         compiler_params=PARAMS,
         name="feed",
     )(tokens, attended, cotangent, small, bias, w_o, w_h, w_r)
 
-    grad_q, reading, grad_numer, grad_total, head = pl.pallas_call(
-        row_kernel,
-        grid=(steps,),
-        in_specs=[rows_of(4 * D)]
-        + [rows_of(D)] * 4
-        + [pl.BlockSpec((1, 128, D), lambda i: (i, 0, 0)), rows_of(128), row_of(), whole(16, D)],
-        out_specs=[rows_of(D)] * 4 + [whole(136, D)],
-        out_shape=[
-            shape_of((rows, D), BF16),
-            shape_of((rows, D), BF16),
-            shape_of((rows, D), F32),
-            shape_of((rows, D), F32),
-            shape_of((136, D), F32),
-        ],
-        compiler_params=PARAMS,
-        name="rowside",
-    )(qkvf, grad_attended, probs, score, inverse, kept, doc_col, doc_ids, edges)
-    heads = lax.all_gather(head, "seq")
-    use = (jnp.arange(4) > seq) & (heads[:, 129, 0] == edges[-1, 0].astype(F32))
-    finish = jnp.sum(jnp.where(use[:, None, None], heads, 0.0), axis=0)
-
-    back = lambda i: steps - 1 - i
-    grads, g_qkvf = pl.pallas_call(
-        column_kernel,
-        grid=(steps,),
-        in_specs=[rows_of(D, back), rows_of(4 * D, back)]
-        + [rows_of(D, back)] * 5
-        + [rows_of(128, back), row_of(back), whole(16, D), whole(8, D), whole(136, D)],
-        out_specs=[rows_of(4 * D, back), whole(D, 4 * D)],
-        out_shape=[shape_of((rows, 4 * D), BF16), shape_of((D, 4 * D), F32)],
-        scratch_shapes=[pltpu.VMEM((136, D), F32)],
-        compiler_params=PARAMS,
-        name="colside",
-    )(
-        tokens, qkvf, grad_attended, grad_q, reading, grad_numer, grad_total, doc_col, doc_ids,
-        edges, small, finish,
+    grad_input, ff, g0, g1, s1, s2 = back(
+        count, tokens, qkvf, grad_attended, probs, score, inverse, kept, grad_middle, doc_ids,
+        small, w_qkvf, pack, ff_small,
     )
-
-    grad_input, g_small_one = pl.pallas_call(
-        input_kernel,
-        grid=(steps,),
-        in_specs=[rows_of(D), rows_of(4 * D), rows_of(D), whole(D, 4 * D), whole(8, D)],
-        out_specs=[rows_of(D), whole(8, D)],
-        out_shape=[shape_of((rows, D), F32), shape_of((8, D), F32)],
-        compiler_params=PARAMS,
-        name="inputside",
-    )(tokens, grads, grad_middle, w_qkvf, small)
-
-    scatter = lambda a, dim=0: lax.psum(
-        lax.psum_scatter(a, "fsdp", scatter_dimension=dim, tiled=True), "seq"
-    )
-    g_qkvf = scatter(g_qkvf)
-    g_wo, g_wh, g_wr = scatter(g_wo), scatter(g_wh), scatter(g_wr, 1).T
-    vector = jnp.concatenate(
-        [g_small_one[0], g_small_one[1], g_small[2], g_small[3], g_bias[0], g_small[4]]
-    )
-    vector = lax.psum(vector, ("fsdp", "seq"))
-    at = lax.axis_index("fsdp")
-    pick = lambda start, size: lax.dynamic_slice(vector, (start + at * size,), (size,))
-    return (
-        out,
-        grad_input,
-        g_qkvf[:, 0:D],
-        g_qkvf[:, D : 2 * D],
-        g_qkvf[:, 2 * D : 3 * D],
-        g_qkvf[:, 3 * D :],
-        g_wo,
-        g_wh,
-        g_wr,
-        pick(0, part),
-        pick(D, part),
-        pick(2 * D, part),
-        pick(3 * D, part),
-        pick(4 * D, 4 * part),
-        pick(4 * D + FF, part),
-    )
+    grads = finish(count, part, ff, g0, g1, s1, s2)
+    return (out, grad_input, *grads[:7], *(a.reshape(-1) for a in grads[7:]))
 
 
 def solution(mesh):

time: 596 us -> 275 us (0.46)
  waiting for transfers between devices: 295 us -> 0 us
  Pallas kernels: 225 us -> 269 us
  blocking collectives: 41.2 us -> 0 us
  between operations: 16.5 us -> 0.67 us
  local copies, waits for them, and re-layouts: 12.5 us -> 4.64 us
    reduce_scatter x4 -> x0, waiting for transfers between devices: 269 us -> none  [on_device(): lax.psum_scatter(a, 'fsdp', scatter_dimension=dim, tiled=True)]
    pallas_call x4 -> x3, Pallas kernels: 130 us -> 173 us  [the longest x1 124 us: back(): pl.pallas_call(functools.partial(back_kernel, count, last), grid=(last +...]
    psum x1 -> x0, blocking collectives: 41.2 us -> none  [on_device(): vector = lax.psum(vector, ('fsdp', 'seq'))]
    all_gather x1 -> x0, waiting for transfers between devices: 21.3 us -> none  [on_device(): heads = lax.all_gather(head, 'seq')]
  transfers between devices with their start and end apart: 6 -> 0, of which waited for: 5 -> 0; matrix products, arithmetic and copies ran while one was open for 1% -> 0% of each run, Pallas kernels for 9% -> 0%
where the time goes in v3:
time: 275 us; the launch traced here: 274 us
  Pallas kernels  269 us (98%)
  local copies, waits for them, and re-layouts  4.64 us (2%)
    pallas_call x1, Pallas kernels, back(): pl.pallas_call(functools.partial(back_kernel, count, last), grid=(last +...  124 us
    pallas_call x1, Pallas kernels, front(): pl.pallas_call(functools.partial(front_kernel, count), grid=(17,), in_spe...  95.5 us
    pallas_call x1, Pallas kernels, on_device(): pl.pallas_call(forward_kernel, grid=(rows // FEED_ROWS,), in_specs=[tall]...  45.4 us

profile of v3, /device:TPU:0, one launch (start us, length us, event | category | flops | bytes accessed | tf_op | source)
XLA Modules:
  0.0 273.8 jit_solution(8018471978604285962)
XLA Ops:
  0.7 95.5 %front.1 = (bf16[2048,2048]{1,0:T(8,128)(2,1)}, bf16[2048,512]{1,0:T(8,128)(2,1)}, f32[2048,512]{1,0:T(8,128)}, f32[2048,512]{1,0:T(8,128)}, f32[2048,512]{1,0:T...) custom-call(bf16[2048,512]{1,0:T(8,128)(2,1)} %xs_ref.1, ...), custom_call_target="tpu_custom_call" | custom-call | tf_op jit(solution)/shard_map/front/pallas_call | solution.py:545
  96.2 45.4 %feed.1 = (bf16[2048,512]{1,0:T(8,128)(2,1)}, f32[2048,512]{1,0:T(8,128)}, bf16[2048,512]{1,0:T(8,128)(2,1)}, bf16[4,8,64,1152]{3,2,1,0:T(8,128)(2,1)}, f32[16,512]{1,0:T(8,128)}) custom-call(bf16[2048,512]{1,0:T(8,128)(2,1)} %xs_ref.1, bf16[2048,512]{1,0:T(8,128)(2,1)} %get-tuple-element.51.o_ref, bf16[2048,512]{1,0:T(8,128)(2,1)} %g_ref.1, ...), custom_call_target="tpu_custom_call" | custom-call | tf_op jit(solution)/shard_map/feed/pallas_call | solution.py:1269
  141.6 124.5 %back.1 = (f32[2048,512]{1,0:T(8,128)}, f32[4,64,1152]{2,1,0:T(8,128)}, f32[4,64,256]{2,1,0:T(8,128)}, f32[4,64,256]{2,1,0:T(8,128)}, f32[16,512]{1,0:T(8,128)}, /*index=5*/f32[8,512]{1,0:T(8,128)}) custom-call(bf16[2048,512]{1,0:T(8,128)(2,1)} %xs_ref.1, bf16[2048,512]{1,0:T(8,128)(2,1)} %xs_ref.1, bf16[2048,2048]{1,0:T(8,128)(2,1)} %get-tuple-element.58.qkvf_ref, ...), custom_call_target="tpu_custom_call" | custom-call | tf_op jit(solution)/shard_map/back/pallas_call | solution.py:1137
  266.0 3.2 %finish.1 = (f32[64,512]{1,0:T(8,128)}, f32[64,512]{1,0:T(8,128)}, f32[64,512]{1,0:T(8,128)}, f32[64,512]{1,0:T(8,128)}, f32[64,512]{1,0:T(8,128)}, /*index=5*/f...) custom-call(f32[4,64,1152]{2,1,0:T(8,128)} %get-tuple-element.69.ff_, ...), custom_call_target="tpu_custom_call" | custom-call | tf_op jit(solution)/shard_map/finish/pallas_call | solution.py:1221
  269.2 4.6 %copy.32 = f32[2048,512]{1,0:T(8,128)} copy(f32[2048,512]{1,0:T(8,128)} %get-tuple-element.103) | data formatting | bytes 8388608

commit v4 on v3

--- a/solution.py
+++ b/solution.py
@@ -221,109 +221,125 @@
 
 
 class Gather:
-    def __init__(self, count, mine, held, sems):
-        self.count, self.mine, self.held = count, mine, held
-        self.across, self.core, self.chip, self.onward, self.local = sems
+    def __init__(self, count, mine, held, base, width, four, sems):
+        self.count, self.mine, self.held, self.four = count, mine, held, four
+        self.far, self.near, self.core, self.chip, self.onward, self.local = sems
         self.seq, self.at, self.sibling, self.beside = places()
-        self.quarter = held.shape[2] // 4
+        self.base, self.share = base, width // (4 if four else 2)
+        self.evens = range(0, count, 2)
 
     def lanes(self, seq):
-        return pl.ds(pl.multiple_of(seq * self.quarter, self.quarter), self.quarter)
-
-    def part(self, owner, seq):
-        return self.held.at[owner, :, self.lanes(seq)]
-
-    def first(self, k):
+        place = seq if self.four else lax.rem(seq, 2)
+        return pl.ds(pl.multiple_of(self.base + place * self.share, 128), self.share)
+
+    def part(self, k, seq):
+        return self.held.at[self.at ^ k, :, self.lanes(seq)]
+
+    def source(self, k):
+        if k:
+            return self.part(k, self.seq)
+        return self.mine.at[:, self.lanes(self.seq)]
+
+    def own(self):
+        return pltpu.make_async_copy(self.source(0), self.part(0, self.seq), self.local)
+
+    def over(self, sems, k, **device):
+        return push(self.source(k), self.part(k, self.seq), sems[0].at[k], sems[1].at[k], **device)
+
+    def come(self, sems, k, owner):
+        here = self.part(owner, self.seq)
+        return push(here, here, sems[0].at[k], sems[1].at[k], seq=self.sibling)
+
+    def far_out(self, k):
         return push(
-            self.mine.at[:, self.lanes(self.seq)], self.part(self.at, self.seq),
-            self.across[0].at[k], self.across[1].at[k], fsdp=self.at ^ k,
-        )
-
-    def first_in(self, k):
-        here = self.part(self.at ^ k, self.seq)
-        return push(here, here, self.across[0].at[k], self.across[1].at[k], fsdp=self.at ^ k)
-
-    def own(self):
-        return pltpu.make_async_copy(
-            self.mine.at[:, self.lanes(self.seq)], self.part(self.at, self.seq), self.local
-        )
+            self.source(0), self.part(0, self.seq), self.far[0].at[k], self.far[1].at[k],
+            fsdp=self.at ^ k,
+        )
+
+    def far_in(self, k):
+        return self.come(self.far, k, k)
+
+    def near_out(self, k):
+        return self.over(self.near, k, fsdp=self.at ^ 1)
+
+    def near_in(self, k):
+        return self.come(self.near, k, k ^ 1)
 
     def start(self):
-        for k in range(1, self.count):
-            self.first(k).start()
         self.own().start()
-
-    def hop(self, sems, source, target, k):
-        if k is None:
-            ref, n = self.held.at[:, :, self.lanes(source)], 0
-        else:
-            ref, n = self.part(self.at ^ k, source), k
-        return push(ref, ref, sems[0].at[n], sems[1].at[n], seq=target)
-
-    def sent(self, n, k):
-        if n == 0:
-            return self.hop(self.core, self.seq, self.sibling, k)
-        if n == 1:
-            return self.hop(self.chip, self.seq, self.beside, k)
-        return self.hop(self.onward, self.beside, self.sibling, k)
-
-    def come(self, n, k):
-        if n == 0:
-            return self.hop(self.core, self.sibling, self.sibling, k)
-        if n == 1:
-            return self.hop(self.chip, self.beside, self.beside, k)
-        return self.hop(self.onward, lax.rem(self.sibling + 2, 4), self.sibling, k)
+        for k in self.evens[1:]:
+            self.far_out(k).start()
+        self.near_out(0).start()
 
     def second(self):
+        for k in self.evens[1:]:
+            self.far_in(k).wait_recv()
+            self.near_out(k).start()
+
+    def hop(self, sems, source, target):
+        here = self.held.at[:, :, self.lanes(source)]
+        return push(here, here, sems[0].at[0], sems[1].at[0], seq=target)
+
+    def third(self):
         self.own().wait()
-        for k in range(1, self.count):
-            self.first_in(k).wait_recv()
-        self.sent(0, None).start()
-        self.sent(1, None).start()
-
-    def third(self):
-        self.come(1, None).wait_recv()
-        self.sent(2, None).start()
+        for k in self.evens:
+            self.near_in(k).wait_recv()
+        self.hop(self.core, self.seq, self.sibling).start()
+        if self.four:
+            self.hop(self.chip, self.seq, self.beside).start()
+
+    def fourth(self):
+        self.hop(self.chip, self.beside, self.beside).wait_recv()
+        self.hop(self.onward, self.beside, self.sibling).start()
 
     def finish(self):
-        for n in range(3):
-            self.sent(n, None).wait_send()
-        self.come(0, None).wait_recv()
-        self.come(2, None).wait_recv()
-        for k in range(1, self.count):
-            self.first(k).wait_send()
-
-    def second_each(self):
+        self.hop(self.core, self.sibling, self.sibling).wait_recv()
+        self.hop(self.core, self.seq, self.sibling).wait_send()
+        if self.four:
+            self.hop(self.onward, lax.rem(self.sibling + 2, 4), self.sibling).wait_recv()
+            self.hop(self.chip, self.seq, self.beside).wait_send()
+            self.hop(self.onward, self.beside, self.sibling).wait_send()
+
+    def core_out(self, k):
+        return self.over(self.core, k, seq=self.sibling)
+
+    def core_in(self, k):
+        here = self.part(k, self.sibling)
+        return push(here, here, self.core[0].at[k], self.core[1].at[k], seq=self.sibling)
+
+    def at_once(self, between):
+        self.start()
+        self.core_out(0).start()
+        for k in self.evens[1:]:
+            self.far_in(k).wait_recv()
+            self.near_out(k).start()
+            self.core_out(k).start()
+        between()
+        for k in self.evens:
+            self.near_in(k).wait_recv()
+            self.core_out(k ^ 1).start()
+        self.own().wait()
         for k in range(self.count):
+            self.core_in(k).wait_recv()
+
+    def drain(self, each=False):
+        for k in self.evens:
+            self.near_out(k).wait_send()
             if k:
-                self.first_in(k).wait_recv()
-            else:
-                self.own().wait()
-            self.sent(0, k).start()
-            self.sent(1, k).start()
-        for k in range(self.count):
-            self.come(1, k).wait_recv()
-            self.sent(2, k).start()
-        for k in range(self.count):
-            self.come(0, k).wait_recv()
-            self.come(2, k).wait_recv()
-
-    def drain_each(self):
-        for k in range(self.count):
-            for n in range(3):
-                self.sent(n, k).wait_send()
-        for k in range(1, self.count):
-            self.first(k).wait_send()
+                self.far_out(k).wait_send()
+        if each:
+            for k in range(self.count):
+                self.core_out(k).wait_send()
 
 
 def gather_sems(count, each):
     n = count if each else 1
     pair = lambda size: [pltpu.SemaphoreType.DMA((size,)), pltpu.SemaphoreType.DMA((size,))]
-    return pair(count) + pair(n) + pair(n) + pair(n) + [pltpu.SemaphoreType.DMA]
+    return pair(count) + pair(count) + pair(n) + pair(1) + pair(1) + [pltpu.SemaphoreType.DMA]
 
 
 def bundle(refs):
-    return (refs[0], refs[1]), (refs[2], refs[3]), (refs[4], refs[5]), (refs[6], refs[7]), refs[8]
+    return [(refs[2 * n], refs[2 * n + 1]) for n in range(5)] + [refs[10]]
 
 
 class States:
@@ -375,33 +391,35 @@
 
 
 def spread_small(vec_refs, bias_ref, out_ref):
-    part = vec_refs[0].shape[1]
-
     def repeat(values):
         width = values.shape[1]
-        rows = lax.broadcasted_iota(jnp.int32, (width, D), 0)
-        lanes = lax.broadcasted_iota(jnp.int32, (width, D), 1)
+        rows = lax.broadcasted_iota(jnp.int32, (width, 128), 0)
+        lanes = lax.broadcasted_iota(jnp.int32, (width, 128), 1)
         pick = jnp.where(lax.rem(lanes, width) == rows, 1.0, 0.0).astype(BF16)
         return dot(jnp.broadcast_to(values, (8, width)).astype(BF16), pick)[0:1]
 
     out_ref[...] = jnp.zeros_like(out_ref)
     for n, ref in enumerate(vec_refs):
         out_ref[n : n + 1] = repeat(ref[...])
-    out_ref[5:6] = repeat(bias_ref[...])
-    return part
+    for b in range(max(bias_ref.shape[1] // 128, 1)):
+        out_ref[5 + b : 6 + b] = repeat(bias_ref[:, b * 128 : (b + 1) * 128])
 
 
 def join_small(count, part, gathered, vec_ref, bias_ref):
     lanes = lax.broadcasted_iota(jnp.int32, (8, D), 1)
     total = jnp.zeros((8, D), F32)
     for f in range(count):
-        total = jnp.where(lanes // part == f, gathered[f], total)
+        total = jnp.where(lanes // part == f, wide(gathered[f], 4), total)
     vec_ref[...] = total
+    size = 4 * part
     for r in range(4):
-        row = jnp.zeros((8, D), F32)
-        for f in range(count):
-            row = jnp.where((lanes + r * D) // (4 * part) == f, gathered[f], row)
-        bias_ref[0:1, r * D : (r + 1) * D] = row[5:6]
+        at = lanes[0:1] + r * D
+        row = jnp.zeros((1, D), F32)
+        for f in range(r * D // size, -(-(r + 1) * D // size)):
+            for b in range(max(size // 128, 1)):
+                use = (at // size == f) & (lax.rem(at, size) // 128 == b)
+                row = jnp.where(use, wide(gathered[f, 5 + b : 6 + b], 4), row)
+        bias_ref[0:1, r * D : (r + 1) * D] = row
 
 
 def front_kernel(
@@ -414,17 +432,17 @@
     step = pl.program_id(0)
     seq, at, _, _ = places()
     link = mine.dtype
-    first_sems, sems = bundle(sems[:9]), sems[9:]
-    o_sems, sems = bundle(sems[:9]), sems[9:]
-    h_sems, sems = bundle(sems[:9]), sems[9:]
-    r_sems, sems = bundle(sems[:9]), sems[9:]
+    groups_of_sems = []
+    for _ in range(5):
+        groups_of_sems.append(bundle(sems[:11]))
+        sems = sems[11:]
     small_send, small_recv, state_send, state_recv, out_sem = sems
-    main = Gather(count, mine, w_all, first_sems)
-    later = [
-        Gather(count, mine_o, wo_out, o_sems),
-        Gather(count, mine_h, wh_out, h_sems),
-        Gather(count, mine_r, wr_out, r_sems),
-    ]
+    main = Gather(count, mine, w_all, D, 3 * D, False, groups_of_sems[0])
+    q_piece = Gather(count, mine, w_all, 0, D, False, groups_of_sems[1])
+    o_piece = Gather(count, mine_o, wo_out, 0, D, True, groups_of_sems[2])
+    h_piece = Gather(count, mine_h, wh_out, 0, FF, True, groups_of_sems[3])
+    r_piece = Gather(count, mine_r, wr_out, 0, D, False, groups_of_sems[4])
+    later = (q_piece, o_piece, h_piece, r_piece)
     states = States(tails, tail_rows, (state_send, state_recv))
 
     def small_copy(k, owner):
@@ -444,21 +462,23 @@
         for n, ref in enumerate((wq_ref, wk_ref, wv_ref, ws_ref)):
             mine[:, n * D : (n + 1) * D] = ref[...].astype(BF16).astype(link)
         spread_small((v0, v1, v2, v3, v4), bias_in, spread)
-        main.start()
         for k in range(1, count):
             small_copy(k, at).start()
-        mine_o[...] = wo_ref[...].astype(BF16).astype(link)
-        mine_h[...] = wh_ref[...].astype(BF16).astype(link)
-        mine_r[...] = wr_ref[...].astype(BF16).astype(link)
-        doc_parts(doc_ref, col_ref, edge_ref)
-        tail[...] = jnp.zeros_like(tail)
-        smalls[at] = spread[...]
-        main.second_each()
-        for k in range(1, count):
-            small_copy(k, at ^ k).wait_recv()
-        join_small(count, v0.shape[1], smalls, vec_out, bias_out)
-        for piece in later:
-            piece.start()
+
+        def between():
+            mine_o[...] = wo_ref[...].astype(BF16).astype(link)
+            mine_h[...] = wh_ref[...].astype(BF16).astype(link)
+            mine_r[...] = wr_ref[...].astype(BF16).astype(link)
+            doc_parts(doc_ref, col_ref, edge_ref)
+            tail[...] = jnp.zeros_like(tail)
+            smalls[at] = spread[...]
+            for k in range(1, count):
+                small_copy(k, at ^ k).wait_recv()
+            join_small(count, v0.shape[1], smalls, vec_out, bias_out)
+            for piece in later:
+                piece.start()
+
+        main.at_once(between)
 
     @pl.when(step < 8)
     def _():
@@ -476,10 +496,20 @@
         tail[64:128] += values
         tail[128:129] += jnp.sum(slots.astype(F32), axis=0, keepdims=True)
 
-    @pl.when(step == 5)
-    def _():
-        for piece in later:
-            piece.second()
+    @pl.when(step == 1)
+    def _():
+        q_piece.second()
+        o_piece.second()
+
+    @pl.when(step == 4)
+    def _():
+        q_piece.third()
+        o_piece.third()
+        h_piece.second()
+
+    @pl.when(step == 6)
+    def _():
+        o_piece.fourth()
 
     @pl.when(step == 7)
     def _():
@@ -491,6 +521,8 @@
 
     @pl.when(step == 8)
     def _():
+        q_piece.finish()
+
         @pl.loop(0, 8)
         def _(n):
             here = pl.ds(pl.multiple_of(n * C, C), C)
@@ -507,10 +539,15 @@
             state[0:128] += use * tails[n].astype(F32)
             state[128:129] += use * tail_rows[n, 0:1]
 
-    @pl.when(step == 12)
-    def _():
-        for piece in later:
-            piece.third()
+    @pl.when(step == 9)
+    def _():
+        h_piece.third()
+        r_piece.second()
+
+    @pl.when(step == 13)
+    def _():
+        r_piece.third()
+        h_piece.fourth()
 
     @pl.when(step >= 9)
     def _():
@@ -523,9 +560,11 @@
 
     @pl.when(step == 16)
     def _():
+        for piece in (o_piece, h_piece, r_piece):
+            piece.finish()
         for piece in later:
-            piece.finish()
-        main.drain_each()
+            piece.drain()
+        main.drain(True)
         states.drain()
         for k in range(1, count):
             small_copy(k, at).wait_send()
@@ -570,8 +609,8 @@
             vmem((part, D), link),
             vmem((part, FF), link),
             vmem((4 * part, D), link),
-            vmem((8, D), F32),
-            vmem((count, 8, D), F32),
+            vmem((8, 128), F32),
+            vmem((count, 8, 128), F32),
             vmem((rows, 128), F32),
             vmem((16, D), F32),
             vmem((136, D), F32),
@@ -580,7 +619,7 @@
             vmem((4, 8, D), F32),
         ]
         + gather_sems(count, True)
-        + gather_sems(count, False) * 3
+        + gather_sems(count, False) * 4
         + [
             pltpu.SemaphoreType.DMA((count,)),
             pltpu.SemaphoreType.DMA((count,)),
@@ -609,7 +648,7 @@
 
 def forward_kernel(
     x_ref, o_ref, g_ref, small_ref, bias_ref, wo_ref, wh_ref, wr_ref,
-    y_ref, dy_ref, do_ref, pack_ref, gsmall_ref, gwo_ref, gwh_ref, gwr_ref,
+    y_ref, dy_ref, do_ref, pack_ref, pack_r_ref, gsmall_ref, gwo_ref, gwh_ref, gwr_ref,
 ):
     step = pl.program_id(0)
 
@@ -649,22 +688,23 @@
 
     @pl.when(step == pl.num_programs(0) - 1)
     def _():
-        _, count, part, _ = pack_ref.shape
+        half, part = pack_ref.shape[3], pack_ref.shape[4]
+        kind = pack_ref.dtype
         for q in range(4):
-            hidden_part = gwh_ref[:, q * 512 : (q + 1) * 512].reshape(count, part, 512)
-            pack_ref[q, :, :, 0:512] = hidden_part.astype(pack_ref.dtype)
-            out_part = gwo_ref[:, q * 128 : (q + 1) * 128].reshape(count, part, 128)
-            pack_ref[q, :, :, 512:640] = out_part.astype(pack_ref.dtype)
-            turned = gwr_ref[q * 128 : (q + 1) * 128].T.reshape(count, 4, part, 128)
-            for j in range(4):
-                pack_ref[q, :, :, 640 + j * 128 : 768 + j * 128] = turned[:, j].astype(
-                    pack_ref.dtype
-                )
+            x, c = q // 2, q % 2
+            hidden_part = gwh_ref[:, q * 512 : (q + 1) * 512].reshape(half, 2, part, 512)
+            out_part = gwo_ref[:, q * 128 : (q + 1) * 128].reshape(half, 2, part, 128)
+            turned = gwr_ref[q * 128 : (q + 1) * 128].T.reshape(half, 2, 4, part, 128)
+            for y in range(2):
+                pack_ref[c, x, y, :, :, 0:512] = hidden_part[:, y].astype(kind)
+                pack_ref[c, x, y, :, :, 512:640] = out_part[:, y].astype(kind)
+                for j in range(4):
+                    pack_r_ref[c, y, :, x, :, j * 128 : (j + 1) * 128] = turned[:, y, j].astype(kind)
 
 
 def row_body(
     n, qkvf_ref, do_ref, p_ref, s_ref, z_ref, kept_ref, col, row, edge_ref,
-    dq_ref, r_ref, dn_ref, dz_ref, head_ref,
+    r_ref, dn_ref, dz_ref, head_ref,
 ):
     first = edge_ref[pl.ds(0, 1)]
     before = edge_ref[pl.ds(8 + jnp.maximum(n - 1, 0), 1)]
@@ -675,8 +715,8 @@
     own = wide(flag(col, first), 4)
     for g in range(2):
         lanes = slice(g * GROUP, (g + 1) * GROUP)
-        queries, keys, values = (
-            qkvf_ref[:, part * D + g * GROUP : part * D + (g + 1) * GROUP] for part in range(3)
+        queries, values = (
+            qkvf_ref[:, part * D + g * GROUP : part * D + (g + 1) * GROUP] for part in (0, 2)
         )
         here, grads = slots[:, lanes], do_ref[:, lanes]
         probs, score, inverse = p_ref[:, lanes], s_ref[:, lanes], z_ref[:, lanes]
@@ -690,13 +730,6 @@
         back_score = shared - probs * head_sums(shared)
         back_numer = back_score * inverse * SCALE
         back_total = -(shared + back_score * score) * inverse
-        low = back_numer.astype(BF16)
-        back_affinity = masked(dot_nt(stacked(low), here), vis)
-        back_queries = select(dot(back_affinity, keys))
-        back_queries = back_queries + carried * dot(
-            low, expand(kept_ref[0, 0:64, lanes]).astype(BF16)
-        )
-        dq_ref[:, lanes] = back_queries.astype(BF16)
         reading = (probs * inverse).astype(BF16)
         r_ref[:, lanes] = reading
         dn_ref[:, lanes] = back_numer
@@ -709,8 +742,27 @@
         head_ref[128:129, lanes] += jnp.sum(mine * back_total, axis=0, keepdims=True)
 
 
+def query_body(n, qkvf_ref, kept_ref, col, row, edge_ref, dn_ref, dq_ref):
+    first = edge_ref[pl.ds(0, 1)]
+    before = edge_ref[pl.ds(8 + jnp.maximum(n - 1, 0), 1)]
+    last = jnp.where(n == 0, first, before)
+    vis = visible(col, row)
+    carried = wide(flag(col, last), 2)
+    slots = jnp.exp(qkvf_ref[:, 3 * D :].astype(F32)).astype(BF16)
+    for g in range(2):
+        lanes = slice(g * GROUP, (g + 1) * GROUP)
+        keys = qkvf_ref[:, D + g * GROUP : D + (g + 1) * GROUP]
+        low = dn_ref[:, lanes].astype(BF16)
+        back_affinity = masked(dot_nt(stacked(low), slots[:, lanes]), vis)
+        back_queries = select(dot(back_affinity, keys))
+        back_queries = back_queries + carried * dot(
+            low, expand(kept_ref[0, 0:64, lanes]).astype(BF16)
+        )
+        dq_ref[:, lanes] = back_queries.astype(BF16)
+
+
 def column_body(
-    n, g, qkvf_ref, do_ref, r_ref, dn_ref, dz_ref, col, row, edge_ref, state, d_ref
+    n, qkvf_ref, do_ref, r_ref, dn_ref, dz_ref, col, row, edge_ref, state, snap, snap_rows, d_ref
 ):
     newest = edge_ref[15:16]
     after = edge_ref[pl.ds(jnp.minimum(n + 1, 7), 1)]
@@ -720,196 +772,206 @@
     carried = wide(flag(col, following), 2)
     own = wide(flag(col, first), 2)
     kept = jnp.where(following == first, 1.0, 0.0)[:, :GROUP]
+    snap[n] = state[0:128].astype(BF16)
+    snap_rows[pl.ds(n, 1)] = state[128:129]
+    for g in range(2):
+        lanes = slice(g * GROUP, (g + 1) * GROUP)
+        queries = qkvf_ref[:, lanes]
+        here = jnp.exp(qkvf_ref[:, 3 * D + g * GROUP : 3 * D + (g + 1) * GROUP].astype(F32))
+        here = here.astype(BF16)
+        grads, reading, back_numer = do_ref[:, lanes], r_ref[:, lanes], dn_ref[:, lanes]
+        key_state = expand(state[0:64, lanes]).astype(BF16)
+        value_state = expand(state[64:128, lanes]).astype(BF16)
+        apart = stacked(here)
+        mix = masked(dot_nt(apart, reading), vis)
+        back_values = select(dot(mix, grads)) + carried * dot(here, value_state)
+        d_ref[:, 2 * D + g * GROUP : 2 * D + (g + 1) * GROUP] = back_values.astype(BF16)
+        back_affinity = masked(dot_nt(apart, back_numer.astype(BF16)), vis)
+        back_keys = select(dot(back_affinity, queries)) + carried * dot(here, key_state)
+        d_ref[:, D + g * GROUP : D + (g + 1) * GROUP] = back_keys.astype(BF16)
+        state[0:64, lanes] = kept * state[0:64, lanes] + compacted(
+            dot_tn((own * back_numer).astype(BF16), queries)
+        )
+        state[64:128, lanes] = kept * state[64:128, lanes] + compacted(
+            dot_tn((own * reading.astype(F32)).astype(BF16), grads)
+        )
+        state[128:129, lanes] = kept * state[128:129, lanes] + jnp.sum(
+            own * dz_ref[:, lanes], axis=0, keepdims=True
+        )
+
+
+def slot_body(n, qkvf_ref, do_ref, r_ref, dn_ref, dz_ref, col, row, edge_ref, snap, snap_rows, d_ref):
+    newest = edge_ref[15:16]
+    after = edge_ref[pl.ds(jnp.minimum(n + 1, 7), 1)]
+    following = jnp.where(n == 7, newest, after)
+    vis = visible_back(col, row)
+    carried = wide(flag(col, following), 2)
     left = lane_heads(C, 128) == 0
-
-    def lanes_of(part):
-        return pl.ds(pl.multiple_of(part * D + g * GROUP, GROUP), GROUP)
-
-    lanes = lanes_of(0)
-    queries, keys, values = (qkvf_ref[:, lanes_of(part)] for part in range(3))
-    written = jnp.exp(qkvf_ref[:, lanes_of(3)].astype(F32))
-    here = written.astype(BF16)
-    back_total = dz_ref[:, lanes]
-    total_high, total_low = split(back_total)
+    total_high, total_low = split(dz_ref[...])
     back_norm = dot(vis, total_high) + dot(vis, total_low)
-    grads, reading, back_numer = do_ref[:, lanes], r_ref[:, lanes], dn_ref[:, lanes]
-    numer_high, numer_low = split(back_numer)
-    key_state = expand(state[0:64, lanes]).astype(BF16)
-    value_state = expand(state[64:128, lanes]).astype(BF16)
-    apart = stacked(here)
-    mix = masked(dot_nt(apart, reading), vis)
-    back_values = select(dot(mix, grads)) + carried * dot(here, value_state)
-    d_ref[:, lanes_of(2)] = back_values.astype(BF16)
-    back_affinity = masked(dot_nt(apart, numer_high), vis)
-    back_keys = select(dot(back_affinity, queries)) + carried * dot(here, key_state)
-    d_ref[:, lanes_of(1)] = back_keys.astype(BF16)
-    back_mix = masked(dot_nt(stacked(values), grads), vis)
-    back_slots = back_norm + select(dot(back_mix, reading))
-    affinity = masked(dot_nt(stacked(keys), queries), vis)
-    parts = []
-    for p in range(2):
-        pair = slice(p * 128, (p + 1) * 128)
-        both = dot(
-            affinity[p * 512 : (p + 1) * 512],
-            jnp.concatenate([numer_high[:, pair], numer_low[:, pair]], axis=1),
-        )
-        both = both[:, :128] + both[:, 128:]
-        parts.append(jnp.where(left, both[:C], both[C:]))
-    back_slots = back_slots + jnp.concatenate(parts, axis=1)
-    back_slots = back_slots + carried * (
-        dot_nt(keys, key_state) + dot_nt(values, value_state) + state[128:129, lanes]
-    )
-    d_ref[:, lanes_of(3)] = (back_slots * written).astype(BF16)
-    state[0:64, lanes] = kept * state[0:64, lanes] + compacted(
-        dot_tn((own * back_numer).astype(BF16), queries)
-    )
-    state[64:128, lanes] = kept * state[64:128, lanes] + compacted(
-        dot_tn((own * reading.astype(F32)).astype(BF16), grads)
-    )
-    state[128:129, lanes] = kept * state[128:129, lanes] + jnp.sum(
-        own * back_total, axis=0, keepdims=True
-    )
+    norm_state = snap_rows[pl.ds(n, 1)]
+    for g in range(2):
+        lanes = slice(g * GROUP, (g + 1) * GROUP)
+        queries, keys, values, logits = (
+            qkvf_ref[:, part * D + g * GROUP : part * D + (g + 1) * GROUP] for part in range(4)
+        )
+        grads, reading = do_ref[:, lanes], r_ref[:, lanes]
+        numer_high, numer_low = split(dn_ref[:, lanes])
+        key_state = expand(snap[n, 0:64, lanes])
+        value_state = expand(snap[n, 64:128, lanes])
+        back_mix = masked(dot_nt(stacked(values), grads), vis)
+        back_slots = back_norm[:, lanes] + select(dot(back_mix, reading))
+        affinity = masked(dot_nt(stacked(keys), queries), vis)
+        parts = []
+        for p in range(2):
+            pair = slice(p * 128, (p + 1) * 128)
+            both = dot(
+                affinity[p * 512 : (p + 1) * 512],
+                jnp.concatenate([numer_high[:, pair], numer_low[:, pair]], axis=1),
+            )
+            both = both[:, :128] + both[:, 128:]
+            parts.append(jnp.where(left, both[:C], both[C:]))
+        back_slots = back_slots + jnp.concatenate(parts, axis=1)
+        back_slots = back_slots + carried * (
+            dot_nt(keys, key_state) + dot_nt(values, value_state) + norm_state[:, lanes]
+        )
+        d_ref[:, 3 * D + g * GROUP : 3 * D + (g + 1) * GROUP] = (
+            back_slots * jnp.exp(logits.astype(F32))
+        ).astype(BF16)
 
 
 class Scatter:
-    def __init__(self, count, source, own, from_core, to_chip, from_chip, from_row, total, out, sems):
-        self.count, self.source, self.own, self.out = count, source, own, out
-        self.from_core, self.to_chip, self.from_chip = from_core, to_chip, from_chip
-        self.to_row, self.from_row, self.total = to_chip, from_row, total
-        (self.core, self.local, self.chip, self.row, self.last, self.done) = sems
+    def __init__(self, count, source, own, axes, direct, out, buffers):
+        self.axes, self.direct, self.out = axes, direct, out
         self.seq, self.at, self.sibling, self.beside = places()
-        self.c = lax.rem(self.seq, 2)
-        self.x = self.seq // 2
-
-    def copy_core(self, n):
-        return push(
-            self.source.at[2 * n + 1 - self.c], self.from_core.at[n],
-            self.core.at[0, n], self.core.at[1, n], seq=self.sibling,
-        )
-
-    def copy_own(self, n):
-        return pltpu.make_async_copy(self.source.at[2 * n + self.c], self.own, self.local)
-
-    def copy_chip(self):
-        return push(
-            self.to_chip, self.from_chip, self.chip.at[0], self.chip.at[1], seq=self.beside
-        )
-
-    def copy_row(self, k):
-        return push(
-            self.to_row.at[self.at ^ k], self.from_row.at[self.at],
-            self.row.at[0, k], self.row.at[1, k], fsdp=self.at ^ k,
-        )
-
-    def row_in(self, k):
-        here = self.from_row.at[self.at ^ k]
-        return push(here, here, self.row.at[0, k], self.row.at[1, k], fsdp=self.at ^ k)
+        self.source, self.own = source, own
+        self.core = lax.rem(self.seq, 2)
+        self.total, self.local, self.last, self.done = buffers[:4]
+        self.stages = []
+        size = source.shape[0]
+        base = 0
+        for n, axis in enumerate(axes):
+            ways = {"core": 2, "x": 2, "y": 2, "z": count // 2, "all": count}[axis]
+            size = size // ways
+            me = {
+                "core": self.core, "x": self.seq // 2, "y": lax.rem(self.at, 2), "z": self.at // 2,
+                "all": self.at,
+            }[axis]
+            held = source
+            if own is not None and n > 0:
+                held = own
+            come, sems = buffers[4 + 2 * n], buffers[5 + 2 * n]
+            self.stages.append((axis, ways, size, base, me, held, come, sems))
+            if own is None or n > 0:
+                base = base + me * size
+
+    def copies(self, n):
+        axis, ways, size, base, me, held, come, sems = self.stages[n]
+        for k in range(1, ways):
+            if axis in ("core", "x"):
+                device = {"seq": self.sibling if axis == "core" else self.beside}
+            else:
+                device = {"fsdp": self.at ^ (2 * k if axis == "z" else k)}
+            yield push(
+                held.at[pl.ds(base + (me ^ k) * size, size)], come.at[k - 1],
+                sems.at[0, k - 1], sems.at[1, k - 1], **device,
+            )
+
+    def copy_own(self):
+        size = self.source.shape[0] // 2
+        return pltpu.make_async_copy(
+            self.source.at[pl.ds(self.core * size, size)], self.own, self.local
+        )
+
+    def start(self):
+        for copy in self.copies(0):
+            copy.start()
+        if self.own is not None:
+            self.copy_own().start()
+
+    def advance(self, n):
+        axis, ways, size, base, me, held, come, sems = self.stages[n]
+        for copy in self.copies(n):
+            copy.wait_recv()
+        mine = held
+        first = base + me * size
+        if n == 0 and self.own is not None:
+            self.copy_own().wait()
+            mine, first = self.own, 0
+
+        def added(slab):
+            total = mine[first + slab].astype(F32)
+            for k in range(1, ways):
+                total = total + come[k - 1, slab].astype(F32)
+            return total
+
+        if n + 1 == len(self.stages):
+            self.total[...] = added(0)
+            self.copy_done().start()
+            for copy in self.sent():
+                copy.start()
+            return
+
+        @pl.loop(0, size)
+        def _(slab):
+            mine[first + slab] = added(slab).astype(mine.dtype)
+
+        for copy in self.copies(n + 1):
+            copy.start()
 
     def copy_done(self):
         return pltpu.make_async_copy(self.total, self.out.at[self.seq], self.done)
 
-    def sent(self, n):
-        if n == 2:
-            here = self.out.at[self.beside]
-            return push(here, here, self.last.at[0, 2], self.last.at[1, 2], seq=self.sibling)
-        target = (self.sibling, self.beside)[n]
-        return push(
-            self.total, self.out.at[self.seq], self.last.at[0, n], self.last.at[1, n], seq=target
-        )
-
-    def come(self, n):
-        if n == 2:
-            here = self.out.at[lax.rem(self.sibling + 2, 4)]
-            return push(here, here, self.last.at[0, 2], self.last.at[1, 2], seq=self.sibling)
-        source = (self.sibling, self.beside)[n]
+    def sent(self):
+        other = lax.rem(self.sibling + 2, 4)
+        for n, target in enumerate((self.sibling, self.beside, other)[: 3 if self.direct else 2]):
+            yield push(
+                self.total, self.out.at[self.seq], self.last.at[0, n], self.last.at[1, n], seq=target
+            )
+
+    def forwarded(self, source):
+        here = self.out.at[source]
+        return push(here, here, self.last.at[0, 2], self.last.at[1, 2], seq=self.sibling)
+
+    def come_in(self, n, source):
         here = self.out.at[source]
         return push(here, here, self.last.at[0, n], self.last.at[1, n], seq=source)
 
-    def mine(self, n, f):
-        if self.own is None:
-            return self.source[2 * n + self.c, f].astype(F32)
-        return self.own[f].astype(F32)
-
-    def start(self):
-        for n in range(2):
-            self.copy_core(n).start()
-        if self.own is not None:
-            self.copy_own(1 - self.x).start()
-
-    def second(self):
-        for n in range(2):
-            self.copy_core(n).wait_recv()
-        n = 1 - self.x
-        if self.own is not None:
-            self.copy_own(n).wait()
-
-        @pl.loop(0, self.count)
-        def _(f):
-            both = self.mine(n, f) + self.from_core[n, f].astype(F32)
-            self.to_chip[f] = both.astype(self.to_chip.dtype)
-
-        self.copy_chip().start()
-        if self.own is not None:
-            self.copy_own(self.x).start()
-
-    def third(self):
-        self.copy_chip().wait_recv()
-        self.copy_chip().wait_send()
-        n = self.x
-        if self.own is not None:
-            self.copy_own(n).wait()
-
-        @pl.loop(0, self.count)
-        def _(f):
-            three = self.mine(n, f) + self.from_core[n, f].astype(F32) + self.from_chip[f].astype(F32)
-            self.to_row[f] = three.astype(self.to_row.dtype)
-
-        for k in range(1, self.count):
-            self.copy_row(k).start()
-        self.total[...] = (
-            self.mine(n, self.at)
-            + self.from_core[n, self.at].astype(F32)
-            + self.from_chip[self.at].astype(F32)
-        )
-
-    def fourth(self):
-        for k in range(1, self.count):
-            self.row_in(k).wait_recv()
-        total = self.total[...]
-        for k in range(1, self.count):
-            total = total + self.from_row[self.at ^ k].astype(F32)
-        self.total[...] = total
-        self.copy_done().start()
-        self.sent(0).start()
-        self.sent(1).start()
-
-    def fifth(self):
-        self.come(1).wait_recv()
-        self.sent(2).start()
+    def forward(self):
+        self.come_in(1, self.beside).wait_recv()
+        self.forwarded(self.beside).start()
 
     def finish(self):
-        self.come(0).wait_recv()
-        self.come(2).wait_recv()
+        other = lax.rem(self.sibling + 2, 4)
+        self.come_in(0, self.sibling).wait_recv()
+        if self.direct:
+            self.come_in(1, self.beside).wait_recv()
+        else:
+            self.forwarded(self.beside).wait_send()
+        self.forwarded(other).wait_recv()
         self.copy_done().wait()
-        for n in range(3):
-            self.sent(n).wait_send()
-        for n in range(2):
-            self.copy_core(n).wait_send()
-        for k in range(1, self.count):
-            self.copy_row(k).wait_send()
-
-
-def scatter_scratch(count, part, lanes, link, hbm):
+        for copy in self.sent():
+            copy.wait_send()
+        for n in range(len(self.stages)):
+            for copy in self.copies(n):
+                copy.wait_send()
+
+
+def scatter_scratch(count, part, lanes, link, axes, hbm):
     vmem, dma = pltpu.VMEM, pltpu.SemaphoreType.DMA
-    block = (count, part, lanes)
-    own = [vmem(block, link)] if hbm else []
-    return (
-        own
-        + [vmem((2, *block), link)]
-        + [vmem(block, link)] * 3
-        + [vmem((part, lanes), F32)]
-        + [dma((2, 2)), dma, dma((2,)), dma((2, count)), dma((2, 3)), dma]
-    )
+    size = 2 * 4 * count // 2
+    out = [vmem((size // 2, part, lanes), link)] if hbm else []
+    out += [vmem((part, lanes), F32), dma, dma((2, 3)), dma]
+    for axis in axes:
+        ways = {"core": 2, "x": 2, "y": 2, "z": count // 2, "all": count}[axis]
+        size = size // ways
+        out += [vmem((ways - 1, size, part, lanes), link), dma((2, ways - 1))]
+    return out
+
+
+OVER_X = ("core", "x", "y", "z")
+OVER_Y = ("core", "y", "z", "x")
+SHORT = ("core", "x", "all")
 
 
 class SmallSum:
@@ -967,62 +1029,88 @@
     ]
 
 
-ROW_STEPS, COLUMN_STEPS = 8, 16
-FIRST_COLUMN = ROW_STEPS + 1
-FIRST_INPUT = FIRST_COLUMN + COLUMN_STEPS
+FIRST_QUERY, TURN = 8, 16
+FIRST_COLUMN, FIRST_SLOT, FIRST_INPUT = 17, 25, 33
 
 
 def back_kernel(
     count, last_step, x_ref, xs_ref, qkvf_ref, do_ref, p_ref, s_ref, z_ref, kept_ref, dy_ref, doc_ref,
-    small_ref, w_ref, ffg_ref, ffs_ref,
-    gi_ref, ff_out, g0_out, g1_out, s1_out, s2_out,
+    small_ref, w_ref, ffg_ref, ffr_ref, ffs_ref,
+    gi_ref, ff_out, fr_out, q_out, kv_out, f_out, s1_out, s2_out,
     d_all, h_turned, reading, numer, total, col_ref, edge_ref, head, state, heads, head_rows,
-    piece0, piece1, last_small, *rest,
+    snap, snap_rows, q_piece, kv_piece, f_piece, last_small, *rest,
 ):
     step = pl.program_id(0)
     seq, at, _, _ = places()
-    link = piece0.dtype
-    ff = Scatter(count, ffg_ref, *rest[:6], ff_out, rest[6:12])
-    rest = rest[12:]
-    first_piece = Scatter(count, piece0, None, *rest[:5], g0_out, rest[5:11])
-    rest = rest[11:]
-    second_piece = Scatter(count, piece1, None, *rest[:5], g1_out, rest[5:11])
-    rest = rest[11:]
-    small_one = SmallSum(count, ffs_ref, *rest[:3], rest[3:5])
-    small_two = SmallSum(count, last_small, *rest[5:8], rest[8:10])
-    states = States(heads, head_rows, (rest[10], rest[11]))
+    link = q_piece.dtype
+
+    def take(size):
+        nonlocal rest
+        out, rest = rest[:size], rest[size:]
+        return out
+
+    (own,) = take(1)
+    ff = Scatter(count, ffg_ref, own, OVER_X, False, ff_out, take(12))
+    (own,) = take(1)
+    fr = Scatter(count, ffr_ref, own, OVER_Y, False, fr_out, take(12))
+    for_q = Scatter(count, q_piece, None, OVER_X, False, q_out, take(12))
+    for_kv = Scatter(count, kv_piece, None, OVER_X, False, kv_out, take(12))
+    for_f = Scatter(count, f_piece, None, SHORT, True, f_out, take(10))
+    small_one = SmallSum(count, ffs_ref, *take(3), take(2))
+    small_two = SmallSum(count, last_small, *take(3), take(2))
+    states = States(heads, head_rows, take(2))
+
+    def chunk(first, turned=False):
+        n = step - first
+        n = 7 - n if turned else n
+        here = pl.ds(pl.multiple_of(n * C, C), C)
+        return n, here, col_ref[here], doc_ref[:, here].astype(F32)
+
+    def weight_grad(piece, d_lanes, lanes, short=False):
+        grad = dot(h_turned[...], d_all[:, d_lanes])
+        half, part = count // 2, piece.shape[1]
+        for q in range(4):
+            x, c = q // 2, q % 2
+            share = grad[:, q * 128 : (q + 1) * 128].reshape(half, 2, part, 128).astype(link)
+            if short:
+                first = (c * 2 + x) * count
+                piece[first : first + count, :, lanes] = share.reshape(count, part, 128)
+                continue
+            for y in range(2):
+                first = ((c * 2 + x) * 2 + y) * half
+                piece[first : first + half, :, lanes] = share[:, y]
 
     @pl.when(step == 0)
     def _():
         greet(count)
         ff.start()
+        fr.start()
         small_one.start()
         doc_parts(doc_ref, col_ref, edge_ref)
         head[...] = jnp.zeros_like(head)
         last_small[...] = jnp.zeros_like(last_small)
 
-    @pl.when(step < ROW_STEPS)
-    def _():
-        n = step
-        here = pl.ds(pl.multiple_of(n * C, C), C)
+    @pl.when(step < FIRST_QUERY)
+    def _():
+        n, here, col, row = chunk(0)
         unit, _ = norm_parts(x_ref[...].astype(F32))
         h_turned[:, here] = (unit * small_ref[0:1] + small_ref[1:2]).astype(BF16).T
         row_body(
-            n, qkvf_ref, do_ref, p_ref, s_ref, z_ref, kept_ref, col_ref[here],
-            doc_ref[:, here].astype(F32), edge_ref,
-            d_all.at[here, 0:D], reading.at[here], numer.at[here], total.at[here], head,
-        )
-
-    @pl.when(step == 2)
-    def _():
-        ff.second()
+            n, qkvf_ref, do_ref, p_ref, s_ref, z_ref, kept_ref, col, row, edge_ref,
+            reading.at[here], numer.at[here], total.at[here], head,
+        )
+
+    @pl.when(step == 3)
+    def _():
+        ff.advance(0)
+        fr.advance(0)
         small_one.second()
 
-    @pl.when(step == 5)
+    @pl.when(step == 6)
     def _():
         small_one.finish(s1_out)
 
-    @pl.when(step == ROW_STEPS - 1)
+    @pl.when(step == FIRST_QUERY - 1)
     def _():
         heads[seq] = head[0:128].astype(link)
         head_rows[seq, 0:1] = head[128:129]
@@ -1030,14 +1118,23 @@
         head_rows[seq, 2:8] = jnp.zeros((6, D), F32)
         states.start()
 
-    def weight_grad(piece, n, lanes):
-        grad = dot(h_turned[...], d_all[:, lanes])
-        piece[n] = grad.reshape(count, D // count, GROUP).astype(link)
-
-    @pl.when(step == ROW_STEPS)
-    def _():
-        weight_grad(piece0, 0, slice(0, GROUP))
-        weight_grad(piece1, 0, slice(GROUP, D))
+    @pl.when((step >= FIRST_QUERY) & (step < TURN))
+    def _():
+        n, here, col, row = chunk(FIRST_QUERY)
+        query_body(n, qkvf_ref, kept_ref, col, row, edge_ref, numer.at[here], d_all.at[here, 0:D])
+
+    @pl.when(step == FIRST_QUERY + 1)
+    def _():
+        fr.advance(1)
+
+    @pl.when(step == FIRST_QUERY + 4)
+    def _():
+        ff.advance(1)
+
+    @pl.when(step == TURN)
+    def _():
+        weight_grad(q_piece, slice(0, D), slice(0, 128))
+        for_q.start()
         states.finish()
         newest = edge_ref[15:16]
         state[...] = jnp.zeros_like(state)
@@ -1046,41 +1143,74 @@
             state[0:128] += use * heads[n].astype(F32)
             state[128:129] += use * head_rows[n, 0:1]
 
-    @pl.when((step >= FIRST_COLUMN) & (step < FIRST_INPUT))
-    def _():
-        n = 7 - lax.rem(step - FIRST_COLUMN, 8)
-        g = (step - FIRST_COLUMN) // 8
-        here = pl.ds(pl.multiple_of(n * C, C), C)
+    @pl.when((step >= FIRST_COLUMN) & (step < FIRST_SLOT))
+    def _():
+        n, here, col, row = chunk(FIRST_COLUMN, True)
         column_body(
-            n, g, qkvf_ref, do_ref, reading.at[here], numer.at[here], total.at[here], col_ref[here],
-            doc_ref[:, here].astype(F32), edge_ref, state, d_all.at[here],
-        )
+            n, qkvf_ref, do_ref, reading.at[here], numer.at[here], total.at[here], col, row, edge_ref,
+            state, snap, snap_rows, d_all.at[here],
+        )
+
+    @pl.when(step == FIRST_COLUMN)
+    def _():
+        ff.advance(2)
+        for_q.advance(0)
+
+    @pl.when(step == FIRST_COLUMN + 1)
+    def _():
+        fr.advance(2)
 
     @pl.when(step == FIRST_COLUMN + 2)
     def _():
-        ff.third()
+        for_q.advance(1)
+
+    @pl.when(step == FIRST_COLUMN + 4)
+    def _():
+        fr.advance(3)
+        for_q.advance(2)
+
+    @pl.when(step == FIRST_COLUMN + 5)
+    def _():
+        ff.advance(3)
+
+    @pl.when(step == FIRST_COLUMN + 6)
+    def _():
+        for_q.advance(3)
+        fr.forward()
 
     @pl.when(step == FIRST_COLUMN + 7)
     def _():
-        for w in range(1, 4):
-            weight_grad(piece0, w, slice(w * D, w * D + GROUP))
-        first_piece.start()
-
-    @pl.when(step == FIRST_COLUMN + 9)
-    def _():
-        first_piece.second()
-
-    @pl.when(step == FIRST_COLUMN + 12)
-    def _():
-        first_piece.third()
-
-    @pl.when(step == FIRST_COLUMN + 15)
-    def _():
-        for w in range(1, 4):
-            weight_grad(piece1, w, slice(w * D + GROUP, (w + 1) * D))
-        second_piece.start()
-        first_piece.fourth()
-        ff.fourth()
+        weight_grad(kv_piece, slice(D, 2 * D), slice(0, 128))
+        weight_grad(kv_piece, slice(2 * D, 3 * D), slice(128, 256))
+        for_kv.start()
+        ff.forward()
+
+    @pl.when((step >= FIRST_SLOT) & (step < FIRST_INPUT))
+    def _():
+        n, here, col, row = chunk(FIRST_SLOT, True)
+        slot_body(
+            n, qkvf_ref, do_ref, reading.at[here], numer.at[here], total.at[here], col, row, edge_ref,
+            snap, snap_rows, d_all.at[here],
+        )
+
+    @pl.when(step == FIRST_SLOT)
+    def _():
+        for_kv.advance(0)
+        for_q.forward()
+
+    @pl.when(step == FIRST_SLOT + 3)
+    def _():
+        for_kv.advance(1)
+
+    @pl.when(step == FIRST_SLOT + 5)
+    def _():
+        for_kv.advance(2)
+
+    @pl.when(step == FIRST_SLOT + 7)
+    def _():
+        weight_grad(f_piece, slice(3 * D, 4 * D), slice(0, 128), True)
+        for_f.start()
+        for_kv.advance(3)
 
     @pl.when(step >= FIRST_INPUT)
     def _():
@@ -1095,30 +1225,30 @@
 
     @pl.when(step == FIRST_INPUT)
     def _():
-        second_piece.second()
-        first_piece.fifth()
-        ff.fifth()
+        for_f.advance(0)
+        for_kv.forward()
 
     @pl.when(step == last_step - 1)
     def _():
-        second_piece.third()
+        for_f.advance(1)
 
     @pl.when(step == last_step)
     def _():
         small_two.start()
-        ff.finish()
-        first_piece.finish()
+        for piece in (ff, fr, for_q, for_kv):
+            piece.finish()
+        states.drain()
         small_two.second()
-        second_piece.fourth()
-        second_piece.fifth()
+        for_f.advance(2)
         small_two.finish(s2_out)
-        second_piece.finish()
-        states.drain()
-
-
-def back(count, tokens, qkvf, do, probs, score, inverse, kept, dy, doc_ids, small, w_all, ffg, ffs):
+        for_f.finish()
+
+
+def back(
+    count, tokens, qkvf, do, probs, score, inverse, kept, dy, doc_ids, small, w_all, ffg, ffr, ffs
+):
     rows = tokens.shape[0]
-    part, link = ffg.shape[2], ffg.dtype
+    part, link = ffg.shape[1], ffg.dtype
     size = 512 if link == BF16 else 256
     last = FIRST_INPUT + rows // size - 1
     once = lambda a: pl.BlockSpec(a.shape, lambda i: (0,) * a.ndim)
@@ -1126,27 +1256,37 @@
     vmem, dma = pltpu.VMEM, pltpu.SemaphoreType.DMA
 
     def early(i):
-        return jnp.minimum(i, ROW_STEPS - 1)
+        return jnp.minimum(i, FIRST_QUERY - 1)
+
+    def twice(i):
+        return jnp.where(i < FIRST_QUERY, i, jnp.clip(i - FIRST_QUERY, 0, 7))
+
+    def always(i):
+        turned = 7 - lax.rem(jnp.clip(i - FIRST_COLUMN, 0, 15), 8)
+        return jnp.where(i < TURN, twice(i), turned)
 
     def both(i):
-        turned = 7 - lax.rem(jnp.clip(i - FIRST_COLUMN, 0, COLUMN_STEPS - 1), 8)
-        return jnp.where(i < ROW_STEPS, i, turned)
+        turned = 7 - lax.rem(jnp.clip(i - FIRST_COLUMN, 0, 15), 8)
+        return jnp.where(i < FIRST_QUERY, i, turned)
 
     late = lambda i: (jnp.maximum(i - FIRST_INPUT, 0), 0)
     tall = pl.BlockSpec((size, D), late)
+    slabs = 4 * count
     return pl.pallas_call(
         functools.partial(back_kernel, count, last),
         grid=(last + 1,),
-        in_specs=[rows_of(D, early), tall, rows_of(4 * D, both), rows_of(D, both)]
+        in_specs=[rows_of(D, early), tall, rows_of(4 * D, always), rows_of(D, both)]
         + [rows_of(D, early)] * 3
-        + [pl.BlockSpec((1, 128, D), lambda i: (early(i), 0, 0)), tall]
-        + [once(doc_ids), once(small), once(w_all), anywhere, once(ffs)],
-        out_specs=[tall] + [anywhere] * 3 + [whole(16, D), whole(8, D)],
+        + [pl.BlockSpec((1, 128, D), lambda i: (twice(i), 0, 0)), tall]
+        + [once(doc_ids), once(small), once(w_all), anywhere, anywhere, once(ffs)],
+        out_specs=[tall] + [anywhere] * 5 + [whole(16, D), whole(8, D)],
         out_shape=[
             shape_of((rows, D), F32),
-            shape_of((4, part, 1152), F32),
-            shape_of((4, part, GROUP), F32),
-            shape_of((4, part, GROUP), F32),
+            shape_of((4, part, 640), F32),
+            shape_of((4, part, D), F32),
+            shape_of((4, part, 128), F32),
+            shape_of((4, part, 256), F32),
+            shape_of((4, part, 128), F32),
             shape_of((16, D), F32),
             shape_of((8, D), F32),
         ],
@@ -1162,12 +1302,18 @@
             vmem((136, D), F32),
             vmem((4, 128, D), link),
             vmem((4, 8, D), F32),
-            vmem((4, count, part, GROUP), link),
-            vmem((4, count, part, GROUP), link),
+            vmem((8, 128, D), BF16),
+            vmem((8, D), F32),
+            vmem((slabs, part, 128), link),
+            vmem((slabs, part, 256), link),
+            vmem((slabs, part, 128), link),
             vmem((8, D), F32),
         ]
-        + scatter_scratch(count, part, 1152, link, True)
-        + scatter_scratch(count, part, GROUP, link, False) * 2
+        + scatter_scratch(count, part, 640, link, OVER_X, True)
+        + scatter_scratch(count, part, D, link, OVER_Y, True)
+        + scatter_scratch(count, part, 128, link, OVER_X, False)
+        + scatter_scratch(count, part, 256, link, OVER_X, False)
+        + scatter_scratch(count, part, 128, link, SHORT, False)
         + small_scratch(count, 16)
         + small_scratch(count, 8)
         + [dma((3, 2)), dma((3, 2))],
@@ -1176,21 +1322,14 @@
         ),
         name="back",
     )(
-        tokens, tokens, qkvf, do, probs, score, inverse, kept, dy, doc_ids, small, w_all, ffg, ffs
+        tokens, tokens, qkvf, do, probs, score, inverse, kept, dy, doc_ids, small, w_all, ffg, ffr,
+        ffs,
     )
 
 
-def finish_kernel(count, part, ff_ref, g0_ref, g1_ref, s1_ref, s2_ref, *outs):
+def finish_kernel(count, part, gi_ref, ff_ref, fr_ref, q_ref, kv_ref, f_ref, s1_ref, s2_ref, gi_out, *outs):
     at = lax.axis_index("fsdp")
-    for n in range(4):
-        outs[n][:, 0:GROUP] = g0_ref[n]
-        outs[n][:, GROUP:D] = g1_ref[n]
-        outs[4][:, n * 128 : (n + 1) * 128] = ff_ref[n, :, 512:640]
-        outs[5][:, n * 512 : (n + 1) * 512] = ff_ref[n, :, 0:512]
-        for j in range(4):
-            outs[6][j * part : (j + 1) * part, n * 128 : (n + 1) * 128] = ff_ref[
-                n, :, 640 + j * 128 : 768 + j * 128
-            ]
+    gi_out[...] = gi_ref[...]
 
     def pick(row, size):
         out = row(0, size)
@@ -1205,27 +1344,40 @@
     def row_of_sums(ref, n):
         return lambda start, size: ref[n : n + 1, start : start + size]
 
-    outs[7][...] = pick(row_of_sums(s2_ref, 0), part)
-    outs[8][...] = pick(row_of_sums(s2_ref, 1), part)
-    outs[9][...] = pick(row_of_sums(s1_ref, 2), part)
-    outs[10][...] = pick(row_of_sums(s1_ref, 3), part)
-    outs[11][...] = pick(bias, 4 * part)
-    outs[12][...] = pick(row_of_sums(s1_ref, 4), part)
-
-
-def finish(count, part, ff, g0, g1, s1, s2):
-    once = lambda shape: pl.BlockSpec(shape, lambda: (0,) * len(shape))
+    @pl.when(pl.program_id(0) == 0)
+    def _():
+        for n in range(4):
+            lanes = slice(n * 128, (n + 1) * 128)
+            outs[0][:, lanes] = q_ref[n]
+            outs[1][:, lanes] = kv_ref[n, :, 0:128]
+            outs[2][:, lanes] = kv_ref[n, :, 128:256]
+            outs[3][:, lanes] = f_ref[n]
+            outs[4][:, lanes] = ff_ref[n, :, 512:640]
+            outs[5][:, n * 512 : (n + 1) * 512] = ff_ref[n, :, 0:512]
+            for j in range(4):
+                outs[6][j * part : (j + 1) * part, lanes] = fr_ref[n, :, j * 128 : (j + 1) * 128]
+        outs[7][...] = pick(row_of_sums(s2_ref, 0), part)
+        outs[8][...] = pick(row_of_sums(s2_ref, 1), part)
+        outs[9][...] = pick(row_of_sums(s1_ref, 2), part)
+        outs[10][...] = pick(row_of_sums(s1_ref, 3), part)
+        outs[11][...] = pick(bias, 4 * part)
+        outs[12][...] = pick(row_of_sums(s1_ref, 4), part)
+
+
+def finish(count, part, grad_input, *sums):
+    once = lambda shape: pl.BlockSpec(shape, lambda i: (0,) * len(shape))
+    tall = pl.BlockSpec((512, D), lambda i: (i, 0))
     shapes = [(part, D)] * 5 + [(part, FF), (4 * part, D)]
     shapes += [(1, part)] * 4 + [(1, 4 * part), (1, part)]
-    args = (ff, g0, g1, s1, s2)
     return pl.pallas_call(
         functools.partial(finish_kernel, count, part),
-        in_specs=[once(a.shape) for a in args],
-        out_specs=[once(s) for s in shapes],
-        out_shape=[shape_of(s, F32) for s in shapes],
+        grid=(grad_input.shape[0] // 512,),
+        in_specs=[tall] + [once(a.shape) for a in sums],
+        out_specs=[tall] + [once(s) for s in shapes],
+        out_shape=[shape_of(s, F32) for s in (grad_input.shape, *shapes)],
         compiler_params=PARAMS,
         name="finish",
-    )(*args)
+    )(grad_input, *sums)
 
 
 def rows_of(lanes, order=lambda i: i):
@@ -1266,17 +1418,20 @@
         a.reshape(-1, a.shape[2]).astype(BF16) for a in (w_qkvf, w_o, w_h, w_r)
     )
     tall = pl.BlockSpec((FEED_ROWS, D), lambda i: (i, 0))
-    out, grad_middle, grad_attended, pack, ff_small = pl.pallas_call(
+    half = count // 2
+    out, grad_middle, grad_attended, pack, pack_r, ff_small = pl.pallas_call(
         forward_kernel,
         grid=(rows // FEED_ROWS,),
         in_specs=[tall] * 3
         + [whole(8, D), whole(1, FF), whole(D, D), whole(D, FF), whole(FF, D)],
-        out_specs=[tall] * 3 + [whole(4, count, part, 1152), whole(16, D)],
+        out_specs=[tall] * 3
+        + [whole(2, 2, 2, half, part, 640), whole(2, 2, half, 2, part, D), whole(16, D)],
         out_shape=[
             shape_of((rows, D), BF16),
             shape_of((rows, D), F32),
             shape_of((rows, D), BF16),
-            shape_of((4, count, part, 1152), link),
+            shape_of((2, 2, 2, half, part, 640), link),
+            shape_of((2, 2, half, 2, part, D), link),
             shape_of((16, D), F32),
         ],
         scratch_shapes=[
@@ -1288,11 +1443,11 @@
         name="feed",
     )(tokens, attended, cotangent, small, bias, w_o, w_h, w_r)
 
-    grad_input, ff, g0, g1, s1, s2 = back(
+    grad_input, *sums = back(
         count, tokens, qkvf, grad_attended, probs, score, inverse, kept, grad_middle, doc_ids,
-        small, w_qkvf, pack, ff_small,
+        small, w_qkvf, pack.reshape(-1, part, 640), pack_r.reshape(-1, part, D), ff_small,
     )
-    grads = finish(count, part, ff, g0, g1, s1, s2)
+    grad_input, *grads = finish(count, part, grad_input, *sums)
     return (out, grad_input, *grads[:7], *(a.reshape(-1) for a in grads[7:]))
 
 

time: 275 us -> 236 us (0.86)
  Pallas kernels: 269 us -> 235 us
  local copies, waits for them, and re-layouts: 4.64 us -> 0 us
    pallas_call x1, Pallas kernels: 95.5 us -> 72.9 us  [front(): pl.pallas_call(functools.partial(front_kernel, count), grid=(17,), in_spe...]
    pallas_call x1, Pallas kernels: 124 us -> 110 us  [back(): pl.pallas_call(functools.partial(back_kernel, count, last), grid=(last +...]
    unnamed x1 -> x0, local copies, waits for them, and re-layouts: 4.64 us -> none
    pallas_call x1, Pallas kernels: 3.16 us -> 6.35 us  [finish(): pl.pallas_call(functools.partial(finish_kernel, count, part), grid=(grad_...]
where the time goes in v4:
time: 236 us
  Pallas kernels  235 us (100%)
    pallas_call x1, Pallas kernels, back(): pl.pallas_call(functools.partial(back_kernel, count, last), grid=(last +...  110 us
    pallas_call x1, Pallas kernels, front(): pl.pallas_call(functools.partial(front_kernel, count), grid=(17,), in_spe...  72.9 us
    pallas_call x1, Pallas kernels, on_device(): pl.pallas_call(forward_kernel, grid=(rows // FEED_ROWS,), in_specs=[tall]...  45.5 us
    pallas_call x1, Pallas kernels, finish(): pl.pallas_call(functools.partial(finish_kernel, count, part), grid=(grad_...  6.35 us

profile of v4, /device:TPU:0, one launch (start us, length us, event | category | flops | bytes accessed | tf_op | source)
XLA Modules:
  0.0 235.9 jit_solution(13031056405304431423)
XLA Ops:
  0.7 72.9 %front.1 = (bf16[2048,2048]{1,0:T(8,128)(2,1)}, bf16[2048,512]{1,0:T(8,128)(2,1)}, f32[2048,512]{1,0:T(8,128)}, f32[2048,512]{1,0:T(8,128)}, f32[2048,512]{1,0:T...) custom-call(bf16[2048,512]{1,0:T(8,128)(2,1)} %xs_ref.1, ...), custom_call_target="tpu_custom_call" | custom-call | tf_op jit(solution)/shard_map/front/pallas_call | solution.py:584
  73.5 45.5 %feed.1 = (bf16[2048,512]{1,0:T(8,128)(2,1)}, f32[2048,512]{1,0:T(8,128)}, bf16[2048,512]{1,0:T(8,128)(2,1)}, bf16[2,2,2,4,64,640]{5,4,3,2,1,0:T(8,128)(2,1)}, b...) custom-call(bf16[2048,512]{1,0:T(8,128)(2,1)} %xs_ref.1, bf16[2048,512]{1,0:T(8,128)(2,1)} %get-tuple-element.55.o_ref, ...), custom_call_target="tpu_custom_call" | custom-call | tf_op jit(solution)/shard_map/feed/pallas_call | solution.py:1422
  119.0 110.4 %back.1 = (f32[2048,512]{1,0:T(8,128)}, f32[4,64,640]{2,1,0:T(8,128)}, f32[4,64,512]{2,1,0:T(8,128)}, f32[4,64,128]{2,1,0:T(8,128)}, f32[4,64,256]{2,1,0:T(8,128...) custom-call(bf16[2048,512]{1,0:T(8,128)(2,1)} %xs_ref.1, bf16[2048,512]{1,0:T(8,128)(2,1)} %xs_ref.1, ...), custom_call_target="tpu_custom_call" | custom-call | tf_op jit(solution)/shard_map/back/pallas_call | solution.py:1275
  229.3 6.4 %finish.1 = (f32[2048,512]{1,0:T(8,128)}, f32[64,512]{1,0:T(8,128)}, f32[64,512]{1,0:T(8,128)}, f32[64,512]{1,0:T(8,128)}, f32[64,512]{1,0:T(8,128)}, /*index=5*...) custom-call(f32[2048,512]{1,0:T(8,128)} %get-tuple-element.73.gi_ref, ...), custom_call_target="tpu_custom_call" | custom-call | tf_op jit(solution)/shard_map/finish/pallas_call | solution.py:1372

commit v5 on v4

--- a/solution.py
+++ b/solution.py
@@ -18,7 +18,9 @@
 F32 = jnp.float32
 BF16 = jnp.bfloat16
 FEED_ROWS = 512
-LIMIT = 62 * 1024 * 1024
+FEED_LANES = 256
+FRONT = 4
+MIB = 1024 * 1024
 
 
 def dot(a, b):
@@ -149,6 +151,14 @@
         one.append(compacted(both[:, :GROUP]))
         two.append(compacted(both[:, GROUP:]))
     return jnp.concatenate(one, axis=1), jnp.concatenate(two, axis=1)
+
+
+def lanes_of(g):
+    return slice(g * GROUP, (g + 1) * GROUP)
+
+
+def part_of(ref, part, g):
+    return ref[:, part * D + g * GROUP : part * D + (g + 1) * GROUP]
 
 
 def attend_body(
@@ -164,34 +174,56 @@
     written = jnp.exp(qkvf_ref[:, 3 * D :].astype(F32))
     slots = written.astype(BF16)
     norm = dot(vis, slots)
-    for g in range(2):
-        lanes = slice(g * GROUP, (g + 1) * GROUP)
-        queries, keys, values = (
-            qkvf_ref[:, part * D + g * GROUP : part * D + (g + 1) * GROUP] for part in range(3)
-        )
-        here = slots[:, lanes]
-        affinity = masked(dot_nt(stacked(queries), keys), vis)
-        numer = select(dot(affinity, here))
-        numer = numer + carried * dot_nt(queries, expand(state[0:64, lanes]).astype(BF16))
-        total = norm[:, lanes] + carried * state[128:129, lanes]
-        inverse = 1.0 / total
-        score = numer * inverse * SCALE
-        grown = jnp.exp(score - head_max(score))
+    key_states = [expand(state[0:64, lanes_of(g)]).astype(BF16) for g in range(2)]
+    value_states = [expand(state[64:128, lanes_of(g)]).astype(BF16) for g in range(2)]
+    norm_state = state[128:129]
+
+    def affine(g):
+        return masked(dot_nt(stacked(part_of(qkvf_ref, 0, g)), part_of(qkvf_ref, 1, g)), vis)
+
+    def scores(g, affinity):
+        lanes = lanes_of(g)
+        numer = select(dot(affinity, slots[:, lanes]))
+        numer = numer + carried * dot_nt(part_of(qkvf_ref, 0, g), key_states[g])
+        inverse = 1.0 / (norm[:, lanes] + carried * norm_state[:, lanes])
+        return numer * inverse * SCALE, inverse
+
+    def grow(score):
+        return jnp.exp(score - head_max(score))
+
+    def read(g, score, inverse, grown):
+        lanes = lanes_of(g)
         probs = grown / head_sums(grown)
-        reading = (probs * inverse).astype(BF16)
-        mix = masked(dot_nt(stacked(reading), here), vis)
-        mixed = select(dot(mix, values))
-        mixed = mixed + carried * dot(reading, expand(state[64:128, lanes]).astype(BF16))
-        o_ref[:, lanes] = mixed.astype(BF16)
         p_ref[:, lanes] = probs
         s_ref[:, lanes] = score
         z_ref[:, lanes] = inverse
+        return (probs * inverse).astype(BF16)
+
+    def mixing(g, reading):
+        return masked(dot_nt(stacked(reading), slots[:, lanes_of(g)]), vis)
+
+    def mixed(g, reading, mix):
+        out = select(dot(mix, part_of(qkvf_ref, 2, g))) + carried * dot(reading, value_states[g])
+        o_ref[:, lanes_of(g)] = out.astype(BF16)
+
+    affinity = affine(0)
+    score, inverse = scores(0, affinity)
+    affinity = affine(1)
+    grown = grow(score)
+    score_two, inverse_two = scores(1, affinity)
+    reading = read(0, score, inverse, grown)
     tail = (wide(flag(col, newest), 4) * written).astype(BF16)
     new_keys, new_values = state_terms(tail, qkvf_ref[:, D : 2 * D], qkvf_ref[:, 2 * D : 3 * D])
     same = jnp.where(last == newest, 1.0, 0.0)
     state[0:64] = same * state[0:64] + new_keys
     state[64:128] = same * state[64:128] + new_values
     state[128:129] = same * state[128:129] + jnp.sum(tail.astype(F32), axis=0, keepdims=True)
+    grown = grow(score_two)
+    mix = mixing(0, reading)
+    reading_two = read(1, score_two, inverse_two, grown)
+    mixed(0, reading, mix)
+    mix = mixing(1, reading_two)
+    mixed(1, reading_two, mix)
 
 
 MESH_ID = pl.DeviceIdType.MESH
@@ -475,19 +507,25 @@
             for k in range(1, count):
                 small_copy(k, at ^ k).wait_recv()
             join_small(count, v0.shape[1], smalls, vec_out, bias_out)
-            for piece in later:
-                piece.start()
+            q_piece.start()
+            o_piece.start()
+
+            @pl.loop(0, 8)
+            def _(n):
+                here = pl.ds(pl.multiple_of(n * C, C), C)
+                unit, _ = norm_parts(x_ref[here].astype(F32))
+                hidden[here] = (unit * vec_out[0:1] + vec_out[1:2]).astype(BF16)
 
         main.at_once(between)
-
-    @pl.when(step < 8)
+        h_piece.start()
+        r_piece.start()
+
+    @pl.when(step < FRONT)
     def _():
-        unit, _ = norm_parts(x_ref[...].astype(F32))
-        normed = (unit * vec_out[0:1] + vec_out[1:2]).astype(BF16)
-        here = pl.ds(pl.multiple_of(step * C, C), C)
-        hidden[here] = normed
+        size = 8 // FRONT * C
+        here = pl.ds(pl.multiple_of(step * size, size), size)
         weights = w_all[:, :, D:].reshape(D, 3 * D).astype(BF16)
-        rows = dot(normed, weights).astype(BF16)
+        rows = dot(hidden[here], weights).astype(BF16)
         qkvf[here, D:] = rows
         slots = wide(flag(col_ref[here], edge_ref[15:16]), 4) * jnp.exp(rows[:, 2 * D :].astype(F32))
         slots = slots.astype(BF16)
@@ -501,36 +539,26 @@
         q_piece.second()
         o_piece.second()
 
-    @pl.when(step == 4)
-    def _():
-        q_piece.third()
-        o_piece.third()
-        h_piece.second()
-
-    @pl.when(step == 6)
-    def _():
-        o_piece.fourth()
-
-    @pl.when(step == 7)
+    @pl.when(step == FRONT - 1)
     def _():
         tails[seq] = tail[0:128].astype(link)
         tail_rows[seq, 0:1] = tail[128:129]
         tail_rows[seq, 1:2] = edge_ref[15:16]
         tail_rows[seq, 2:8] = jnp.zeros((6, D), F32)
         states.start()
-
-    @pl.when(step == 8)
-    def _():
+        q_piece.third()
         q_piece.finish()
 
-        @pl.loop(0, 8)
+        @pl.loop(0, FRONT)
         def _(n):
-            here = pl.ds(pl.multiple_of(n * C, C), C)
+            size = 8 // FRONT * C
+            here = pl.ds(pl.multiple_of(n * size, size), size)
             weights = w_all[:, :, 0:D].reshape(D, D).astype(BF16)
             qkvf[here, 0:D] = dot(hidden[here], weights).astype(BF16)
 
         for copy in save():
             copy.start()
+        o_piece.third()
         states.finish()
         first = edge_ref[0:1]
         state[...] = jnp.zeros_like(state)
@@ -538,27 +566,39 @@
             use = jnp.where(tail_rows[n, 1:2] == first, 1.0, 0.0) * (n < seq).astype(F32)
             state[0:128] += use * tails[n].astype(F32)
             state[128:129] += use * tail_rows[n, 0:1]
-
-    @pl.when(step == 9)
-    def _():
-        h_piece.third()
-        r_piece.second()
-
-    @pl.when(step == 13)
-    def _():
-        r_piece.third()
-        h_piece.fourth()
-
-    @pl.when(step >= 9)
-    def _():
-        n = step - 9
-        here = pl.ds(pl.multiple_of(n * C, C), C)
-        attend_body(
-            n, qkvf.at[here], col_ref[here], doc_ref[:, here].astype(F32), edge_ref,
-            state, o_ref, p_ref, s_ref, z_ref, kept_ref,
-        )
-
-    @pl.when(step == 16)
+        h_piece.second()
+
+    per = 8 // FRONT
+    for u in range(per):
+
+        @pl.when(step >= FRONT)
+        def _(u=u):
+            n = (step - FRONT) * per + u
+            here = pl.ds(pl.multiple_of(n * C, C), C)
+            block = pl.ds(u * C, C)
+            attend_body(
+                n, qkvf.at[here], col_ref[here], doc_ref[:, here].astype(F32), edge_ref, state,
+                o_ref.at[block], p_ref.at[block], s_ref.at[block], z_ref.at[block],
+                kept_ref.at[pl.ds(u, 1)],
+            )
+
+        if u == 0:
+
+            @pl.when(step == FRONT)
+            def _():
+                o_piece.fourth()
+
+            @pl.when(step == FRONT + 1)
+            def _():
+                r_piece.second()
+                h_piece.third()
+
+            @pl.when(step == FRONT + 3)
+            def _():
+                r_piece.third()
+                h_piece.fourth()
+
+    @pl.when(step == 2 * FRONT - 1)
     def _():
         for piece in (o_piece, h_piece, r_piece):
             piece.finish()
@@ -577,17 +617,18 @@
     part = weights[0].shape[0]
     link = BF16 if part % 16 == 0 else F32
     once = lambda a: pl.BlockSpec(a.shape, lambda i: (0,) * a.ndim)
-    early = lambda i: jnp.minimum(i, 7)
-    late = lambda i: jnp.maximum(i - 9, 0)
+    late = lambda i: jnp.maximum(i - FRONT, 0)
+    per = 8 // FRONT
+    tall = pl.BlockSpec((per * C, D), lambda i: (late(i), 0))
     anywhere = pl.BlockSpec(memory_space=pl.ANY)
     vmem = pltpu.VMEM
     return pl.pallas_call(
         functools.partial(front_kernel, count),
-        grid=(17,),
-        in_specs=[rows_of(D, early), once(doc_ids)] + [once(a) for a in (*weights, *vectors, bias)],
+        grid=(2 * FRONT,),
+        in_specs=[once(tokens), once(doc_ids)] + [once(a) for a in (*weights, *vectors, bias)],
         out_specs=[anywhere]
-        + [rows_of(D, late)] * 4
-        + [pl.BlockSpec((1, 128, D), lambda i: (late(i), 0, 0))]
+        + [tall] * 4
+        + [pl.BlockSpec((per, 128, D), lambda i: (late(i), 0, 0))]
         + [anywhere] * 4
         + [whole(8, D), whole(1, FF)],
         out_shape=[shape_of((rows, 4 * D), BF16), shape_of((rows, D), BF16)]
@@ -628,7 +669,7 @@
             pltpu.SemaphoreType.DMA((2,)),
         ],
         compiler_params=pltpu.CompilerParams(
-            vmem_limit_bytes=LIMIT, collective_id=1, has_side_effects=True
+            vmem_limit_bytes=62 * MIB, collective_id=1, has_side_effects=True
         ),
         name="front",
     )(tokens, doc_ids, *weights, *vectors, bias)
@@ -664,18 +705,34 @@
     out = middle + small_ref[4:5]
     grad_hidden = jnp.zeros((x_ref.shape[0], D), F32)
     cot32 = cot.astype(F32)
-    for j in range(4):
-        cols = slice(j * 512, (j + 1) * 512)
+    tiles = FF // FEED_LANES
+
+    def into(j):
+        cols = slice(j * FEED_LANES, (j + 1) * FEED_LANES)
         inner = dot(hidden, wh_ref[:, cols]) + bias_ref[0:1, cols]
+        return inner, dot_nt(cot, wr_ref[cols, :])
+
+    def bend(inner, grad):
         gated, slope = gelu_both(inner)
-        active = gated.astype(BF16)
-        out = out + dot(active, wr_ref[cols, :])
+        return gated.astype(BF16), (grad * slope).astype(BF16)
+
+    def outof(j, active, low):
+        cols = slice(j * FEED_LANES, (j + 1) * FEED_LANES)
+        there = slice(cols.start % D, cols.start % D + FEED_LANES)
+        row = 8 + cols.start // D
         gwr_ref[:, cols] += dot_tn(cot, active)
-        grad = dot_nt(cot, wr_ref[cols, :]) * slope
-        low = grad.astype(BF16)
-        gsmall_ref[8 + j : 9 + j] += jnp.sum(low.astype(F32), axis=0, keepdims=True)
+        gsmall_ref[row : row + 1, there] += jnp.sum(low.astype(F32), axis=0, keepdims=True)
         gwh_ref[:, cols] += dot_tn(hidden, low)
-        grad_hidden = grad_hidden + dot_nt(low, wh_ref[:, cols])
+        return dot(active, wr_ref[cols, :]), dot_nt(low, wh_ref[:, cols])
+
+    coming = into(0)
+    for j in range(tiles):
+        bent = bend(*coming)
+        if j + 1 < tiles:
+            coming = into(j + 1)
+        to_out, to_hidden = outof(j, *bent)
+        out = out + to_out
+        grad_hidden = grad_hidden + to_hidden
     y_ref[...] = out.astype(BF16)
     gsmall_ref[2:3] += jnp.sum(grad_hidden * unit, axis=0, keepdims=True)
     gsmall_ref[3:4] += jnp.sum(grad_hidden, axis=0, keepdims=True)
@@ -704,7 +761,7 @@
 
 def row_body(
     n, qkvf_ref, do_ref, p_ref, s_ref, z_ref, kept_ref, col, row, edge_ref,
-    r_ref, dn_ref, dz_ref, head_ref,
+    r_ref, dn_ref, dz_ref, head_ref, aside,
 ):
     first = edge_ref[pl.ds(0, 1)]
     before = edge_ref[pl.ds(8 + jnp.maximum(n - 1, 0), 1)]
@@ -712,21 +769,21 @@
     vis = visible(col, row)
     carried = wide(flag(col, last), 2)
     slots = jnp.exp(qkvf_ref[:, 3 * D :].astype(F32)).astype(BF16)
-    own = wide(flag(col, first), 4)
-    for g in range(2):
-        lanes = slice(g * GROUP, (g + 1) * GROUP)
-        queries, values = (
-            qkvf_ref[:, part * D + g * GROUP : part * D + (g + 1) * GROUP] for part in (0, 2)
-        )
-        here, grads = slots[:, lanes], do_ref[:, lanes]
+    own = wide(flag(col, first), 2)
+    states = [expand(kept_ref[0, 64:128, lanes_of(g)]).astype(BF16) for g in range(2)]
+
+    def mixing(g):
+        return masked(dot_nt(stacked(do_ref[:, lanes_of(g)]), part_of(qkvf_ref, 2, g)), vis)
+
+    def to_reading(g, back_mix):
+        lanes = lanes_of(g)
+        back = select(dot(back_mix, slots[:, lanes]))
+        return back + carried * dot_nt(do_ref[:, lanes], states[g])
+
+    def to_scores(g, back_reading):
+        lanes = lanes_of(g)
         probs, score, inverse = p_ref[:, lanes], s_ref[:, lanes], z_ref[:, lanes]
-        back_mix = masked(dot_nt(stacked(grads), values), vis)
-        back_reading = select(dot(back_mix, here))
-        back_reading = back_reading + carried * dot_nt(
-            grads, expand(kept_ref[0, 64:128, lanes]).astype(BF16)
-        )
-        back_probs = back_reading * inverse
-        shared = back_probs * probs
+        shared = back_reading * inverse * probs
         back_score = shared - probs * head_sums(shared)
         back_numer = back_score * inverse * SCALE
         back_total = -(shared + back_score * score) * inverse
@@ -734,12 +791,27 @@
         r_ref[:, lanes] = reading
         dn_ref[:, lanes] = back_numer
         dz_ref[:, lanes] = back_total
-        mine = own[:, lanes]
-        head_ref[0:64, lanes] += compacted(dot_tn((mine * back_numer).astype(BF16), queries))
+        return back_numer, back_total, reading
+
+    def to_state(g, back_numer, back_total, reading):
+        lanes = lanes_of(g)
+        head_ref[0:64, lanes] += compacted(
+            dot_tn((own * back_numer).astype(BF16), part_of(qkvf_ref, 0, g))
+        )
         head_ref[64:128, lanes] += compacted(
-            dot_tn((mine * reading.astype(F32)).astype(BF16), grads)
+            dot_tn((own * reading.astype(F32)).astype(BF16), do_ref[:, lanes])
         )
-        head_ref[128:129, lanes] += jnp.sum(mine * back_total, axis=0, keepdims=True)
+        head_ref[128:129, lanes] += jnp.sum(own * back_total, axis=0, keepdims=True)
+
+    back_mix = mixing(0)
+    back_mix_two = mixing(1)
+    aside()
+    back_reading = to_reading(0, back_mix)
+    back_reading_two = to_reading(1, back_mix_two)
+    parts = to_scores(0, back_reading)
+    to_state(0, *parts)
+    parts = to_scores(1, back_reading_two)
+    to_state(1, *parts)
 
 
 def query_body(n, qkvf_ref, kept_ref, col, row, edge_ref, dn_ref, dq_ref):
@@ -749,16 +821,19 @@
     vis = visible(col, row)
     carried = wide(flag(col, last), 2)
     slots = jnp.exp(qkvf_ref[:, 3 * D :].astype(F32)).astype(BF16)
-    for g in range(2):
-        lanes = slice(g * GROUP, (g + 1) * GROUP)
-        keys = qkvf_ref[:, D + g * GROUP : D + (g + 1) * GROUP]
-        low = dn_ref[:, lanes].astype(BF16)
-        back_affinity = masked(dot_nt(stacked(low), slots[:, lanes]), vis)
-        back_queries = select(dot(back_affinity, keys))
-        back_queries = back_queries + carried * dot(
-            low, expand(kept_ref[0, 0:64, lanes]).astype(BF16)
-        )
-        dq_ref[:, lanes] = back_queries.astype(BF16)
+    lows = [dn_ref[:, lanes_of(g)].astype(BF16) for g in range(2)]
+    states = [expand(kept_ref[0, 0:64, lanes_of(g)]).astype(BF16) for g in range(2)]
+
+    def affine(g):
+        return masked(dot_nt(stacked(lows[g]), slots[:, lanes_of(g)]), vis)
+
+    def to_queries(g, back_affinity):
+        out = select(dot(back_affinity, part_of(qkvf_ref, 1, g))) + carried * dot(lows[g], states[g])
+        dq_ref[:, lanes_of(g)] = out.astype(BF16)
+
+    one, two = affine(0), affine(1)
+    to_queries(0, one)
+    to_queries(1, two)
 
 
 def column_body(
@@ -774,30 +849,52 @@
     kept = jnp.where(following == first, 1.0, 0.0)[:, :GROUP]
     snap[n] = state[0:128].astype(BF16)
     snap_rows[pl.ds(n, 1)] = state[128:129]
-    for g in range(2):
-        lanes = slice(g * GROUP, (g + 1) * GROUP)
-        queries = qkvf_ref[:, lanes]
-        here = jnp.exp(qkvf_ref[:, 3 * D + g * GROUP : 3 * D + (g + 1) * GROUP].astype(F32))
-        here = here.astype(BF16)
-        grads, reading, back_numer = do_ref[:, lanes], r_ref[:, lanes], dn_ref[:, lanes]
-        key_state = expand(state[0:64, lanes]).astype(BF16)
-        value_state = expand(state[64:128, lanes]).astype(BF16)
-        apart = stacked(here)
-        mix = masked(dot_nt(apart, reading), vis)
-        back_values = select(dot(mix, grads)) + carried * dot(here, value_state)
-        d_ref[:, 2 * D + g * GROUP : 2 * D + (g + 1) * GROUP] = back_values.astype(BF16)
-        back_affinity = masked(dot_nt(apart, back_numer.astype(BF16)), vis)
-        back_keys = select(dot(back_affinity, queries)) + carried * dot(here, key_state)
-        d_ref[:, D + g * GROUP : D + (g + 1) * GROUP] = back_keys.astype(BF16)
+    key_states = [expand(state[0:64, lanes_of(g)]).astype(BF16) for g in range(2)]
+    value_states = [expand(state[64:128, lanes_of(g)]).astype(BF16) for g in range(2)]
+    slots = jnp.exp(qkvf_ref[:, 3 * D :].astype(F32)).astype(BF16)
+    numers = [dn_ref[:, lanes_of(g)] for g in range(2)]
+
+    def mixing(g, apart):
+        return masked(dot_nt(apart, r_ref[:, lanes_of(g)]), vis)
+
+    def affine(g, apart):
+        return masked(dot_nt(apart, numers[g].astype(BF16)), vis)
+
+    def to_values(g, mix):
+        lanes = lanes_of(g)
+        out = select(dot(mix, do_ref[:, lanes])) + carried * dot(slots[:, lanes], value_states[g])
+        d_ref[:, 2 * D + g * GROUP : 2 * D + (g + 1) * GROUP] = out.astype(BF16)
+
+    def to_keys(g, back_affinity):
+        lanes = lanes_of(g)
+        out = select(dot(back_affinity, part_of(qkvf_ref, 0, g)))
+        out = out + carried * dot(slots[:, lanes], key_states[g])
+        d_ref[:, D + g * GROUP : D + (g + 1) * GROUP] = out.astype(BF16)
+
+    def to_state(g):
+        lanes = lanes_of(g)
         state[0:64, lanes] = kept * state[0:64, lanes] + compacted(
-            dot_tn((own * back_numer).astype(BF16), queries)
+            dot_tn((own * numers[g]).astype(BF16), part_of(qkvf_ref, 0, g))
         )
         state[64:128, lanes] = kept * state[64:128, lanes] + compacted(
-            dot_tn((own * reading.astype(F32)).astype(BF16), grads)
+            dot_tn((own * r_ref[:, lanes].astype(F32)).astype(BF16), do_ref[:, lanes])
         )
         state[128:129, lanes] = kept * state[128:129, lanes] + jnp.sum(
             own * dz_ref[:, lanes], axis=0, keepdims=True
         )
+
+    apart = stacked(slots[:, lanes_of(0)])
+    mix = mixing(0, apart)
+    back_affinity = affine(0, apart)
+    apart = stacked(slots[:, lanes_of(1)])
+    mix_two = mixing(1, apart)
+    to_values(0, mix)
+    affinity_two = affine(1, apart)
+    to_keys(0, back_affinity)
+    to_state(0)
+    to_values(1, mix_two)
+    to_keys(1, affinity_two)
+    to_state(1)
 
 
 def slot_body(n, qkvf_ref, do_ref, r_ref, dn_ref, dz_ref, col, row, edge_ref, snap, snap_rows, d_ref):
@@ -807,37 +904,58 @@
     vis = visible_back(col, row)
     carried = wide(flag(col, following), 2)
     left = lane_heads(C, 128) == 0
-    total_high, total_low = split(dz_ref[...])
-    back_norm = dot(vis, total_high) + dot(vis, total_low)
     norm_state = snap_rows[pl.ds(n, 1)]
-    for g in range(2):
-        lanes = slice(g * GROUP, (g + 1) * GROUP)
-        queries, keys, values, logits = (
-            qkvf_ref[:, part * D + g * GROUP : part * D + (g + 1) * GROUP] for part in range(4)
-        )
-        grads, reading = do_ref[:, lanes], r_ref[:, lanes]
-        numer_high, numer_low = split(dn_ref[:, lanes])
-        key_state = expand(snap[n, 0:64, lanes])
-        value_state = expand(snap[n, 64:128, lanes])
-        back_mix = masked(dot_nt(stacked(values), grads), vis)
-        back_slots = back_norm[:, lanes] + select(dot(back_mix, reading))
-        affinity = masked(dot_nt(stacked(keys), queries), vis)
+    key_states = [expand(snap[n, 0:64, lanes_of(g)]) for g in range(2)]
+    value_states = [expand(snap[n, 64:128, lanes_of(g)]) for g in range(2)]
+
+    def mixing(g):
+        return masked(dot_nt(stacked(part_of(qkvf_ref, 2, g)), do_ref[:, lanes_of(g)]), vis)
+
+    def affine(g):
+        return masked(dot_nt(stacked(part_of(qkvf_ref, 1, g)), part_of(qkvf_ref, 0, g)), vis)
+
+    def from_mix(g, back_mix):
+        return select(dot(back_mix, r_ref[:, lanes_of(g)]))
+
+    def from_affinity(g, affinity):
+        high, low = split(dn_ref[:, lanes_of(g)])
         parts = []
         for p in range(2):
             pair = slice(p * 128, (p + 1) * 128)
             both = dot(
                 affinity[p * 512 : (p + 1) * 512],
-                jnp.concatenate([numer_high[:, pair], numer_low[:, pair]], axis=1),
+                jnp.concatenate([high[:, pair], low[:, pair]], axis=1),
             )
             both = both[:, :128] + both[:, 128:]
             parts.append(jnp.where(left, both[:C], both[C:]))
-        back_slots = back_slots + jnp.concatenate(parts, axis=1)
-        back_slots = back_slots + carried * (
-            dot_nt(keys, key_state) + dot_nt(values, value_state) + norm_state[:, lanes]
+        return jnp.concatenate(parts, axis=1)
+
+    def from_totals():
+        high, low = split(dz_ref[...])
+        return dot(vis, high) + dot(vis, low)
+
+    def from_state(g):
+        return carried * (
+            dot_nt(part_of(qkvf_ref, 1, g), key_states[g])
+            + dot_nt(part_of(qkvf_ref, 2, g), value_states[g])
+            + norm_state[:, lanes_of(g)]
         )
-        d_ref[:, 3 * D + g * GROUP : 3 * D + (g + 1) * GROUP] = (
-            back_slots * jnp.exp(logits.astype(F32))
-        ).astype(BF16)
+
+    def to_slots(g, back_slots):
+        written = jnp.exp(part_of(qkvf_ref, 3, g).astype(F32))
+        d_ref[:, 3 * D + g * GROUP : 3 * D + (g + 1) * GROUP] = (back_slots * written).astype(BF16)
+
+    norm = from_totals()
+    mix = mixing(0)
+    affinity = affine(0)
+    mix_two = mixing(1)
+    total = from_mix(0, mix)
+    affinity_two = affine(1)
+    total = total + from_affinity(0, affinity)
+    total_two = from_mix(1, mix_two)
+    to_slots(0, total + norm[:, lanes_of(0)] + from_state(0))
+    total_two = total_two + from_affinity(1, affinity_two)
+    to_slots(1, total_two + norm[:, lanes_of(1)] + from_state(1))
 
 
 class Scatter:
@@ -1029,16 +1147,15 @@
     ]
 
 
-FIRST_QUERY, TURN = 8, 16
-FIRST_COLUMN, FIRST_SLOT, FIRST_INPUT = 17, 25, 33
+QUERY, COLUMN, SLOT, INPUT = 8, 16, 24, 32
 
 
 def back_kernel(
-    count, last_step, x_ref, xs_ref, qkvf_ref, do_ref, p_ref, s_ref, z_ref, kept_ref, dy_ref, doc_ref,
+    count, per, x_ref, xs_ref, qkvf_ref, do_ref, p_ref, s_ref, z_ref, kept_ref, dy_ref, doc_ref,
     small_ref, w_ref, ffg_ref, ffr_ref, ffs_ref,
     gi_ref, ff_out, fr_out, q_out, kv_out, f_out, s1_out, s2_out,
     d_all, h_turned, reading, numer, total, col_ref, edge_ref, head, state, heads, head_rows,
-    snap, snap_rows, q_piece, kv_piece, f_piece, last_small, *rest,
+    snap, snap_rows, w_held, w_sem, q_piece, kv_piece, f_piece, last_small, *rest,
 ):
     step = pl.program_id(0)
     seq, at, _, _ = places()
@@ -1060,11 +1177,15 @@
     small_two = SmallSum(count, last_small, *take(3), take(2))
     states = States(heads, head_rows, take(2))
 
-    def chunk(first, turned=False):
-        n = step - first
+    def chunk(u, first, turned=False):
+        n = step * per + u - first
         n = 7 - n if turned else n
         here = pl.ds(pl.multiple_of(n * C, C), C)
-        return n, here, col_ref[here], doc_ref[:, here].astype(F32)
+        block = pl.ds((per - 1 - u if turned else u) * C, C)
+        return n, here, block, col_ref[here], doc_ref[:, here].astype(F32)
+
+    def fetch():
+        return pltpu.make_async_copy(w_ref, w_held, w_sem)
 
     def weight_grad(piece, d_lanes, lanes, short=False):
         grad = dot(h_turned[...], d_all[:, d_lanes])
@@ -1083,56 +1204,14 @@
     @pl.when(step == 0)
     def _():
         greet(count)
+        fetch().start()
         ff.start()
-        fr.start()
         small_one.start()
         doc_parts(doc_ref, col_ref, edge_ref)
         head[...] = jnp.zeros_like(head)
         last_small[...] = jnp.zeros_like(last_small)
 
-    @pl.when(step < FIRST_QUERY)
-    def _():
-        n, here, col, row = chunk(0)
-        unit, _ = norm_parts(x_ref[...].astype(F32))
-        h_turned[:, here] = (unit * small_ref[0:1] + small_ref[1:2]).astype(BF16).T
-        row_body(
-            n, qkvf_ref, do_ref, p_ref, s_ref, z_ref, kept_ref, col, row, edge_ref,
-            reading.at[here], numer.at[here], total.at[here], head,
-        )
-
-    @pl.when(step == 3)
-    def _():
-        ff.advance(0)
-        fr.advance(0)
-        small_one.second()
-
-    @pl.when(step == 6)
-    def _():
-        small_one.finish(s1_out)
-
-    @pl.when(step == FIRST_QUERY - 1)
-    def _():
-        heads[seq] = head[0:128].astype(link)
-        head_rows[seq, 0:1] = head[128:129]
-        head_rows[seq, 1:2] = edge_ref[0:1]
-        head_rows[seq, 2:8] = jnp.zeros((6, D), F32)
-        states.start()
-
-    @pl.when((step >= FIRST_QUERY) & (step < TURN))
-    def _():
-        n, here, col, row = chunk(FIRST_QUERY)
-        query_body(n, qkvf_ref, kept_ref, col, row, edge_ref, numer.at[here], d_all.at[here, 0:D])
-
-    @pl.when(step == FIRST_QUERY + 1)
-    def _():
-        fr.advance(1)
-
-    @pl.when(step == FIRST_QUERY + 4)
-    def _():
-        ff.advance(1)
-
-    @pl.when(step == TURN)
-    def _():
+    def turn():
         weight_grad(q_piece, slice(0, D), slice(0, 128))
         for_q.start()
         states.finish()
@@ -1143,105 +1222,120 @@
             state[0:128] += use * heads[n].astype(F32)
             state[128:129] += use * head_rows[n, 0:1]
 
-    @pl.when((step >= FIRST_COLUMN) & (step < FIRST_SLOT))
-    def _():
-        n, here, col, row = chunk(FIRST_COLUMN, True)
-        column_body(
-            n, qkvf_ref, do_ref, reading.at[here], numer.at[here], total.at[here], col, row, edge_ref,
-            state, snap, snap_rows, d_all.at[here],
-        )
-
-    @pl.when(step == FIRST_COLUMN)
-    def _():
-        ff.advance(2)
-        for_q.advance(0)
-
-    @pl.when(step == FIRST_COLUMN + 1)
-    def _():
-        fr.advance(2)
-
-    @pl.when(step == FIRST_COLUMN + 2)
-    def _():
-        for_q.advance(1)
-
-    @pl.when(step == FIRST_COLUMN + 4)
-    def _():
-        fr.advance(3)
-        for_q.advance(2)
-
-    @pl.when(step == FIRST_COLUMN + 5)
-    def _():
-        ff.advance(3)
-
-    @pl.when(step == FIRST_COLUMN + 6)
-    def _():
-        for_q.advance(3)
-        fr.forward()
-
-    @pl.when(step == FIRST_COLUMN + 7)
-    def _():
+    def send_states():
+        heads[seq] = head[0:128].astype(link)
+        head_rows[seq, 0:1] = head[128:129]
+        head_rows[seq, 1:2] = edge_ref[0:1]
+        head_rows[seq, 2:8] = jnp.zeros((6, D), F32)
+        states.start()
+
+    def key_value_grads():
         weight_grad(kv_piece, slice(D, 2 * D), slice(0, 128))
         weight_grad(kv_piece, slice(2 * D, 3 * D), slice(128, 256))
         for_kv.start()
-        ff.forward()
-
-    @pl.when((step >= FIRST_SLOT) & (step < FIRST_INPUT))
-    def _():
-        n, here, col, row = chunk(FIRST_SLOT, True)
-        slot_body(
-            n, qkvf_ref, do_ref, reading.at[here], numer.at[here], total.at[here], col, row, edge_ref,
-            snap, snap_rows, d_all.at[here],
-        )
-
-    @pl.when(step == FIRST_SLOT)
-    def _():
-        for_kv.advance(0)
-        for_q.forward()
-
-    @pl.when(step == FIRST_SLOT + 3)
-    def _():
-        for_kv.advance(1)
-
-    @pl.when(step == FIRST_SLOT + 5)
-    def _():
-        for_kv.advance(2)
-
-    @pl.when(step == FIRST_SLOT + 7)
-    def _():
+
+    def slot_grads():
         weight_grad(f_piece, slice(3 * D, 4 * D), slice(0, 128), True)
         for_f.start()
-        for_kv.advance(3)
-
-    @pl.when(step >= FIRST_INPUT)
-    def _():
-        n = step - FIRST_INPUT
-        size = xs_ref.shape[0]
-        here = pl.ds(pl.multiple_of(n * size, size), size)
-        grad = dot_nt(d_all[here], w_ref[...])
-        unit, scale = norm_parts(xs_ref[...].astype(F32))
-        last_small[0:1] += jnp.sum(grad * unit, axis=0, keepdims=True)
-        last_small[1:2] += jnp.sum(grad, axis=0, keepdims=True)
-        gi_ref[...] = dy_ref[...] + norm_back(unit, scale, small_ref[0:1], grad)
-
-    @pl.when(step == FIRST_INPUT)
-    def _():
-        for_f.advance(0)
+
+    def last():
+        small_two.start()
+        for_f.advance(2)
+        small_two.second()
         for_kv.forward()
-
-    @pl.when(step == last_step - 1)
-    def _():
-        for_f.advance(1)
-
-    @pl.when(step == last_step)
-    def _():
-        small_two.start()
-        for piece in (ff, fr, for_q, for_kv):
+        for piece in (ff, fr, for_q):
             piece.finish()
         states.drain()
-        small_two.second()
-        for_f.advance(2)
         small_two.finish(s2_out)
+        for_kv.finish()
         for_f.finish()
+
+    schedule = {
+        0: [fr.start],
+        2: [lambda: ff.advance(0), small_one.second],
+        4: [lambda: fr.advance(0)],
+        QUERY - 1: [send_states],
+        QUERY + 7: [turn],
+        COLUMN: [lambda: ff.advance(1)],
+        COLUMN + 1: [lambda: fr.advance(1), lambda: for_q.advance(0)],
+        COLUMN + 4: [lambda: for_q.advance(1)],
+        COLUMN + 5: [lambda: ff.advance(2)],
+        COLUMN + 7: [key_value_grads, lambda: for_q.advance(2)],
+        SLOT: [lambda: fr.advance(2)],
+        SLOT + 1: [lambda: for_kv.advance(0)],
+        SLOT + 2: [lambda: ff.advance(3)],
+        SLOT + 4: [lambda: fr.advance(3), lambda: for_q.advance(3)],
+        SLOT + 6: [lambda: for_kv.advance(1)],
+        SLOT + 7: [slot_grads],
+        INPUT + 1: [lambda: for_f.advance(0), lambda: for_kv.advance(2)],
+        INPUT + 3: [ff.forward, for_q.forward, fr.forward, lambda: small_one.finish(s1_out)],
+        INPUT + 5: [lambda: for_f.advance(1), lambda: for_kv.advance(3)],
+        INPUT + 7: [last],
+    }
+
+    for u in range(per):
+
+        @pl.when(step < QUERY // per)
+        def _(u=u):
+            n, here, block, col, row = chunk(u, 0)
+
+            def aside():
+                unit, _ = norm_parts(x_ref[block].astype(F32))
+                h_turned[:, here] = (unit * small_ref[0:1] + small_ref[1:2]).astype(BF16).T
+
+            row_body(
+                n, qkvf_ref.at[block], do_ref.at[block], p_ref.at[block], s_ref.at[block],
+                z_ref.at[block], kept_ref.at[pl.ds(u, 1)], col, row, edge_ref,
+                reading.at[here], numer.at[here], total.at[here], head, aside,
+            )
+
+        @pl.when((step >= QUERY // per) & (step < COLUMN // per))
+        def _(u=u):
+            n, here, block, col, row = chunk(u, QUERY)
+            query_body(
+                n, qkvf_ref.at[block], kept_ref.at[pl.ds(u, 1)], col, row, edge_ref,
+                numer.at[here], d_all.at[here, 0:D],
+            )
+
+        @pl.when((step >= COLUMN // per) & (step < SLOT // per))
+        def _(u=u):
+            n, here, block, col, row = chunk(u, COLUMN, True)
+            column_body(
+                n, qkvf_ref.at[block], do_ref.at[block], reading.at[here], numer.at[here],
+                total.at[here], col, row, edge_ref, state, snap, snap_rows, d_all.at[here],
+            )
+
+        @pl.when((step >= SLOT // per) & (step < INPUT // per))
+        def _(u=u):
+            n, here, block, col, row = chunk(u, SLOT, True)
+            slot_body(
+                n, qkvf_ref.at[block], do_ref.at[block], reading.at[here], numer.at[here],
+                total.at[here], col, row, edge_ref, snap, snap_rows, d_all.at[here],
+            )
+
+        if u == 0:
+
+            @pl.when(step == INPUT // per)
+            def _():
+                fetch().wait()
+
+            @pl.when(step >= INPUT // per)
+            def _():
+                size = xs_ref.shape[0]
+                here = pl.ds(pl.multiple_of((step - INPUT // per) * size, size), size)
+                grad = dot_nt(d_all[here], w_held[...])
+                unit, scale = norm_parts(xs_ref[...].astype(F32))
+                last_small[0:1] += jnp.sum(grad * unit, axis=0, keepdims=True)
+                last_small[1:2] += jnp.sum(grad, axis=0, keepdims=True)
+                gi_ref[...] = dy_ref[...] + norm_back(unit, scale, small_ref[0:1], grad)
+
+        for when, actions in schedule.items():
+            if when % per == u:
+
+                @pl.when(step == when // per)
+                def _(actions=actions):
+                    for action in actions:
+                        action()
 
 
 def back(
@@ -1249,36 +1343,39 @@
 ):
     rows = tokens.shape[0]
     part, link = ffg.shape[1], ffg.dtype
-    size = 512 if link == BF16 else 256
-    last = FIRST_INPUT + rows // size - 1
+    per = 2 if link == BF16 else 1
+    size = per * C
+    blocks = 8 // per
     once = lambda a: pl.BlockSpec(a.shape, lambda i: (0,) * a.ndim)
     anywhere = pl.BlockSpec(memory_space=pl.ANY)
     vmem, dma = pltpu.VMEM, pltpu.SemaphoreType.DMA
 
     def early(i):
-        return jnp.minimum(i, FIRST_QUERY - 1)
+        return jnp.minimum(i, blocks - 1)
 
     def twice(i):
-        return jnp.where(i < FIRST_QUERY, i, jnp.clip(i - FIRST_QUERY, 0, 7))
+        return jnp.where(i < blocks, i, jnp.clip(i - blocks, 0, blocks - 1))
+
+    def turned(i):
+        return blocks - 1 - lax.rem(jnp.clip(i - 2 * blocks, 0, 2 * blocks - 1), blocks)
 
     def always(i):
-        turned = 7 - lax.rem(jnp.clip(i - FIRST_COLUMN, 0, 15), 8)
-        return jnp.where(i < TURN, twice(i), turned)
+        return jnp.where(i < 2 * blocks, twice(i), turned(i))
 
     def both(i):
-        turned = 7 - lax.rem(jnp.clip(i - FIRST_COLUMN, 0, 15), 8)
-        return jnp.where(i < FIRST_QUERY, i, turned)
-
-    late = lambda i: (jnp.maximum(i - FIRST_INPUT, 0), 0)
+        return jnp.where(i < blocks, i, turned(i))
+
+    late = lambda i: (jnp.maximum(i - 4 * blocks, 0), 0)
     tall = pl.BlockSpec((size, D), late)
+    some = lambda lanes, order: pl.BlockSpec((size, lanes), lambda i: (order(i), 0))
     slabs = 4 * count
     return pl.pallas_call(
-        functools.partial(back_kernel, count, last),
-        grid=(last + 1,),
-        in_specs=[rows_of(D, early), tall, rows_of(4 * D, always), rows_of(D, both)]
-        + [rows_of(D, early)] * 3
-        + [pl.BlockSpec((1, 128, D), lambda i: (twice(i), 0, 0)), tall]
-        + [once(doc_ids), once(small), once(w_all), anywhere, anywhere, once(ffs)],
+        functools.partial(back_kernel, count, per),
+        grid=(5 * blocks,),
+        in_specs=[some(D, early), tall, some(4 * D, always), some(D, both)]
+        + [some(D, early)] * 3
+        + [pl.BlockSpec((per, 128, D), lambda i: (twice(i), 0, 0)), tall]
+        + [once(doc_ids), once(small), anywhere, anywhere, anywhere, once(ffs)],
         out_specs=[tall] + [anywhere] * 5 + [whole(16, D), whole(8, D)],
         out_shape=[
             shape_of((rows, D), F32),
@@ -1304,6 +1401,8 @@
             vmem((4, 8, D), F32),
             vmem((8, 128, D), BF16),
             vmem((8, D), F32),
+            vmem(w_all.shape, BF16),
+            dma,
             vmem((slabs, part, 128), link),
             vmem((slabs, part, 256), link),
             vmem((slabs, part, 128), link),
@@ -1318,7 +1417,7 @@
         + small_scratch(count, 8)
         + [dma((3, 2)), dma((3, 2))],
         compiler_params=pltpu.CompilerParams(
-            vmem_limit_bytes=LIMIT, collective_id=2, has_side_effects=True
+            vmem_limit_bytes=(62 if link == BF16 else 63) * MIB, collective_id=2, has_side_effects=True
         ),
         name="back",
     )(
@@ -1327,9 +1426,18 @@
     )
 
 
-def finish_kernel(count, part, gi_ref, ff_ref, fr_ref, q_ref, kv_ref, f_ref, s1_ref, s2_ref, gi_out, *outs):
+def finish_kernel(
+    count, part, gi_ref, ff_ref, fr_ref, q_ref, kv_ref, f_ref, s1_ref, s2_ref, gi_out, *rest
+):
     at = lax.axis_index("fsdp")
-    gi_out[...] = gi_ref[...]
+    *outs, held, sems = rest
+    size = held.shape[0] // 8
+
+    def move(n, out):
+        here = pl.ds(n * size, size)
+        if out:
+            return pltpu.make_async_copy(held.at[here], gi_out.at[here], sems.at[1, n])
+        return pltpu.make_async_copy(gi_ref.at[here], held.at[here], sems.at[0, n])
 
     def pick(row, size):
         out = row(0, size)
@@ -1344,37 +1452,45 @@
     def row_of_sums(ref, n):
         return lambda start, size: ref[n : n + 1, start : start + size]
 
-    @pl.when(pl.program_id(0) == 0)
-    def _():
-        for n in range(4):
-            lanes = slice(n * 128, (n + 1) * 128)
-            outs[0][:, lanes] = q_ref[n]
-            outs[1][:, lanes] = kv_ref[n, :, 0:128]
-            outs[2][:, lanes] = kv_ref[n, :, 128:256]
-            outs[3][:, lanes] = f_ref[n]
-            outs[4][:, lanes] = ff_ref[n, :, 512:640]
-            outs[5][:, n * 512 : (n + 1) * 512] = ff_ref[n, :, 0:512]
-            for j in range(4):
-                outs[6][j * part : (j + 1) * part, lanes] = fr_ref[n, :, j * 128 : (j + 1) * 128]
-        outs[7][...] = pick(row_of_sums(s2_ref, 0), part)
-        outs[8][...] = pick(row_of_sums(s2_ref, 1), part)
-        outs[9][...] = pick(row_of_sums(s1_ref, 2), part)
-        outs[10][...] = pick(row_of_sums(s1_ref, 3), part)
-        outs[11][...] = pick(bias, 4 * part)
-        outs[12][...] = pick(row_of_sums(s1_ref, 4), part)
+    for n in range(8):
+        move(n, False).start()
+    for n in range(4):
+        lanes = slice(n * 128, (n + 1) * 128)
+        outs[0][:, lanes] = q_ref[n]
+        outs[1][:, lanes] = kv_ref[n, :, 0:128]
+        outs[2][:, lanes] = kv_ref[n, :, 128:256]
+        outs[3][:, lanes] = f_ref[n]
+        outs[4][:, lanes] = ff_ref[n, :, 512:640]
+        outs[5][:, n * 512 : (n + 1) * 512] = ff_ref[n, :, 0:512]
+        for j in range(4):
+            outs[6][j * part : (j + 1) * part, lanes] = fr_ref[n, :, j * 128 : (j + 1) * 128]
+    for n in range(8):
+        move(n, False).wait()
+        move(n, True).start()
+    outs[7][...] = pick(row_of_sums(s2_ref, 0), part)
+    outs[8][...] = pick(row_of_sums(s2_ref, 1), part)
+    outs[9][...] = pick(row_of_sums(s1_ref, 2), part)
+    outs[10][...] = pick(row_of_sums(s1_ref, 3), part)
+    outs[11][...] = pick(bias, 4 * part)
+    outs[12][...] = pick(row_of_sums(s1_ref, 4), part)
+    for n in range(8):
+        move(n, True).wait()
 
 
 def finish(count, part, grad_input, *sums):
-    once = lambda shape: pl.BlockSpec(shape, lambda i: (0,) * len(shape))
-    tall = pl.BlockSpec((512, D), lambda i: (i, 0))
+    once = lambda shape: pl.BlockSpec(shape, lambda: (0,) * len(shape))
+    anywhere = pl.BlockSpec(memory_space=pl.ANY)
     shapes = [(part, D)] * 5 + [(part, FF), (4 * part, D)]
     shapes += [(1, part)] * 4 + [(1, 4 * part), (1, part)]
     return pl.pallas_call(
         functools.partial(finish_kernel, count, part),
-        grid=(grad_input.shape[0] // 512,),
-        in_specs=[tall] + [once(a.shape) for a in sums],
-        out_specs=[tall] + [once(s) for s in shapes],
+        in_specs=[anywhere] + [once(a.shape) for a in sums],
+        out_specs=[anywhere] + [once(s) for s in shapes],
         out_shape=[shape_of(s, F32) for s in (grad_input.shape, *shapes)],
+        scratch_shapes=[
+            pltpu.VMEM(grad_input.shape, F32),
+            pltpu.SemaphoreType.DMA((2, 8)),
+        ],
         compiler_params=PARAMS,
         name="finish",
     )(grad_input, *sums)
@@ -1396,7 +1512,7 @@
     return jax.ShapeDtypeStruct(shape, kind)
 
 
-PARAMS = pltpu.CompilerParams(vmem_limit_bytes=LIMIT)
+PARAMS = pltpu.CompilerParams(vmem_limit_bytes=62 * MIB)
 
 
 def on_device(

time: 236 us -> 202 us (0.86)
  Pallas kernels: 235 us -> 201 us
    pallas_call x3, Pallas kernels: 190 us -> 158 us  [the longest x1 87.4 us: back(): pl.pallas_call(functools.partial(back_kernel, count, per), grid=(5 * bloc...]
where the time goes in v5:
time: 202 us
  Pallas kernels  201 us (100%)
    pallas_call x1, Pallas kernels, back(): pl.pallas_call(functools.partial(back_kernel, count, per), grid=(5 * bloc...  87.4 us
    pallas_call x1, Pallas kernels, front(): pl.pallas_call(functools.partial(front_kernel, count), grid=(2 * FRONT,),...  64 us
    pallas_call x1, Pallas kernels, on_device(): pl.pallas_call(forward_kernel, grid=(rows // FEED_ROWS,), in_specs=[tall]...  43.6 us
    pallas_call x1, Pallas kernels, finish(): pl.pallas_call(functools.partial(finish_kernel, count, part), in_specs=[a...  6.22 us

profile of v5, /device:TPU:0, one launch (start us, length us, event | category | flops | bytes accessed | tf_op | source)
XLA Modules:
  0.0 202.1 jit_solution(3876293875636592227)
XLA Ops:
  0.7 64.0 %front.1 = (bf16[2048,2048]{1,0:T(8,128)(2,1)}, bf16[2048,512]{1,0:T(8,128)(2,1)}, f32[2048,512]{1,0:T(8,128)}, f32[2048,512]{1,0:T(8,128)}, f32[2048,512]{1,0:T...) custom-call(bf16[2048,512]{1,0:T(8,128)(2,1)} %xs_ref.1, ...), custom_call_target="tpu_custom_call" | custom-call | tf_op jit(solution)/shard_map/front/pallas_call | solution.py:625
  64.6 43.6 %feed.1 = (bf16[2048,512]{1,0:T(8,128)(2,1)}, f32[2048,512]{1,0:T(8,128)}, bf16[2048,512]{1,0:T(8,128)(2,1)}, bf16[2,2,2,4,64,640]{5,4,3,2,1,0:T(8,128)(2,1)}, b...) custom-call(bf16[2048,512]{1,0:T(8,128)(2,1)} %xs_ref.1, bf16[2048,512]{1,0:T(8,128)(2,1)} %get-tuple-element.55.o_ref, ...), custom_call_target="tpu_custom_call" | custom-call | tf_op jit(solution)/shard_map/feed/pallas_call | solution.py:1538
  108.3 87.4 %back.1 = (f32[2048,512]{1,0:T(8,128)}, f32[4,64,640]{2,1,0:T(8,128)}, f32[4,64,512]{2,1,0:T(8,128)}, f32[4,64,128]{2,1,0:T(8,128)}, f32[4,64,256]{2,1,0:T(8,128...) custom-call(bf16[2048,512]{1,0:T(8,128)(2,1)} %xs_ref.1, bf16[2048,512]{1,0:T(8,128)(2,1)} %xs_ref.1, ...), custom_call_target="tpu_custom_call" | custom-call | tf_op jit(solution)/shard_map/back/pallas_call | solution.py:1372
  195.7 6.2 %finish.1 = (f32[2048,512]{1,0:T(8,128)}, f32[64,512]{1,0:T(8,128)}, f32[64,512]{1,0:T(8,128)}, f32[64,512]{1,0:T(8,128)}, f32[64,512]{1,0:T(8,128)}, /*index=5*...) custom-call(f32[2048,512]{1,0:T(8,128)} %get-tuple-element.73.gi_ref, ...), custom_call_target="tpu_custom_call" | custom-call | tf_op jit(solution)/shard_map/finish/pallas_call | solution.py:1485
